TPU v7x, 32 devices: a whole 2x2x4 slice. The times are simulated.
32 devices in a mesh: rep: 4 (over y, x), shard: 8 (over z, core).
Axes of the slice: x: 2, y: 2, z: 4, core: 2. Of those that a mesh axis runs over, the one named last changes fastest.
Arguments:
- tokens: bfloat16 [32, 256, 1024], P(('rep', 'shard')), may hold values from -6 to 6
- states: bfloat16 [32, 384, 1024], P(('rep', 'shard')), may hold values from -6 to 6
- cotangent: bfloat16 [32, 256, 1024], P(('rep', 'shard')), may hold values from -6 to 6
- dec_len: int32 [32], P(('rep', 'shard')), may hold values from 64 to 256, as said below
- enc_len: int32 [32], P(('rep', 'shard')), may hold values from 96 to 384, as said below
- self_weights: float32 [4, 1024, 1024], P(None, 'shard'), may hold values from -0.5625 to 0.5625
- cross_weights: float32 [4, 1024, 1024], P(None, 'shard'), may hold values from -0.5625 to 0.5625
- fc_in: float32 [1024, 4096], P('shard'), may hold values from -0.1875 to 0.1875
- fc_out: float32 [4096, 1024], P('shard'), may hold values from -0.09375 to 0.09375
- norm_params: float32 [2, 3, 1024], replicated, may hold values from -1.5 to 1.5, as said below
- self_moment: float32 [4, 1024, 1024], P(None, 'shard'), may hold values from -217.2232 to 217.2232
- cross_moment: float32 [4, 1024, 1024], P(None, 'shard'), may hold values from -217.2232 to 217.2232
- fc_in_moment: float32 [1024, 4096], P('shard'), may hold values from -162.9174 to 162.9174
- fc_out_moment: float32 [4096, 1024], P('shard'), may hold values from -325.8348 to 325.8348
- norm_moment: float32 [2, 3, 1024], P(None, None, 'shard'), may hold values from -543.058 to 543.058
Outputs:
- block_out: bfloat16 [32, 256, 1024], P(('rep', 'shard'))
- tokens_grad: bfloat16 [32, 256, 1024], P(('rep', 'shard'))
- states_grad: bfloat16 [32, 384, 1024], P(('rep', 'shard'))
- self_grad: float32 [4, 1024, 1024], P(None, 'shard')
- cross_grad: float32 [4, 1024, 1024], P(None, 'shard')
- fc_in_grad: float32 [1024, 4096], P('shard')
- fc_out_grad: float32 [4096, 1024], P('shard')
- norm_grad: float32 [2, 3, 1024], P(None, None, 'shard')
- self_moment_new: float32 [4, 1024, 1024], P(None, 'shard')
- cross_moment_new: float32 [4, 1024, 1024], P(None, 'shard')
- fc_in_moment_new: float32 [1024, 4096], P('shard')
- fc_out_moment_new: float32 [4096, 1024], P('shard')
- norm_moment_new: float32 [2, 3, 1024], P(None, None, 'shard')
- self_new: float32 [4, 1024, 1024], P(None, 'shard')
- cross_new: float32 [4, 1024, 1024], P(None, 'shard')
- fc_in_new: float32 [1024, 4096], P('shard')
- fc_out_new: float32 [4096, 1024], P('shard')
- norm_new: float32 [2, 3, 1024], P(None, None, 'shard')
- self_low: bfloat16 [4, 1024, 1024], P(None, 'shard')
- cross_low: bfloat16 [4, 1024, 1024], P(None, 'shard')
- fc_in_low: bfloat16 [1024, 4096], P('shard')
- fc_out_low: bfloat16 [4096, 1024], P('shard')
Inputs may be any that keep to these rules, and one draw needn't show every extreme that they name: `dec_len`: at least a quarter of the slots are used; some sequence of every draw uses all 256. `enc_len`: at least a quarter of the slots are used; some sequence of every draw uses all 384. `norm_params`: gains between 0.7 and 1.4.
All inputs are finite; a program needn't handle non-finite values.
Results may differ from a plain program's by a relative error of at most 0.024.
Values may be sent and summed in bfloat16 or wider, within the bound.
No kernel may reach another device: no remote copies, remote signals or barrier semaphores. Data moves between devices by JAX's collectives and lax.ppermute only.
A program may use at most 256 MiB of HBM per device.

v0:
```python
import math

import jax
import jax.numpy as jnp
from jax import lax
from jax.sharding import PartitionSpec as P

HEADS = 16
HEAD_DIM = 64
NS_STEPS = 3


NORM_EPSILON = 1e-05
MOMENTUM_DECAY = 0.9
MATRIX_RATE = 0.6
VECTOR_RATE = 0.05
SCHULZ_FIRST = 3.4445
SCHULZ_SECOND = -4.775
SCHULZ_THIRD = 2.0315


def matmul(left, right):
    return jnp.dot(left, right, preferred_element_type=jnp.float32)


def matmul_left_t(left, right):
    return lax.dot_general(
        left, right, (((0,), (0,)), ((), ())), preferred_element_type=jnp.float32
    )


def matmul_right_t(left, right):
    return lax.dot_general(
        left, right, (((1,), (1,)), ((), ())), preferred_element_type=jnp.float32
    )


def normalize_parts(values, gain, bias):
    centered = values - jnp.mean(values, axis=-1, keepdims=True)
    inverse = lax.rsqrt(jnp.mean(centered * centered, axis=-1, keepdims=True) + NORM_EPSILON)
    unit_part = centered * inverse
    return (unit_part * gain + bias, unit_part, inverse)


def normalize_back(grad_out, unit_part, inverse, gain):
    grad_unit = grad_out * gain
    grad_in = inverse * (
        grad_unit
        - jnp.mean(grad_unit, axis=-1, keepdims=True)
        - unit_part * jnp.mean(grad_unit * unit_part, axis=-1, keepdims=True)
    )
    return (grad_in, jnp.sum(grad_out * unit_part, axis=0), jnp.sum(grad_out, axis=0))


def split_into_heads(values):
    return values.reshape(values.shape[0], HEADS, HEAD_DIM)


def scores_of(query_rows, incoming_keys, valid):
    raw_scores = jnp.einsum(
        "pwj,rwj->wpr",
        split_into_heads(query_rows),
        split_into_heads(incoming_keys),
        preferred_element_type=jnp.float32,
    )
    return jnp.where(valid[None], raw_scores * HEAD_DIM ** (-0.5), -jnp.inf)


def attend_forward(query_rows, incoming_keys, incoming_values, valid):
    logit_scores = scores_of(query_rows, incoming_keys, valid)
    row_max = jnp.max(logit_scores, axis=-1, keepdims=True)
    exponent = jnp.exp(logit_scores - row_max)
    row_total = jnp.sum(exponent, axis=-1, keepdims=True)
    attention_weights = (exponent / row_total).astype(jnp.bfloat16)
    attended_values = jnp.einsum(
        "onw,wov->nov",
        attention_weights,
        split_into_heads(incoming_values),
        preferred_element_type=jnp.float32,
    )
    return (
        attended_values.reshape(query_rows.shape[0], -1).astype(jnp.bfloat16),
        row_max + jnp.log(row_total),
    )


def attend_backward(query_rows, incoming_keys, incoming_values, valid, log_total, grad_mixed):
    logit_scores = scores_of(query_rows, incoming_keys, valid)
    attention_weights = jnp.exp(logit_scores - log_total)
    head_gradient_rows = split_into_heads(grad_mixed)
    grad_values = jnp.einsum(
        "cak,acu->kcu",
        attention_weights.astype(jnp.bfloat16),
        head_gradient_rows,
        preferred_element_type=jnp.float32,
    )
    grad_prob = jnp.einsum(
        "pwj,rwj->wpr",
        head_gradient_rows,
        split_into_heads(incoming_values),
        preferred_element_type=jnp.float32,
    )
    score_gradient = (
        attention_weights
        * (grad_prob - jnp.sum(grad_prob * attention_weights, axis=-1, keepdims=True))
    ).astype(jnp.bfloat16)
    grad_query = jnp.einsum(
        "onw,wov->nov",
        score_gradient,
        split_into_heads(incoming_keys),
        preferred_element_type=jnp.float32,
    ) * HEAD_DIM ** (-0.5)
    grad_keys = jnp.einsum(
        "cak,acu->kcu",
        score_gradient,
        split_into_heads(query_rows),
        preferred_element_type=jnp.float32,
    ) * HEAD_DIM ** (-0.5)
    return (
        grad_query.reshape(query_rows.shape[0], -1).astype(jnp.bfloat16),
        grad_keys.reshape(incoming_keys.shape[0], -1).astype(jnp.bfloat16),
        grad_values.reshape(incoming_keys.shape[0], -1).astype(jnp.bfloat16),
    )


def orthogonalize(matrix):
    current = matrix
    wide_float = current.astype(jnp.float32)
    current = (wide_float / (jnp.sqrt(jnp.sum(wide_float * wide_float)) + 1e-07)).astype(
        jnp.bfloat16
    )
    for sweep_index in range(NS_STEPS):
        gram_matrix = matmul_right_t(current, current).astype(jnp.bfloat16)
        polynomial = (
            SCHULZ_SECOND * gram_matrix.astype(jnp.float32)
            + SCHULZ_THIRD * matmul(gram_matrix, gram_matrix)
        ).astype(jnp.bfloat16)
        current = (SCHULZ_FIRST * current.astype(jnp.float32) + matmul(polynomial, current)).astype(
            jnp.bfloat16
        )
    return current


def stretch(shape):
    return math.sqrt(max(shape[0], shape[1]) / min(shape[0], shape[1]))


def on_device(
    tokens,
    states,
    cotangent,
    dec_len,
    enc_len,
    self_weights,
    cross_weights,
    fc_in,
    fc_out,
    norm_params,
    self_moment,
    cross_moment,
    fc_in_moment,
    fc_out_moment,
    norm_moment,
):
    local_shards = (
        self_weights.astype(jnp.bfloat16),
        cross_weights.astype(jnp.bfloat16),
        fc_in.astype(jnp.bfloat16),
        fc_out.astype(jnp.bfloat16),
    )
    self_full, cross_full, in_full, out_full = (
        lax.all_gather(local_shards[0], "shard", axis=1, tiled=True),
        lax.all_gather(local_shards[1], "shard", axis=1, tiled=True),
        lax.all_gather(local_shards[2], "shard", axis=0, tiled=True),
        lax.all_gather(local_shards[3], "shard", axis=0, tiled=True),
    )
    source = tokens[0].astype(jnp.float32)
    encoded = states[0]
    slot_count = tokens.shape[1]
    enc_count = states.shape[1]
    place = jnp.arange(slot_count)
    enc_place = jnp.arange(enc_count)
    self_valid = (place[None, :] <= place[:, None]) & (place[None, :] < dec_len[0])
    cross_valid = jnp.broadcast_to(enc_place[None, :] < enc_len[0], (slot_count, enc_count))
    gain_rows = norm_params[0]
    bias_rows = norm_params[1]
    first, first_unit, first_inv = normalize_parts(source, gain_rows[0], bias_rows[0])
    first_low = first.astype(jnp.bfloat16)
    query_rows = matmul(first_low, self_full[0]).astype(jnp.bfloat16)
    incoming_keys = matmul(first_low, self_full[1]).astype(jnp.bfloat16)
    incoming_values = matmul(first_low, self_full[2]).astype(jnp.bfloat16)
    attended_values, self_log = attend_forward(
        query_rows, incoming_keys, incoming_values, self_valid
    )
    after_self = source + matmul(attended_values, self_full[3])
    second, second_unit, second_inv = normalize_parts(after_self, gain_rows[1], bias_rows[1])
    second_low = second.astype(jnp.bfloat16)
    cross_query = matmul(second_low, cross_full[0]).astype(jnp.bfloat16)
    cross_keys = matmul(encoded, cross_full[1]).astype(jnp.bfloat16)
    cross_values = matmul(encoded, cross_full[2]).astype(jnp.bfloat16)
    cross_mixed, cross_log = attend_forward(cross_query, cross_keys, cross_values, cross_valid)
    after_cross = after_self + matmul(cross_mixed, cross_full[3])
    third, third_unit, third_inv = normalize_parts(after_cross, gain_rows[2], bias_rows[2])
    third_low = third.astype(jnp.bfloat16)
    pre_act = matmul(third_low, in_full)
    hidden = jax.nn.gelu(pre_act).astype(jnp.bfloat16)
    block_out = after_cross + matmul(hidden, out_full)
    self_full, cross_full, in_full, out_full = (
        lax.all_gather(local_shards[0], "shard", axis=1, tiled=True),
        lax.all_gather(local_shards[1], "shard", axis=1, tiled=True),
        lax.all_gather(local_shards[2], "shard", axis=0, tiled=True),
        lax.all_gather(local_shards[3], "shard", axis=0, tiled=True),
    )
    grad_out = cotangent[0].astype(jnp.float32)
    grad_branch = grad_out.astype(jnp.bfloat16)
    out_grad = matmul_left_t(hidden, grad_branch)
    grad_hidden = matmul_right_t(grad_branch, out_full)
    grad_pre = jax.vjp(jax.nn.gelu, pre_act)[1](grad_hidden)[0].astype(jnp.bfloat16)
    in_grad = matmul_left_t(third_low, grad_pre)
    grad_third = matmul_right_t(grad_pre, in_full)
    grad_norm, third_gain, third_bias = normalize_back(
        grad_third, third_unit, third_inv, gain_rows[2]
    )
    grad_cross = grad_out + grad_norm
    grad_branch = grad_cross.astype(jnp.bfloat16)
    cross_out_grad = matmul_left_t(cross_mixed, grad_branch)
    grad_mixed = matmul_right_t(grad_branch, cross_full[3]).astype(jnp.bfloat16)
    grad_cq, grad_ck, grad_cv = attend_backward(
        cross_query, cross_keys, cross_values, cross_valid, cross_log, grad_mixed
    )
    cross_query_grad = matmul_left_t(second_low, grad_cq)
    cross_key_grad = matmul_left_t(encoded, grad_ck)
    cross_value_grad = matmul_left_t(encoded, grad_cv)
    grad_second = matmul_right_t(grad_cq, cross_full[0])
    grad_states = matmul_right_t(grad_ck, cross_full[1]) + matmul_right_t(grad_cv, cross_full[2])
    grad_norm, second_gain, second_bias = normalize_back(
        grad_second, second_unit, second_inv, gain_rows[1]
    )
    grad_self = grad_cross + grad_norm
    grad_branch = grad_self.astype(jnp.bfloat16)
    self_out_grad = matmul_left_t(attended_values, grad_branch)
    grad_mixed = matmul_right_t(grad_branch, self_full[3]).astype(jnp.bfloat16)
    grad_sq, grad_sk, grad_sv = attend_backward(
        query_rows, incoming_keys, incoming_values, self_valid, self_log, grad_mixed
    )
    self_query_grad = matmul_left_t(first_low, grad_sq)
    self_key_grad = matmul_left_t(first_low, grad_sk)
    self_value_grad = matmul_left_t(first_low, grad_sv)
    grad_first = (
        matmul_right_t(grad_sq, self_full[0])
        + matmul_right_t(grad_sk, self_full[1])
        + matmul_right_t(grad_sv, self_full[2])
    )
    grad_norm, first_gain, first_bias = normalize_back(
        grad_first, first_unit, first_inv, gain_rows[0]
    )
    grad_tokens = grad_self + grad_norm
    self_local = jnp.stack([self_query_grad, self_key_grad, self_value_grad, self_out_grad])
    cross_local = jnp.stack([cross_query_grad, cross_key_grad, cross_value_grad, cross_out_grad])
    norm_local = jnp.stack(
        [
            jnp.stack([first_gain, second_gain, third_gain]),
            jnp.stack([first_bias, second_bias, third_bias]),
        ]
    )
    reduced = (
        lax.psum_scatter(
            self_local.astype(jnp.bfloat16), "shard", scatter_dimension=1, tiled=True
        ).astype(jnp.float32),
        lax.psum_scatter(
            cross_local.astype(jnp.bfloat16), "shard", scatter_dimension=1, tiled=True
        ).astype(jnp.float32),
        lax.psum_scatter(
            in_grad.astype(jnp.bfloat16), "shard", scatter_dimension=0, tiled=True
        ).astype(jnp.float32),
        lax.psum_scatter(
            out_grad.astype(jnp.bfloat16), "shard", scatter_dimension=0, tiled=True
        ).astype(jnp.float32),
        lax.psum_scatter(
            norm_local.astype(jnp.bfloat16), "shard", scatter_dimension=2, tiled=True
        ).astype(jnp.float32),
    )
    self_grad, cross_grad, fc_in_grad, fc_out_grad, norm_grad = (
        lax.psum(reduced[0].astype(jnp.bfloat16), "rep").astype(jnp.float32),
        lax.psum(reduced[1].astype(jnp.bfloat16), "rep").astype(jnp.float32),
        lax.psum(reduced[2].astype(jnp.bfloat16), "rep").astype(jnp.float32),
        lax.psum(reduced[3].astype(jnp.bfloat16), "rep").astype(jnp.float32),
        lax.psum(reduced[4].astype(jnp.bfloat16), "rep").astype(jnp.float32),
    )
    self_fresh = MOMENTUM_DECAY * self_moment + self_grad
    cross_fresh = MOMENTUM_DECAY * cross_moment + cross_grad
    in_fresh = MOMENTUM_DECAY * fc_in_moment + fc_in_grad
    out_fresh = MOMENTUM_DECAY * fc_out_moment + fc_out_grad
    norm_fresh = MOMENTUM_DECAY * norm_moment + norm_grad
    shard_count = lax.axis_size("shard")
    my_place = lax.axis_index("shard")
    self_whole, cross_whole, in_whole, out_whole = (
        lax.all_gather(self_fresh.astype(jnp.bfloat16), "shard", axis=1, tiled=True),
        lax.all_gather(cross_fresh.astype(jnp.bfloat16), "shard", axis=1, tiled=True),
        lax.all_gather(in_fresh.astype(jnp.bfloat16), "shard", axis=0, tiled=True),
        lax.all_gather(out_fresh.astype(jnp.bfloat16), "shard", axis=0, tiled=True),
    )
    square_whole = jnp.concatenate([self_whole, cross_whole])
    square_index = jnp.arange(8)
    number = my_place + 0
    picked = lax.dynamic_index_in_dim(square_whole, jnp.minimum(number, 7), 0, keepdims=False)
    result = orthogonalize(picked).astype(jnp.float32)
    hit = (square_index == number)[:, None, None]
    square_terms = jnp.where(hit, result[None], 0.0)
    in_owner = 8 % shard_count
    out_owner = 9 % shard_count
    wide_result = orthogonalize(jnp.where(my_place == out_owner, out_whole.T, in_whole)).astype(
        jnp.float32
    )
    in_term = jnp.where(my_place == in_owner, wide_result, 0.0)
    out_term = jnp.where(my_place == out_owner, wide_result.T, 0.0)
    self_orth, cross_orth, in_orth, out_orth = (
        lax.psum_scatter(
            square_terms[:4].astype(jnp.bfloat16), "shard", scatter_dimension=1, tiled=True
        ).astype(jnp.float32),
        lax.psum_scatter(
            square_terms[4:].astype(jnp.bfloat16), "shard", scatter_dimension=1, tiled=True
        ).astype(jnp.float32),
        lax.psum_scatter(
            in_term.astype(jnp.bfloat16), "shard", scatter_dimension=0, tiled=True
        ).astype(jnp.float32),
        lax.psum_scatter(
            out_term.astype(jnp.bfloat16), "shard", scatter_dimension=0, tiled=True
        ).astype(jnp.float32),
    )
    self_new = self_weights - MATRIX_RATE * stretch(self_full.shape[1:]) * self_orth
    cross_new = cross_weights - MATRIX_RATE * stretch(cross_full.shape[1:]) * cross_orth
    in_new = fc_in - MATRIX_RATE * stretch(in_full.shape) * in_orth
    out_new = fc_out - MATRIX_RATE * stretch(out_full.shape) * out_orth
    width_part = norm_moment.shape[2]
    own_params = lax.dynamic_slice_in_dim(norm_params, my_place * width_part, width_part, 2)
    total_tokens = lax.axis_size("rep") * shard_count * tokens.shape[0] * tokens.shape[1]
    norm_new = own_params - VECTOR_RATE * norm_fresh / math.sqrt(total_tokens)
    return (
        block_out[None].astype(jnp.bfloat16),
        grad_tokens[None].astype(jnp.bfloat16),
        grad_states[None].astype(jnp.bfloat16),
        self_grad,
        cross_grad,
        fc_in_grad,
        fc_out_grad,
        norm_grad,
        self_fresh,
        cross_fresh,
        in_fresh,
        out_fresh,
        norm_fresh,
        self_new,
        cross_new,
        in_new,
        out_new,
        norm_new,
        self_new.astype(jnp.bfloat16),
        cross_new.astype(jnp.bfloat16),
        in_new.astype(jnp.bfloat16),
        out_new.astype(jnp.bfloat16),
    )


def solution(mesh):
    placed = (
        P(("rep", "shard"), None, None),
        P(("rep", "shard"), None, None),
        P(("rep", "shard"), None, None),
        P(("rep", "shard")),
        P(("rep", "shard")),
        P(None, "shard", None),
        P(None, "shard", None),
        P("shard", None),
        P("shard", None),
        P(),
        P(None, "shard", None),
        P(None, "shard", None),
        P("shard", None),
        P("shard", None),
        P(None, None, "shard"),
    )
    return jax.shard_map(
        on_device,
        mesh=mesh,
        in_specs=placed,
        out_specs=(
            P(("rep", "shard"), None, None),
            P(("rep", "shard"), None, None),
            P(("rep", "shard"), None, None),
            P(None, "shard", None),
            P(None, "shard", None),
            P("shard", None),
            P("shard", None),
            P(None, None, "shard"),
            P(None, "shard", None),
            P(None, "shard", None),
            P("shard", None),
            P("shard", None),
            P(None, None, "shard"),
            P(None, "shard", None),
            P(None, "shard", None),
            P("shard", None),
            P("shard", None),
            P(None, None, "shard"),
            P(None, "shard", None),
            P(None, "shard", None),
            P("shard", None),
            P("shard", None),
        ),
        check_vma=False,
    )
```

profile of v0, /device:TPU:0, one launch (start us, length us, event | category | flops | bytes accessed | tf_op | source)
XLA Modules:
  0.0 1549.5 jit_solution(5913253685795772157)
XLA Ops:
  19.0 76.1 %all-gather.9.cloned.1.call-done = bf16[4,1024,1024]{2,1,0:T(8,128)(2,1)} async-done(((bf16[4,128,1024]{2,1,0:T(8,128)(2,1)}), bf16[4,1024,1024]{2,1,0:T(8,128)(2,1)}) %all-gather.9.cloned.1.call-update) | async-done | bytes 8388624 | tf_op jit(solution)/shard_map/all_gather | solution.py:172
  103.2 74.7 %all-gather.11.cloned.1.call-done = bf16[4,1024,1024]{2,1,0:T(8,128)(2,1)} async-done(((bf16[4,128,1024]{2,1,0:T(8,128)(2,1)}), bf16[4,1024,1024]{2,1,0:T(8,128)(2,1)}) %all-gather.11.cloned.1.call-update) | async-done | bytes 8388624 | tf_op jit(solution)/shard_map/all_gather | solution.py:173
  209.1 51.6 %all-gather.13.cloned.1.call-done = bf16[1024,4096]{1,0:T(8,128)(2,1)} async-done(((bf16[128,4096]{1,0:T(8,128)(2,1)}), bf16[1024,4096]{1,0:T(8,128)(2,1)}) %all-gather.13.cloned.1.call-update) | async-done | bytes 8388624 | tf_op jit(solution)/shard_map/all_gather | solution.py:174
  273.6 69.8 %all-gather.15.cloned.1.call-done = bf16[4096,1024]{1,0:T(8,128)(2,1)} async-done(((bf16[512,1024]{1,0:T(8,128)(2,1)}), bf16[4096,1024]{1,0:T(8,128)(2,1)}) %all-gather.15.cloned.1.call-update) | async-done | bytes 8388624 | tf_op jit(solution)/shard_map/all_gather | solution.py:175
  343.3 9.1 fusion.15
  352.5 6.8 multiply_reduce_fusion.2
  416.9 7.4 convolution_convert_fusion.1
  424.3 9.3 reduce-scatter.18.cloned.1.call-done
  433.7 90.1 %reduce-scatter.12.cloned.1.call-done = bf16[4,128,1024]{2,1,0:T(8,128)(2,1)} async-done(((bf16[4,1024,1024]{2,1,0:T(8,128)(2,1)}), bf16[4,128,1024]{2,1,0:T(8,128)(2,1)}) %reduce-scatter.12.cloned.1.call-update) | async-done | bytes 1048592 | tf_op jit(solution)/shard_map/reduce_scatter | solution.py:267
  523.8 90.3 %reduce-scatter.14.cloned.1.call-done = bf16[4,128,1024]{2,1,0:T(8,128)(2,1)} async-done(((bf16[4,1024,1024]{2,1,0:T(8,128)(2,1)}), bf16[4,128,1024]{2,1,0:T(8,128)(2,1)}) %reduce-scatter.14.cloned.1.call-update) | async-done | bytes 1048592 | tf_op jit(solution)/shard_map/reduce_scatter | solution.py:270
  614.1 90.3 %reduce-scatter.16.cloned.1.call-done = bf16[128,4096]{1,0:T(8,128)(2,1)} async-done(((bf16[1024,4096]{1,0:T(8,128)(2,1)}), bf16[128,4096]{1,0:T(8,128)(2,1)}) %reduce-scatter.16.cloned.1.call-update) | async-done | bytes 1048592 | tf_op jit(solution)/shard_map/reduce_scatter | solution.py:273
  704.4 106.9 %all-reduce.3.cloned.1.call-done = (bf16[512,1024]{0,1:T(8,128)(2,1)}, bf16[4,128,1024]{2,1,0:T(8,128)(2,1)}, bf16[4,128,1024]{2,1,0:T(8,128)(2,1)}, bf16[128,4096]{1,0:T(8,128)(2,1)}) async-done(((bf16[512,1024]{0,1:T(8,128)(2,1)}, bf16[4,128,1024]{2,1,0:T(8,128)(2,1)}, bf16[4,128,1024]{2,1,0:T(8,128)(2,1)}, bf16[128,4096]{1,0:T(8,128)(2,1)}), (bf16[512,1024]{0,1:T(8,128)(2,1)}, ...) | async-done | bytes 4194320 | tf_op jit(solution)/shard_map/psum | solution.py:287
  844.0 54.4 %all-gather.23.cloned.1.call-done = bf16[1024,4096]{1,0:T(8,128)(2,1)} async-done(((bf16[128,4096]{1,0:T(8,128)(2,1)}), bf16[1024,4096]{1,0:T(8,128)(2,1)}) %all-gather.23.cloned.1.call-update) | async-done | bytes 8388624 | tf_op jit(solution)/shard_map/all_gather | solution.py:300
  898.4 82.9 %all-gather.21.cloned.1.call-done = bf16[4096,1024]{0,1:T(8,128)(2,1)} async-done(((bf16[512,1024]{0,1:T(8,128)(2,1)}), bf16[4096,1024]{0,1:T(8,128)(2,1)}) %all-gather.21.cloned.1.call-update) | async-done | bytes 8388624 | tf_op jit(solution)/shard_map/all_gather | solution.py:301
  981.3 10.7 fusion
  992.7 7.8 fusion.1
  1003.8 9.1 fusion.166
  1012.8 19.0 %add_convert_fusion.2 = bf16[1024,4096]{1,0:T(8,128)(2,1)} fusion(bf16[1024,4096]{1,0:T(8,128)(2,1)} %copy-done.19, bf16[1024,1024]{1,0:T(8,128)(2,1)S(1)} %fusion.166), kind=kOutput, calls=%fused_computation.13 | convolution fusion | flops 10759438336 | bytes 18874368 | tf_op jit(solution)/shard_map/dot_general | solution.py:23
  1031.8 15.1 fusion.167
  1046.9 19.0 %add_convert_fusion.1 = bf16[1024,4096]{1,0:T(8,128)(2,1)} fusion(bf16[1024,4096]{1,0:T(8,128)(2,1)} %add_convert_fusion.2, bf16[1024,1024]{1,0:T(8,128)(2,1)S(1)} %fusion.167), kind=kOutput, calls=%fused_computation.12 | convolution fusion | flops 10759438336 | bytes 18874368 | tf_op jit(solution)/shard_map/dot_general | solution.py:23
  1065.9 14.7 fusion.168
  1080.6 21.1 %fusion.4 = (bf16[4096,1024]{0,1:T(8,128)(2,1)}, bf16[1024,4096]{1,0:T(8,128)(2,1)}) fusion(pred[]{:T(512)S(6)} %eq.20, pred[]{:T(512)S(6)} %eq.19, bf16[1024,4096]{1,0:T(8,128)(2,1)} %add_convert_fusion.1, bf16[1024,1024]{1,0:T(8,128)(2,1)S(1)} %fusion.168), kind=kOutput, calls=%fused_computation.14 | convolution fusion | flops 10780409856 | bytes 27262978 | tf_op jit(solution)/shard_map/dot_general | solution.py:23
  1102.0 44.9 %all-gather.17.cloned.1.call-done = bf16[4,1024,1024]{2,1,0:T(8,128)(2,1)} async-done(((bf16[4,128,1024]{2,1,0:T(8,128)(2,1)}), bf16[4,1024,1024]{2,1,0:T(8,128)(2,1)}) %all-gather.17.cloned.1.call-update) | async-done | bytes 8388624 | tf_op jit(solution)/shard_map/all_gather | solution.py:298
  1154.7 8.9 add_convert_fusion.10
  1169.6 8.9 add_convert_fusion.8
  1184.7 9.0 fusion.25
  1217.1 7.1 fusion.91
  1225.3 10.3 psum.39
  1241.7 26.8 %reduce-scatter.26.cloned.1.call-done = bf16[512,1024]{0,1:T(8,128)(2,1)} async-done(((bf16[4096,1024]{0,1:T(8,128)(2,1)}), bf16[512,1024]{0,1:T(8,128)(2,1)}) %reduce-scatter.26.cloned.1.call-update) | async-done | bytes 1048592 | tf_op jit(solution)/shard_map/reduce_scatter | solution.py:327
  1277.8 80.9 %reduce-scatter.20.cloned.1.call-done = bf16[4,128,1024]{2,1,0:T(8,128)(2,1)} async-done(((bf16[4,1024,1024]{2,1,0:T(8,128)(2,1)}), bf16[4,128,1024]{2,1,0:T(8,128)(2,1)}) %reduce-scatter.20.cloned.1.call-update) | async-done | bytes 1048592 | tf_op jit(solution)/shard_map/reduce_scatter | solution.py:318
  1362.0 86.8 %reduce-scatter.22.cloned.1.call-done = bf16[4,128,1024]{2,1,0:T(8,128)(2,1)} async-done(((bf16[4,1024,1024]{2,1,0:T(8,128)(2,1)}), bf16[4,128,1024]{2,1,0:T(8,128)(2,1)}) %reduce-scatter.22.cloned.1.call-update) | async-done | bytes 1048592 | tf_op jit(solution)/shard_map/reduce_scatter | solution.py:321
  1453.0 86.0 %reduce-scatter.24.cloned.1.call-done = bf16[128,4096]{1,0:T(8,128)(2,1)} async-done(((bf16[1024,4096]{1,0:T(8,128)(2,1)}), bf16[128,4096]{1,0:T(8,128)(2,1)}) %reduce-scatter.24.cloned.1.call-update) | async-done | bytes 1048592 | tf_op jit(solution)/shard_map/reduce_scatter | solution.py:324
  (290 shorter events, 225.1 us)
Async XLA Ops:
  7.2 170.7 %copy-start = (bf16[1,384,1024]{2,1,0:T(8,128)(2,1)S(1)}, bf16[1,384,1024]{2,1,0:T(8,128)(2,1)}, u32[]{:S(2)}) copy-start(bf16[1,384,1024]{2,1,0:T(8,128)(2,1)} %param.16) | copy-start | bytes 2359300
  7.2 87.9 %all-gather.9.cloned.1.call-start = ((), (), s32[]{:S(2)}) async-start(), calls=%async_computation.9 | async-start | bytes 9437184 | tf_op jit(solution)/shard_map/all_gather | solution.py:172
  10.2 167.7 %all-gather.11.cloned.1.call-start = ((), (), s32[]{:S(2)}) async-start(), calls=%async_computation.10 | async-start | bytes 9437184 | tf_op jit(solution)/shard_map/all_gather | solution.py:173
  11.4 249.3 %all-gather.13.cloned.1.call-start = ((), (), s32[]{:S(2)}) async-start(), calls=%async_computation.11 | async-start | bytes 9437184 | tf_op jit(solution)/shard_map/all_gather | solution.py:174
  14.2 329.1 %all-gather.15.cloned.1.call-start = ((), (), s32[]{:S(2)}) async-start(), calls=%async_computation.12 | async-start | bytes 9437184 | tf_op jit(solution)/shard_map/all_gather | solution.py:175
  17.0 416.6 %reduce-scatter.18.cloned.1.call-start = ((), (), s32[]{:S(2)}) async-start(), calls=%async_computation.16 | async-start | bytes 9437184 | tf_op jit(solution)/shard_map/reduce_scatter | solution.py:276
  18.6 819.6 %copy-start.53 = (f32[256]{0:T(256)}, f32[256]{0:T(256)S(1)}, u32[]{:S(2)}) copy-start(f32[256]{0:T(256)S(1)} %broadcast_multiply_fusion.8) | copy-start | bytes 3076
  18.9 819.3 %copy-start.56 = (f32[256]{0:T(256)}, f32[256]{0:T(256)S(1)}, u32[]{:S(2)}) copy-start(f32[256]{0:T(256)S(1)} %add_rsqrt_fusion.2) | copy-start | bytes 3076
  18.9 819.3 %copy-start.51 = (f32[1,1,1024]{2,0,1:T(1,128)}, f32[1,1,1024]{2,0,1:T(1,128)S(1)}, u32[]{:S(2)}) copy-start(f32[1,1,1024]{2,0,1:T(1,128)S(1)} %get-tuple-element.135) | copy-start | bytes 12292
  97.6 87.4 %copy-start.35 = (bf16[256,1024]{0,1:T(8,128)(2,1)}, bf16[256,1024]{0,1:T(8,128)(2,1)S(1)}, u32[]{:S(2)}) copy-start(bf16[256,1024]{0,1:T(8,128)(2,1)S(1)} %copy.92) | copy-start | bytes 1572868
  100.4 83.2 %copy-start.23 = (bf16[256,1024]{0,1:T(8,128)(2,1)}, bf16[256,1024]{0,1:T(8,128)(2,1)S(1)}, u32[]{:S(2)}) copy-start(bf16[256,1024]{0,1:T(8,128)(2,1)S(1)} %copy.93) | copy-start | bytes 1572868
  103.2 80.4 %copy-start.25 = (bf16[256,1024]{0,1:T(8,128)(2,1)}, bf16[256,1024]{0,1:T(8,128)(2,1)S(1)}, u32[]{:S(2)}) copy-start(bf16[256,1024]{0,1:T(8,128)(2,1)S(1)} %copy.94) | copy-start | bytes 1572868
  208.8 208.1 %copy-start.9 = (f32[256,1024]{1,0:T(8,128)}, f32[256,1024]{1,0:T(8,128)S(1)}, u32[]{:S(2)}) copy-start(f32[256,1024]{1,0:T(8,128)S(1)} %get-tuple-element.144) | copy-start | bytes 3145732
  260.7 7.8 copy-start.49
  273.5 250.3 %reduce-scatter.12.cloned.1.call-start = ((), (), s32[]{:S(2)}) async-start(), calls=%async_computation.13 | async-start | bytes 9437184 | tf_op jit(solution)/shard_map/reduce_scatter | solution.py:267
  400.3 213.8 %reduce-scatter.14.cloned.1.call-start = ((), (), s32[]{:S(2)}) async-start(), calls=%async_computation.14 | async-start | bytes 9437184 | tf_op jit(solution)/shard_map/reduce_scatter | solution.py:270
  416.8 287.5 %reduce-scatter.16.cloned.1.call-start = ((), (), s32[]{:S(2)}) async-start(), calls=%async_computation.15 | async-start | bytes 9437184 | tf_op jit(solution)/shard_map/reduce_scatter | solution.py:273
  424.3 387.0 %all-reduce.3.cloned.1.call-start = ((), (), s32[]{:S(2)}) async-start(), calls=%async_computation.26 | async-start | bytes 8388608 | tf_op jit(solution)/shard_map/psum | solution.py:287
  704.4 194.0 %all-gather.23.cloned.1.call-start = ((), (), s32[]{:S(2)}) async-start(), calls=%async_computation.22 | async-start | bytes 9437184 | tf_op jit(solution)/shard_map/all_gather | solution.py:300
  816.2 165.1 %all-gather.21.cloned.1.call-start = ((), (), s32[]{:S(2)}) async-start(), calls=%async_computation.21 | async-start | bytes 9437184 | tf_op jit(solution)/shard_map/all_gather | solution.py:301
  823.0 279.1 %all-gather.19.cloned.1.call-start = ((), (), s32[]{:S(2)}) async-start(), calls=%async_computation.18 | async-start | bytes 9437184 | tf_op jit(solution)/shard_map/all_gather | solution.py:299
  828.1 318.9 %all-gather.17.cloned.1.call-start = ((), (), s32[]{:S(2)}) async-start(), calls=%async_computation.17 | async-start | bytes 9437184 | tf_op jit(solution)/shard_map/all_gather | solution.py:298
  832.9 391.2 %reduce-scatter.28.cloned.1.call-start = ((), (), s32[]{:S(2)}) async-start(), calls=%async_computation.25 | async-start | bytes 294912
  844.0 424.5 %reduce-scatter.26.cloned.1.call-start = ((), (), s32[]{:S(2)}) async-start(), calls=%async_computation.24 | async-start | bytes 9437184 | tf_op jit(solution)/shard_map/reduce_scatter | solution.py:327
  1101.8 256.9 %reduce-scatter.20.cloned.1.call-start = ((), (), s32[]{:S(2)}) async-start(), calls=%async_computation.19 | async-start | bytes 9437184 | tf_op jit(solution)/shard_map/reduce_scatter | solution.py:318
  1204.2 244.6 %reduce-scatter.22.cloned.1.call-start = ((), (), s32[]{:S(2)}) async-start(), calls=%async_computation.20 | async-start | bytes 9437184 | tf_op jit(solution)/shard_map/reduce_scatter | solution.py:321
  1204.8 334.2 %reduce-scatter.24.cloned.1.call-start = ((), (), s32[]{:S(2)}) async-start(), calls=%async_computation.23 | async-start | bytes 9437184 | tf_op jit(solution)/shard_map/reduce_scatter | solution.py:324
  1217.1 19.1 %copy-start.58 = (f32[2,3,128]{2,0,1:T(2,128)S(1)}, f32[2,3,128]{2,0,1:T(2,128)}, u32[]{:S(2)}) copy-start(f32[2,3,128]{2,0,1:T(2,128)} %param.29) | copy-start | bytes 9220
  1224.2 15.8 %copy-start.18 = (f32[512,1024]{0,1:T(8,128)S(1)}, f32[512,1024]{0,1:T(8,128)}, u32[]{:S(2)}) copy-start(f32[512,1024]{0,1:T(8,128)} %get-tuple-element.115) | copy-start | bytes 6291460
  1272.5 86.2 %copy-start.15 = (f32[4,128,1024]{2,1,0:T(8,128)S(1)}, f32[4,128,1024]{2,1,0:T(8,128)}, u32[]{:S(2)}) copy-start(f32[4,128,1024]{2,1,0:T(8,128)} %param.20) | copy-start | bytes 6291460
  1362.0 176.9 %copy-start.17 = (f32[128,4096]{1,0:T(8,128)S(1)}, f32[128,4096]{1,0:T(8,128)}, u32[]{:S(2)}) copy-start(f32[128,4096]{1,0:T(8,128)} %param.22) | copy-start | bytes 6291460
  1448.8 93.4 %copy-start.1 = (bf16[1,384,1024]{2,1,0:T(8,128)(2,1)S(1)}, bf16[1,384,1024]{2,1,0:T(8,128)(2,1)}, u32[]{:S(2)}) copy-start(bf16[1,384,1024]{2,1,0:T(8,128)(2,1)} %param.16) | copy-start | bytes 2359300
  (52 other events, 186.0 us)
Sparse Core Ops, SparseCore 0:
  10.3 84.7 all-gather.8
  97.3 80.5 all-gather.10
  180.1 80.5 all-gather.12
  262.7 80.5 all-gather.14
  345.5 88.1 reduce-scatter.17
  435.8 87.9 reduce-scatter.11
  526.1 87.9 reduce-scatter.13
  616.4 87.9 reduce-scatter.15
  708.0 103.2 all-reduce.2
  816.3 82.0 all-gather.22
  900.7 80.5 all-gather.20
  983.4 80.5 all-gather.18
  1066.3 80.5 all-gather.16
  1149.7 28.8 reduce-scatter.27
  1180.8 87.7 reduce-scatter.25
  1270.7 87.9 reduce-scatter.19
  1360.8 87.9 reduce-scatter.21
  1451.0 87.9 reduce-scatter.23
where the time goes:
time: 1560 us; the launch traced here: 1550 us
  waiting for transfers between devices  1120 us (72%)
  matrix products  264 us (17%)
  other arithmetic  84.7 us (5%)
  local copies, waits for them, and re-layouts  47.6 us (3%)
  between operations  18.7 us (1%)
    dot_general x16, matrix products, matmul(): return jnp.dot(left, right, preferred_element_type=jnp.float32)  121 us
    psum x1, waiting for transfers between devices, on_device(): lax.psum(reduced[3].astype(jnp.bfloat16), 'rep').astype(jnp.float32)  107 us
    dot_general x16, matrix products, matmul_right_t(): lax.dot_general(left, right, (((1,), (1,)), ((), ())), preferred_element_...  95.5 us
    reduce_scatter x1, waiting for transfers between devices, on_device(): lax.psum_scatter(cross_local.astype(jnp.bfloat16), 'shard', scatter_dimen...  90.3 us
    reduce_scatter x1, waiting for transfers between devices, on_device(): lax.psum_scatter(in_grad.astype(jnp.bfloat16), 'shard', scatter_dimension...  90.3 us
    reduce_scatter x1, waiting for transfers between devices, on_device(): lax.psum_scatter(self_local.astype(jnp.bfloat16), 'shard', scatter_dimens...  90.1 us
    reduce_scatter x1, waiting for transfers between devices, on_device(): lax.psum_scatter(square_terms[4:].astype(jnp.bfloat16), 'shard', scatter_...  86.8 us
    reduce_scatter x1, waiting for transfers between devices, on_device(): lax.psum_scatter(in_term.astype(jnp.bfloat16), 'shard', scatter_dimension...  86 us
  transfers between devices with their start and end apart: 18, of which 16 were waited for; matrix products, arithmetic and copies ran while one was open for 24% of the time, Pallas kernels for 0%

commit v1 on v0

v1 whole, which is shorter than its diff:
```python
import math

import jax
import jax.numpy as jnp
from jax import lax
from jax.experimental import pallas as pl
from jax.experimental.pallas import tpu as pltpu
from jax.sharding import PartitionSpec as P

HEADS = 16
HEAD_DIM = 64
NS_STEPS = 3


NORM_EPSILON = 1e-05
MOMENTUM_DECAY = 0.9
MATRIX_RATE = 0.6
VECTOR_RATE = 0.05
SCHULZ_FIRST = 3.4445
SCHULZ_SECOND = -4.775
SCHULZ_THIRD = 2.0315


def matmul(left, right):
    return jnp.dot(left, right, preferred_element_type=jnp.float32)


def matmul_left_t(left, right):
    return lax.dot_general(
        left, right, (((0,), (0,)), ((), ())), preferred_element_type=jnp.float32
    )


def matmul_right_t(left, right):
    return lax.dot_general(
        left, right, (((1,), (1,)), ((), ())), preferred_element_type=jnp.float32
    )


def normalize_parts(values, gain, bias):
    centered = values - jnp.mean(values, axis=-1, keepdims=True)
    inverse = lax.rsqrt(jnp.mean(centered * centered, axis=-1, keepdims=True) + NORM_EPSILON)
    unit_part = centered * inverse
    return (unit_part * gain + bias, unit_part, inverse)


def normalize_back(grad_out, unit_part, inverse, gain):
    grad_unit = grad_out * gain
    grad_in = inverse * (
        grad_unit
        - jnp.mean(grad_unit, axis=-1, keepdims=True)
        - unit_part * jnp.mean(grad_unit * unit_part, axis=-1, keepdims=True)
    )
    return (grad_in, jnp.sum(grad_out * unit_part, axis=0), jnp.sum(grad_out, axis=0))


PAIR = 2 * HEAD_DIM
SMALL = pl.CostEstimate(flops=1024, bytes_accessed=1024, transcendentals=0)


def attention_parts(count_ref, causal, query_part, keys, is_first):
    lane = lax.broadcasted_iota(jnp.int32, (1, PAIR), 1)
    own = (lane < HEAD_DIM) == is_first
    scores = matmul_right_t(jnp.where(own, query_part, 0), keys) * HEAD_DIM ** (-0.5)
    key_place = lax.broadcasted_iota(jnp.int32, scores.shape, 1)
    valid = key_place < count_ref[0]
    if causal:
        valid = valid & (key_place <= lax.broadcasted_iota(jnp.int32, scores.shape, 0))
    scores = jnp.where(valid, scores, -jnp.inf)
    exponent = jnp.exp(scores - jnp.max(scores, axis=-1, keepdims=True))
    return exponent / jnp.sum(exponent, axis=-1, keepdims=True), own


def head_pairs(width, body):
    def step(index, carry):
        body(pl.ds(pl.multiple_of(index * PAIR, PAIR), PAIR))
        return carry

    lax.fori_loop(0, width // PAIR, step, 0)


def attention_call(kernel, out_shapes, count, arrays, waited):
    rows, width = arrays[0].shape
    keys = arrays[1].shape[0]
    vmem = pl.BlockSpec(memory_space=pltpu.VMEM)
    return pl.pallas_call(
        kernel,
        out_shape=tuple(out_shapes),
        in_specs=[pl.BlockSpec(memory_space=pltpu.SMEM)]
        + [vmem] * len(arrays)
        + [pl.BlockSpec(memory_space=pl.ANY)] * len(waited),
        out_specs=tuple([vmem] * len(out_shapes)),
        compiler_params=pltpu.CompilerParams(vmem_limit_bytes=56 * 2**20),
        cost_estimate=SMALL,
    )(count, *arrays, *waited)


def attend_forward(query_rows, incoming_keys, incoming_values, count, causal, *waited):
    def kernel(count_ref, query_ref, key_ref, value_ref, *refs):
        mixed_ref = refs[-1]

        def one_pair(columns):
            query_part, keys = query_ref[:, columns], key_ref[:, columns]
            values = value_ref[:, columns]
            mixed = None
            for is_first in (True, False):
                weights, own = attention_parts(count_ref, causal, query_part, keys, is_first)
                here = matmul(weights.astype(jnp.bfloat16), values)
                mixed = here if mixed is None else jnp.where(own, here, mixed)
            mixed_ref[:, columns] = mixed.astype(jnp.bfloat16)

        head_pairs(query_ref.shape[1], one_pair)

    return attention_call(
        kernel,
        [low(*query_rows.shape)],
        count,
        [query_rows, incoming_keys, incoming_values],
        waited,
    )[0]


def attend_backward(
    query_rows, incoming_keys, incoming_values, count, causal, grad_mixed, *waited
):
    def kernel(count_ref, query_ref, key_ref, value_ref, grad_ref, *refs):
        grad_query, grad_keys, grad_values = refs[-3:]
        scale = HEAD_DIM ** (-0.5)

        def one_pair(columns):
            query_part, keys = query_ref[:, columns], key_ref[:, columns]
            values, grads = value_ref[:, columns], grad_ref[:, columns]
            found = None
            for is_first in (True, False):
                weights, own = attention_parts(count_ref, causal, query_part, keys, is_first)
                grad_prob = matmul_right_t(jnp.where(own, grads, 0), values)
                shift = jnp.sum(grad_prob * weights, axis=-1, keepdims=True)
                score_grad = (weights * (grad_prob - shift)).astype(jnp.bfloat16)
                here = (
                    matmul(score_grad, keys) * scale,
                    matmul_left_t(score_grad, query_part) * scale,
                    matmul_left_t(weights.astype(jnp.bfloat16), grads),
                )
                if found is None:
                    found = here
                else:
                    found = [jnp.where(own, new, old) for new, old in zip(here, found)]
            for ref, value in zip((grad_query, grad_keys, grad_values), found):
                ref[:, columns] = value.astype(jnp.bfloat16)

        head_pairs(query_ref.shape[1], one_pair)

    return attention_call(
        kernel,
        [low(*query_rows.shape), low(*incoming_keys.shape), low(*incoming_keys.shape)],
        count,
        [query_rows, incoming_keys, incoming_values, grad_mixed],
        waited,
    )


TILE = 256


def in_tiles(size, body):
    def step(index, carry):
        body(pl.ds(pl.multiple_of(index * TILE, TILE), TILE))
        return carry

    lax.fori_loop(0, size // TILE, step, 0)


def wide_view(ref, rows):
    return ref[rows, :].astype(jnp.float32)


def first_and_opposite(rows, total):
    return slice(0, rows), slice(total // 2, total // 2 + rows)


def square_schulz(mine, sibling, rows, *waited):
    size = mine.shape[1]
    half = mine.shape[0]

    def kernel(mine_ref, sibling_ref, *refs):
        result, current, gram, poly, total = refs[len(waited) :]
        current[:half], current[half:] = mine_ref[...], sibling_ref[...]
        total[...] = jnp.zeros_like(total)

        def add_squares(rows):
            part = wide_view(current, rows)
            total[...] += jnp.sum(part * part, axis=0, keepdims=True)

        in_tiles(size, add_squares)
        scale = 1.0 / (jnp.sqrt(jnp.sum(total[...])) + 1e-07)

        def scaled(rows):
            current[rows, :] = (wide_view(current, rows) * scale).astype(jnp.bfloat16)

        in_tiles(size, scaled)
        for sweep_index in range(NS_STEPS):

            def gram_rows(rows):
                gram[rows, :] = matmul_right_t(current[rows, :], current[...]).astype(
                    jnp.bfloat16
                )

            def poly_rows(rows):
                poly[rows, :] = (
                    SCHULZ_SECOND * wide_view(gram, rows)
                    + SCHULZ_THIRD * matmul(gram[rows, :], gram[...])
                ).astype(jnp.bfloat16)

            def next_rows(rows):
                gram[rows, :] = (
                    SCHULZ_FIRST * wide_view(current, rows) + matmul(poly[rows, :], current[...])
                ).astype(jnp.bfloat16)

            in_tiles(size, gram_rows)
            if sweep_index == NS_STEPS - 1:
                for block, here in enumerate(first_and_opposite(rows, half)):
                    poly_rows(here)
                    result[block] = (
                        SCHULZ_FIRST * wide_view(current, here)
                        + matmul(poly[here, :], current[...])
                    ).astype(jnp.bfloat16)
            else:
                in_tiles(size, poly_rows)
                in_tiles(size, next_rows)
                current[...] = gram[...]

    vmem = pl.BlockSpec(memory_space=pltpu.VMEM)
    return pl.pallas_call(
        kernel,
        out_shape=low(2, rows, size),
        in_specs=[vmem] * 2 + [pl.BlockSpec(memory_space=pl.ANY)] * len(waited),
        out_specs=vmem,
        scratch_shapes=[pltpu.VMEM((size, size), jnp.bfloat16)] * 3
        + [pltpu.VMEM((1, size), jnp.float32)],
        compiler_params=pltpu.CompilerParams(vmem_limit_bytes=56 * 2**20),
        cost_estimate=SMALL,
    )(mine, sibling, *waited)


def gram_parts(place, mine, sibling, reps, *waited):
    size = mine.shape[1]
    half = mine.shape[0]
    part = size // (2 * reps)

    def kernel(place_ref, mine_ref, sibling_ref, *refs):
        to_x, to_y, kept, later, both, gram = refs[len(waited) :]
        both[:half], both[half:] = mine_ref[...], sibling_ref[...]
        is_lower = place_ref[3] == 1

        def row_products(rows):
            gram[rows, :] = matmul_right_t(both[rows, :], both[...]).astype(jnp.bfloat16)

        def column_products(columns):
            gram[columns, :] = matmul_left_t(both[:, columns], both[...]).astype(jnp.bfloat16)

        @pl.when(is_lower)
        def _():
            in_tiles(size, row_products)

        @pl.when(jnp.logical_not(is_lower))
        def _():
            in_tiles(size, column_products)

        def piece(step, index):
            first_row = (place_ref[0] ^ step) * (2 * part) + index * part
            return gram[pl.ds(pl.multiple_of(first_row, part), part), :]

        to_x[0, 0], to_x[0, 1] = piece(1, 0), piece(3, 0)
        to_y[0, 0], to_y[0, 1] = piece(2, 1), piece(3, 1)
        kept[0, 0], kept[0, 1] = piece(0, 0), piece(0, 1)
        later[0, 0], later[0, 1] = piece(2, 0), piece(1, 1)

    vmem = pl.BlockSpec(memory_space=pltpu.VMEM)
    return pl.pallas_call(
        kernel,
        out_shape=tuple([low(1, 2, part, size)] * 4),
        in_specs=[pl.BlockSpec(memory_space=pltpu.SMEM)]
        + [vmem] * 2
        + [pl.BlockSpec(memory_space=pl.ANY)] * len(waited),
        out_specs=tuple([vmem] * 4),
        scratch_shapes=[pltpu.VMEM((size, size), jnp.bfloat16)] * 2,
        compiler_params=pltpu.CompilerParams(vmem_limit_bytes=56 * 2**20),
        cost_estimate=SMALL,
    )(place, mine, sibling, *waited)


def gram_schulz(place, quarters, mine, sibling, rows, *waited):
    size = mine.shape[1]
    half_rows = mine.shape[0]
    part = quarters[0].shape[0]

    def kernel(place_ref, q_ref, x_ref, y_ref, a_ref, b_ref, mine_ref, sibling_ref, *refs):
        result, gram, product, current, poly, half, unit = refs[len(waited) :]
        my_rep = place_ref[0]

        def put(step, offset, ref):
            first_row = (my_rep ^ step) * part + offset
            size_here = ref.shape[0]
            gram[pl.ds(pl.multiple_of(first_row, size_here), size_here), :] = ref[...]

        put(0, 0, q_ref)
        put(1, 0, x_ref)
        put(2, 0, y_ref)
        put(3, 0, a_ref)
        put(3, part // 2, b_ref)

        def trace_of(index, total):
            rows = pl.ds(pl.multiple_of(index * TILE, TILE), TILE)
            here = wide_view(gram, rows)
            row_number = lax.broadcasted_iota(jnp.int32, here.shape, 0) + index * TILE
            column_number = lax.broadcasted_iota(jnp.int32, here.shape, 1)
            return total + jnp.sum(jnp.where(row_number == column_number, here, 0.0))

        trace = lax.fori_loop(0, size // TILE, trace_of, jnp.float32(0.0))
        scale = (1.0 / (jnp.sqrt(jnp.full((8, 128), trace)) + 1e-07))[0:1, 0:1]
        unit[:half_rows] = (mine_ref[...].astype(jnp.float32) * scale).astype(jnp.bfloat16)
        unit[half_rows:] = (sibling_ref[...].astype(jnp.float32) * scale).astype(jnp.bfloat16)

        def scaled(rows):
            current[rows, :] = (wide_view(gram, rows) * (scale * scale)).astype(jnp.bfloat16)

        in_tiles(size, scaled)
        factor = 1.0
        for sweep_index in range(NS_STEPS):

            def poly_rows(rows):
                poly[rows, :] = (
                    SCHULZ_SECOND * wide_view(current, rows)
                    + SCHULZ_THIRD * matmul(current[rows, :], current[...])
                ).astype(jnp.bfloat16)

            def product_rows(rows):
                half[rows, :] = (
                    SCHULZ_FIRST * wide_view(product, rows)
                    + factor * wide_view(poly, rows)
                    + matmul(poly[rows, :], product[...])
                ).astype(jnp.bfloat16)

            def half_rows_of(rows):
                half[rows, :] = (
                    SCHULZ_FIRST * wide_view(current, rows) + matmul(poly[rows, :], current[...])
                ).astype(jnp.bfloat16)

            def current_rows(rows):
                current[rows, :] = (
                    SCHULZ_FIRST * wide_view(half, rows) + matmul(half[rows, :], poly[...])
                ).astype(jnp.bfloat16)

            in_tiles(size, poly_rows)
            if sweep_index == 0:
                product[...] = poly[...]
            else:
                in_tiles(size, product_rows)
                product[...] = half[...]
            factor = factor * SCHULZ_FIRST
            if sweep_index < NS_STEPS - 1:
                in_tiles(size, half_rows_of)
                in_tiles(size, current_rows)

        is_lower = place_ref[3] == 1
        for block, here in enumerate(first_and_opposite(rows, half_rows)):
            plain = factor * wide_view(unit, here)

            @pl.when(is_lower)
            def _():
                turned = matmul(product[here, :], unit[...])
                result[block] = (plain + turned).astype(jnp.bfloat16)

            @pl.when(jnp.logical_not(is_lower))
            def _():
                turned = matmul(unit[here, :], product[...])
                result[block] = (plain + turned).astype(jnp.bfloat16)

    vmem = pl.BlockSpec(memory_space=pltpu.VMEM)
    return pl.pallas_call(
        kernel,
        out_shape=low(2, rows, size),
        in_specs=[pl.BlockSpec(memory_space=pltpu.SMEM)]
        + [vmem] * 7
        + [pl.BlockSpec(memory_space=pl.ANY)] * len(waited),
        out_specs=vmem,
        scratch_shapes=[pltpu.VMEM((size, size), jnp.bfloat16)] * 6,
        compiler_params=pltpu.CompilerParams(vmem_limit_bytes=56 * 2**20),
        cost_estimate=SMALL,
    )(place, *quarters, mine, sibling, *waited)


def low(*shape):
    return jax.ShapeDtypeStruct(shape, jnp.bfloat16)


def fresh_blocks(place, own, arrived, moments, *waited):
    kinds, rows, width = own.shape
    chips = len(arrived) + 1

    def kernel(place_ref, own_ref, *refs):
        arrived_refs = refs[: chips - 1]
        moment_ref = refs[chips - 1]
        grad_ref, *out = refs[chips + len(waited) : -1]
        fresh_ref = refs[-1]
        for kind in range(kinds):
            grad_ref[kind] = add_low(own_ref[kind], *[ref[kind] for ref in arrived_refs])
            fresh_ref[kind] = (
                MOMENTUM_DECAY * moment_ref[kind] + grad_ref[kind].astype(jnp.float32)
            ).astype(jnp.bfloat16)
        for turn in range(chips):
            chip = lax.rem(place_ref[1] + chips - turn, chips)
            out[turn][...] = fresh_ref[jnp.where(chip < chips // 2, 0, 1)]

    vmem = pl.BlockSpec(memory_space=pltpu.VMEM)
    return pl.pallas_call(
        kernel,
        out_shape=tuple([low(kinds, rows, width)] + [low(rows, width)] * chips),
        in_specs=[pl.BlockSpec(memory_space=pltpu.SMEM)]
        + [vmem] * (chips + 1)
        + [pl.BlockSpec(memory_space=pl.ANY)] * len(waited),
        out_specs=tuple([vmem] * (chips + 1)),
        scratch_shapes=[pltpu.VMEM((kinds, rows, width), jnp.bfloat16)],
        compiler_params=pltpu.CompilerParams(vmem_limit_bytes=56 * 2**20),
        cost_estimate=SMALL,
    )(place, own, *arrived, moments, *waited)


def first_seen(arrays):
    kept, index = [], []
    for array in arrays:
        found = [place for place, other in enumerate(kept) if other is array]
        if not found:
            kept.append(array)
        index.append(found[0] if found else len(kept) - 1)
    return kept, index


def weight_rows(place, kinds, received=None, waited=()):
    count = len(kinds)
    steps = len(kinds[0][0])
    rows, width = kinds[0][0][0].shape[1] // 2, kinds[0][1][0].shape[1]
    half = rows // 2
    is_own = received is not None
    aligned = all(kind[2] % 128 == 0 for kind in kinds)
    lefts, left_index = first_seen([left for kind in kinds for left in kind[0]])
    rights, right_index = first_seen([right for kind in kinds for right in kind[1]])
    core_rows = [
        kinds[left_index.index(index) // steps][2] for index in range(len(lefts))
    ]
    if not aligned:
        def chosen(left, size):
            cut = left.reshape(left.shape[0], -1, 2, size)
            first_core = (place[2] == 0) if is_own else (place[2] == 1)
            return jnp.where(first_core, cut[:, :, 0], cut[:, :, 1]).reshape(left.shape[0], rows)

        lefts = [chosen(left, size) for left, size in zip(lefts, core_rows)]
    arrays = lefts + rights + (list(received) if is_own else [])

    def kernel(place_ref, *refs):
        left_refs = refs[: len(lefts)]
        right_refs = refs[len(lefts) : len(lefts) + len(rights)]
        received_refs = refs[len(lefts) + len(rights) : len(arrays)]
        rest = refs[len(arrays) + len(waited) :]
        core = place_ref[2] if is_own else 1 - place_ref[2]

        def columns(index):
            ref, size = left_refs[index], core_rows[index]
            if not aligned:
                return ref[...]
            parts = [
                ref[:, pl.ds(pl.multiple_of((2 * chip + core) * size, 128), size)]
                for chip in range(rows // size)
            ]
            return jnp.concatenate(parts, axis=1)

        for kind in range(count):
            for block in range(steps):
                spot = kind * steps + block
                total = matmul_left_t(
                    columns(left_index[spot]), right_refs[right_index[spot]][...]
                )
                step = (place_ref[0] ^ block) if kinds[kind][3] else block
                if is_own:
                    total = total + received_refs[kind][step].astype(jnp.float32)
                    rest[4][kind, step] = total.astype(jnp.bfloat16)
                else:
                    rest[kind][step] = total.astype(jnp.bfloat16)
            if is_own:
                to_x, to_y, kept, later, sums = rest
                to_x[kind, 0], to_x[kind, 1] = sums[kind, 1, :half], sums[kind, 3, :half]
                to_y[kind, 0], to_y[kind, 1] = sums[kind, 2, half:], sums[kind, 3, half:]
                kept[kind, 0], kept[kind, 1] = sums[kind, 0, :half], sums[kind, 0, half:]
                later[kind, 0], later[kind, 1] = sums[kind, 2, :half], sums[kind, 1, half:]

    if is_own:
        out_shapes = [low(count, 2, half, width)] * 4
    else:
        out_shapes = [low(steps, rows, width)] * count
    vmem = pl.BlockSpec(memory_space=pltpu.VMEM)
    flops = sum(2 * rows * width * left.shape[0] for kind in kinds for left in kind[0])
    return pl.pallas_call(
        kernel,
        out_shape=tuple(out_shapes),
        in_specs=[pl.BlockSpec(memory_space=pltpu.SMEM)]
        + [vmem] * len(arrays)
        + [pl.BlockSpec(memory_space=pl.ANY)] * len(waited),
        out_specs=tuple([vmem] * len(out_shapes)),
        scratch_shapes=(
            [pltpu.VMEM((count, steps, rows, width), jnp.bfloat16)] if is_own else []
        ),
        compiler_params=pltpu.CompilerParams(vmem_limit_bytes=56 * 2**20),
        cost_estimate=SMALL,
    )(place, *arrays, *waited)


def later_sums(later, by_x, by_y, waited):
    def kernel(later_ref, x_ref, y_ref, *refs):
        to_y, to_x = refs[-2:]
        for kind in range(later_ref.shape[0]):
            to_y[kind] = add_low(later_ref[kind, 0], x_ref[kind, 1])
            to_x[kind] = add_low(later_ref[kind, 1], y_ref[kind, 1])

    vmem = pl.BlockSpec(memory_space=pltpu.VMEM)
    shape = low(later.shape[0], *later.shape[2:])
    return pl.pallas_call(
        kernel,
        out_shape=(shape, shape),
        in_specs=[vmem] * 3 + [pl.BlockSpec(memory_space=pl.ANY)] * len(waited),
        out_specs=(vmem, vmem),
        compiler_params=pltpu.CompilerParams(vmem_limit_bytes=56 * 2**20),
        cost_estimate=SMALL,
    )(later, by_x, by_y, *waited)


def held_until(value, *waited):
    def kernel(*refs):
        del refs

    anywhere = pl.BlockSpec(memory_space=pl.ANY)
    return pl.pallas_call(
        kernel,
        out_shape=jax.ShapeDtypeStruct(value.shape, value.dtype),
        in_specs=[anywhere] * (1 + len(waited)),
        out_specs=anywhere,
        input_output_aliases={0: 0},
        compiler_params=pltpu.CompilerParams(
            vmem_limit_bytes=56 * 2**20, has_side_effects=True
        ),
        cost_estimate=SMALL,
    )(value, *waited)


def sorted_blocks(place, kept, by_x, by_y, last_x, last_y, chips, waited):
    kinds, _, half, width = kept.shape
    rows = 2 * half // chips

    def kernel(place_ref, kept_ref, x_ref, y_ref, last_x_ref, last_y_ref, *refs):
        out, whole = refs[len(waited) : -1], refs[-1]
        for kind in range(kinds):
            whole[: chips // 2] = add_low(
                kept_ref[kind, 0], x_ref[kind, 0], last_y_ref[kind]
            ).reshape(chips // 2, rows, width)
            whole[chips // 2 :] = add_low(
                kept_ref[kind, 1], y_ref[kind, 0], last_x_ref[kind]
            ).reshape(chips // 2, rows, width)
            for turn in range(chips):
                out[turn][kind] = whole[lax.rem(place_ref[1] + turn, chips)]

    vmem = pl.BlockSpec(memory_space=pltpu.VMEM)
    return pl.pallas_call(
        kernel,
        out_shape=tuple([low(kinds, rows, width)] * chips),
        in_specs=[pl.BlockSpec(memory_space=pltpu.SMEM)]
        + [vmem] * 5
        + [pl.BlockSpec(memory_space=pl.ANY)] * len(waited),
        out_specs=tuple([vmem] * chips),
        scratch_shapes=[pltpu.VMEM((chips, rows, width), jnp.bfloat16)],
        compiler_params=pltpu.CompilerParams(vmem_limit_bytes=56 * 2**20),
        cost_estimate=SMALL,
    )(place, kept, by_x, by_y, last_x, last_y, *waited)


def held_until(value, *waited):
    def kernel(*refs):
        del refs

    anywhere = pl.BlockSpec(memory_space=pl.ANY)
    return pl.pallas_call(
        kernel,
        out_shape=jax.ShapeDtypeStruct(value.shape, value.dtype),
        in_specs=[anywhere] * (1 + len(waited)),
        out_specs=anywhere,
        input_output_aliases={0: 0},
        compiler_params=pltpu.CompilerParams(
            vmem_limit_bytes=56 * 2**20, has_side_effects=True
        ),
        cost_estimate=SMALL,
    )(value, *waited)


def stretch(shape):
    return math.sqrt(max(shape[0], shape[1]) / min(shape[0], shape[1]))


def add_low(*terms):
    total = terms[0].astype(jnp.float32)
    for term in terms[1:]:
        total = total + term.astype(jnp.float32)
    return total.astype(jnp.bfloat16)


def phase_blocks(arrived, by_x, by_y, waited):
    given = [*(arrived or []), *([by_x, by_y] if by_x is not None else [])]
    width = given[0].shape[-1]
    if arrived:
        rows, turns = arrived[0].shape[0], len(arrived)
        total = rows * turns
        half = total // 2
    else:
        total, half = 0, by_x.shape[0] // 3
    send = total + (half if by_x is not None else 0)
    came = by_x.shape[0] if by_x is not None else 0
    out_shapes = [low(send, width)] * 2 + [low(2 * came + total, width)]

    def kernel(*refs):
        inputs = list(refs[: len(given)])
        to_x, to_y, to_core = refs[len(given) + len(waited) :]
        if arrived:
            for turn in range(turns):
                here = slice(turn * rows, (turn + 1) * rows)
                block = inputs.pop(0)[...]
                to_x[here] = to_y[here] = block
                first_row = 2 * came + turn * rows
                to_core[first_row : first_row + rows] = block
        if by_x is not None:
            x_ref, y_ref = inputs.pop(0), inputs.pop(0)
            to_x[total:] = y_ref[:half]
            to_y[total:] = x_ref[half : 2 * half]
            to_core[:came], to_core[came : 2 * came] = x_ref[...], y_ref[...]

    vmem = pl.BlockSpec(memory_space=pltpu.VMEM)
    return pl.pallas_call(
        kernel,
        out_shape=tuple(out_shapes),
        in_specs=[vmem] * len(given) + [pl.BlockSpec(memory_space=pl.ANY)] * len(waited),
        out_specs=tuple([vmem] * len(out_shapes)),
        compiler_params=pltpu.CompilerParams(vmem_limit_bytes=56 * 2**20),
        cost_estimate=SMALL,
    )(*given, *waited)


def block_shares(shares):
    flat = [part[0] if isinstance(part, tuple) else part for share in shares for part in share]
    starts = [part[1] for share in shares for part in share[1:]]
    return flat, starts


def start_blocks(place_ref, flat_refs, starts, out, sem_of, kind, chips, by_rep):
    reps, rows = flat_refs[0].shape[1:3]
    turns = chips - 1
    half = turns * rows // 2
    my_rep, my_chip, my_core = place_ref[0], place_ref[1], place_ref[2]
    cuts = []
    for turn in range(turns):
        low_end, high_end = turn * rows, (turn + 1) * rows
        middle = min(max(half, low_end), high_end)
        if middle > low_end:
            cuts.append((0, low_end, turn, 0, middle - low_end))
        if high_end > middle:
            cuts.append((1, middle - half, turn, middle - low_end, high_end - middle))
    copies = [[] for step in range(reps)]

    def start(step, source, target):
        copy = pltpu.make_async_copy(source, target, sem_of(step, len(copies[step])))
        copy.start()
        copies[step].append(copy)

    for step in range(reps):
        from_rep = my_rep ^ step
        to_rep = from_rep if by_rep else step
        for side in range(2):
            core = my_core if side == 0 else 1 - my_core
            own, *moved = flat_refs[6 * side : 6 * side + 6]
            first_rows = starts[5 * side : 5 * side + 5]
            start(step, own.at[kind, from_rep], out.at[to_rep, my_chip, core])
            if step < reps - 1:
                for turn in range(turns):
                    start(
                        step,
                        moved[step].at[pl.ds(first_rows[step] + turn * rows, rows)],
                        out.at[to_rep, lax.rem(my_chip + 1 + turn, chips), core],
                    )
            else:
                for part, source_row, turn, target_row, count in cuts:
                    start(
                        step,
                        moved[3 + part].at[pl.ds(first_rows[3 + part] + source_row, count)],
                        out.at[
                            to_rep,
                            lax.rem(my_chip + 1 + turn, chips),
                            core,
                            pl.ds(target_row, count),
                        ],
                    )
    return copies


def placed_blocks(place, shares, kind, chips, waited):
    reps, rows, width = shares[0][0].shape[1:]
    flat, starts = block_shares(shares)

    def kernel(place_ref, *refs):
        results = refs[len(flat) + len(waited) : -3]
        out, sems, out_sems = refs[-3:]
        copies = start_blocks(
            place_ref,
            refs[: len(flat)],
            starts,
            out,
            lambda step, index: sems.at[step, index],
            kind,
            chips,
            True,
        )
        for step in range(reps):
            for copy in copies[step]:
                copy.wait()
        writes = [
            pltpu.make_async_copy(out.at[step], results[step], out_sems.at[step])
            for step in range(reps)
        ]
        for write in writes:
            write.start()
        for write in writes:
            write.wait()

    shape = (reps, chips, 2, rows, width)
    anywhere = pl.BlockSpec(memory_space=pl.ANY)
    full = pl.pallas_call(
        kernel,
        out_shape=tuple([low(*shape[1:])] * reps),
        in_specs=[pl.BlockSpec(memory_space=pltpu.SMEM)] + [anywhere] * (len(flat) + len(waited)),
        out_specs=tuple([anywhere] * reps),
        scratch_shapes=[
            pltpu.VMEM(shape, jnp.bfloat16),
            pltpu.SemaphoreType.DMA((reps, 2 * chips + 2)),
            pltpu.SemaphoreType.DMA((reps,)),
        ],
        compiler_params=pltpu.CompilerParams(vmem_limit_bytes=56 * 2**20),
        cost_estimate=SMALL,
    )(place, *flat, *waited)
    return [matrix.reshape(-1, width) for matrix in full]


GELU_SCALE = math.sqrt(2.0 / math.pi)
GELU_CUBE = 0.044715


def feed_forward(place, in_shares, out_shares, chips, third_low, residual, grad_branch):
    reps, rows, width = in_shares[0][0].shape[1:]
    in_flat, in_starts = block_shares(in_shares)
    out_flat, out_starts = block_shares(out_shares)
    tokens = third_low.shape[0]

    def kernel(place_ref, third_ref, residual_ref, branch_ref, *refs):
        in_refs = refs[: len(in_flat)]
        out_refs = refs[len(in_flat) : len(in_flat) + len(out_flat)]
        block_out, grad_third, *parts = refs[len(in_flat) + len(out_flat) : -3]
        hidden, grad_pre = parts[:reps], parts[reps:]
        in_full, out_full, sems = refs[-3:]
        in_copies = start_blocks(
            place_ref, in_refs, in_starts, in_full,
            lambda step, index: sems.at[0, step, index], 2, chips, False,
        )
        out_copies = start_blocks(
            place_ref, out_refs, out_starts, out_full,
            lambda step, index: sems.at[1, step, index], 3, chips, False,
        )
        for step in range(reps):
            for copy in in_copies[step]:
                copy.wait()
            in_weights = in_full[step].reshape(-1, width)
            pre = matmul(third_ref[...], in_weights)
            for copy in out_copies[step]:
                copy.wait()
            out_weights = out_full[step].reshape(-1, width)
            grad_hidden = matmul_right_t(branch_ref[...], out_weights)
            square = pre * pre
            bent = jnp.tanh(GELU_SCALE * pre * (1.0 + GELU_CUBE * square))
            units = (0.5 * pre * (1.0 + bent)).astype(jnp.bfloat16)
            slope = 0.5 * (1.0 + bent) + 0.5 * pre * (1.0 - bent * bent) * GELU_SCALE * (
                1.0 + 3.0 * GELU_CUBE * square
            )
            grads = (grad_hidden * slope).astype(jnp.bfloat16)
            hidden[step][...] = units
            grad_pre[step][...] = grads
            to_third = matmul_right_t(grads, in_weights)
            to_out = matmul(units, out_weights)
            if step == 0:
                grad_third[...] = to_third
                block_out[...] = residual_ref[...] + to_out
            else:
                grad_third[...] += to_third
                block_out[...] += to_out

    vmem = pl.BlockSpec(memory_space=pltpu.VMEM)
    whole = jax.ShapeDtypeStruct((tokens, width), jnp.float32)
    shape = (reps, chips, 2, rows, width)
    results = pl.pallas_call(
        kernel,
        out_shape=(whole, whole, *[low(tokens, width)] * (2 * reps)),
        in_specs=[pl.BlockSpec(memory_space=pltpu.SMEM)]
        + [vmem] * 3
        + [pl.BlockSpec(memory_space=pl.ANY)] * (len(in_flat) + len(out_flat)),
        out_specs=(vmem,) * (2 + 2 * reps),
        scratch_shapes=[
            pltpu.VMEM(shape, jnp.bfloat16),
            pltpu.VMEM(shape, jnp.bfloat16),
            pltpu.SemaphoreType.DMA((2, reps, 2 * chips + 2)),
        ],
        compiler_params=pltpu.CompilerParams(vmem_limit_bytes=56 * 2**20),
        cost_estimate=SMALL,
    )(place, third_low, residual, grad_branch, *in_flat, *out_flat)
    block_out, grad_third, *parts = results
    return block_out, grad_third, parts[:reps], parts[reps:]


def prepared(place, matrices, moments, shards, sub, waited):
    reps, rows, width = matrices[0].shape

    def kernel(place_ref, *refs):
        stacks, hidden_in, hidden_out = refs[0:2], refs[2], refs[3]
        old_stacks, old_in, old_out = refs[4:6], refs[6], refs[7]
        whole, *outs = refs[8 + len(waited) :]
        quarters, wide_old, square_old, sems = outs[:3], outs[3], outs[4], outs[5]
        my_rep = place_ref[0]
        copies = []

        def start(source, target):
            copy = pltpu.make_async_copy(source, target, sems.at[len(copies)])
            copy.start()
            copies.append(copy)

        for kind in range(2):
            start(old_stacks[kind].at[my_rep], square_old.at[kind])
        start(old_out.at[pl.ds(pl.multiple_of(my_rep * sub, sub), sub)], wide_old.at[1])
        for shard in range(shards):
            first = pl.multiple_of((shard * reps + my_rep) * sub, sub)
            start(
                old_in.at[:, pl.ds(first, sub)],
                wide_old.at[0, :, pl.ds(shard * sub, sub)],
            )
        for kind in range(2):
            whole[kind] = stacks[kind][...].astype(jnp.bfloat16)
        for step in range(reps):
            for shard in range(shards):
                first = (shard * reps + step) * sub
                whole[2, step, :, shard * sub : (shard + 1) * sub] = hidden_in[
                    :, first : first + sub
                ].astype(jnp.bfloat16)
            whole[3, step] = hidden_out[step * sub : (step + 1) * sub].astype(jnp.bfloat16)
        for kind in range(1, 4):
            quarters[kind - 1][...] = whole[kind, my_rep]
        for copy in copies:
            copy.wait()

    vmem = pl.BlockSpec(memory_space=pltpu.VMEM)
    anywhere = pl.BlockSpec(memory_space=pl.ANY)
    old = jax.ShapeDtypeStruct((2, rows, width), jnp.float32)
    whole, *parts, wide_old, square_old = pl.pallas_call(
        kernel,
        out_shape=(low(4, reps, rows, width), *[low(rows, width)] * 3, old, old),
        in_specs=[pl.BlockSpec(memory_space=pltpu.SMEM)]
        + [vmem] * 4
        + [anywhere] * (4 + len(waited)),
        out_specs=(vmem,) * 6,
        scratch_shapes=[pltpu.SemaphoreType.DMA((shards + 3,))],
        compiler_params=pltpu.CompilerParams(vmem_limit_bytes=56 * 2**20),
        cost_estimate=SMALL,
    )(place, *matrices, *moments, *waited)
    return whole, parts, wide_old, square_old


def on_device(
    tokens,
    states,
    cotangent,
    dec_len,
    enc_len,
    self_weights,
    cross_weights,
    fc_in,
    fc_out,
    norm_params,
    self_moment,
    cross_moment,
    fc_in_moment,
    fc_out_moment,
    norm_moment,
):
    reps = lax.axis_size("rep")
    shards = lax.axis_size("shard")
    chips = shards // 2
    my_rep = lax.axis_index("rep")
    my_place = lax.axis_index("shard")
    my_chip = my_place // 2
    my_core = lax.rem(my_place, 2)
    even = my_core == 0
    width = self_weights.shape[2]
    rows = self_weights.shape[1]
    hidden_width = fc_in.shape[1]
    sub = hidden_width // (shards * reps)

    def swap(values):
        return lax.ppermute(values, "shard", [(index, index ^ 1) for index in range(shards)])

    def from_chip(values, turn):
        pairs = [
            (2 * ((chip + turn) % chips) + core, 2 * chip + core)
            for chip in range(chips)
            for core in range(2)
        ]
        return lax.ppermute(values, "shard", pairs)

    def from_rep(values, step):
        return lax.ppermute(values, "rep", [(index ^ step, index) for index in range(reps)])

    low_bit = (my_rep & 1) == 1
    high_bit = (my_rep & 2) == 2

    def by_rep(steps):
        turned = [jnp.where(low_bit, steps[step ^ 1], steps[step]) for step in range(reps)]
        return [jnp.where(high_bit, turned[step ^ 2], turned[step]) for step in range(reps)]

    is_lower = my_chip < chips // 2
    place_now = jnp.stack([my_rep, my_chip, my_core, is_lower]).astype(jnp.int32)

    def gather_kinds(quarter, prepare):
        arrived, by_x, by_y, came = [], [], [], []
        arrived.append([from_chip(quarter, turn) for turn in range(1, chips)])
        shards, quarters, *others = prepare(arrived[0][0])
        count = shards.shape[0]
        other_shards = swap(shards)
        for phase in range(count + 1):
            waited = [came[-1]] if phase > 1 else [shards, *quarters] if phase == 0 else []
            to_x, to_y, to_core = phase_blocks(
                arrived[phase] if phase < count else None,
                by_x[-1] if phase > 0 else None,
                by_y[-1] if phase > 0 else None,
                [*waited, other_shards] if phase == 1 else waited,
            )
            if phase + 1 < count:
                quarter = held_until(quarters[phase], to_core)
                arrived.append([from_chip(quarter, turn) for turn in range(1, chips)])
            by_x.append(from_rep(to_x, 1))
            by_y.append(from_rep(to_y, 2))
            came.append(swap(to_core))
        came.append((swap(by_x[-1]), swap(by_y[-1])))
        total = (chips - 1) * rows
        shares = []
        for kind in range(count):
            size = total if kind == 0 else total + total // 2
            next_size = total // 2 if kind == count - 1 else total + total // 2
            behind = next_size - total // 2
            before = 0 if kind == 0 else 2 * (total if kind == 1 else total + total // 2)
            mine = [
                shards,
                (jnp.concatenate(arrived[kind]), 0),
                (by_x[kind], 0),
                (by_y[kind], 0),
                (by_x[kind + 1], behind),
                (by_y[kind + 1], behind),
            ]
            last = came[kind + 2]
            siblings = [
                other_shards,
                (came[kind], before),
                (came[kind + 1], 0),
                (came[kind + 1], size),
                (last[0], behind) if kind == count - 1 else (last, behind),
                (last[1], behind) if kind == count - 1 else (last, next_size + behind),
            ]
            shares.append((mine, siblings))
        return shares, others

    def of_rep(values):
        return lax.dynamic_index_in_dim(values, my_rep, 0, keepdims=False)

    def in_quarters(matrix):
        return matrix.reshape(rows, shards, reps, sub).transpose(2, 0, 1, 3).reshape(
            reps, rows, shards * sub
        )

    def in_shard(pieces):
        cut = jnp.stack(pieces).reshape(reps, rows, shards, sub)
        return cut.transpose(1, 2, 0, 3).reshape(rows, hidden_width)

    def prepare(first):
        matrices = [self_weights, cross_weights, fc_in, fc_out]
        moments = [self_moment, cross_moment, fc_in_moment, fc_out_moment]
        if sub % 128 == 0:
            return prepared(place_now, matrices, moments, shards, sub, [first])
        whole = jnp.stack(
            [
                self_weights.astype(jnp.bfloat16),
                cross_weights.astype(jnp.bfloat16),
                in_quarters(fc_in.astype(jnp.bfloat16)),
                fc_out.reshape(reps, sub, width).astype(jnp.bfloat16),
            ]
        )
        wide_old = [of_rep(in_quarters(fc_in_moment)), of_rep(moments[3].reshape(reps, sub, width))]
        square_old = [of_rep(self_moment), of_rep(cross_moment)]
        quarters = [of_rep(whole[kind]) for kind in range(1, 4)]
        return whole, quarters, jnp.stack(wide_old), jnp.stack(square_old)

    shares, (wide_moments, square_moments) = gather_kinds(
        of_rep(self_weights).astype(jnp.bfloat16), prepare
    )
    self_full = placed_blocks(place_now, shares[0], 0, chips, [])
    cross_full = placed_blocks(place_now, shares[1], 1, chips, [])

    def first_sums(kinds, others, *waited):
        received = [swap(other) for other in others]
        to_x, to_y, kept, later = weight_rows(place_now, kinds, received, waited)
        return kept, later, from_rep(to_x, 1), from_rep(to_y, 2)

    def second_sums(stage, *waited):
        kept, later, by_x, by_y = stage
        to_y, to_x = later_sums(later, by_x, by_y, waited)
        return (kept, by_x, by_y, from_rep(to_x, 1), from_rep(to_y, 2)), to_x

    def third_sums(stage, *waited):
        blocks = sorted_blocks(place_now, *stage, chips, waited)
        arrived = [from_chip(blocks[chips - turn], turn) for turn in range(1, chips)]
        return blocks[0], arrived

    def share_pair(pair, *waited):
        by_x, by_y = from_rep(pair, 1), from_rep(pair, 2)
        across = jnp.stack([from_rep(by_y[0], 1), from_rep(by_x[1], 2)])
        return [pair, by_x, by_y, across]

    def to_replicas(steps):
        return by_rep([step[0] for step in steps]), by_rep([step[1] for step in steps])

    source = tokens[0].astype(jnp.float32)
    encoded = states[0]
    gain_rows = norm_params[0]
    bias_rows = norm_params[1]
    first, first_unit, first_inv = normalize_parts(source, gain_rows[0], bias_rows[0])
    first_low = first.astype(jnp.bfloat16)
    query_rows = matmul(first_low, self_full[0]).astype(jnp.bfloat16)
    incoming_keys = matmul(first_low, self_full[1]).astype(jnp.bfloat16)
    incoming_values = matmul(first_low, self_full[2]).astype(jnp.bfloat16)
    attended_values = attend_forward(query_rows, incoming_keys, incoming_values, dec_len, True)
    after_self = source + matmul(attended_values, self_full[3])
    second, second_unit, second_inv = normalize_parts(after_self, gain_rows[1], bias_rows[1])
    second_low = second.astype(jnp.bfloat16)
    cross_query = matmul(second_low, cross_full[0]).astype(jnp.bfloat16)
    cross_keys = matmul(encoded, cross_full[1]).astype(jnp.bfloat16)
    cross_values = matmul(encoded, cross_full[2]).astype(jnp.bfloat16)
    cross_mixed = attend_forward(cross_query, cross_keys, cross_values, enc_len, False)
    after_cross = after_self + matmul(cross_mixed, cross_full[3])
    third, third_unit, third_inv = normalize_parts(after_cross, gain_rows[2], bias_rows[2])
    third_low = third.astype(jnp.bfloat16)
    grad_out = cotangent[0].astype(jnp.float32)
    grad_branch = cotangent[0]
    block_out, grad_third, hidden, grad_pre = feed_forward(
        place_now, shares[2], shares[3], chips, third_low, after_cross, grad_branch
    )
    wide_kinds = [
        ([third_low] * reps, grad_pre, rows, False),
        (hidden, [grad_branch] * reps, sub, False),
    ]
    wide_other = weight_rows(place_now, wide_kinds)
    wide_stage = first_sums(wide_kinds, wide_other)
    grad_norm, third_gain, third_bias = normalize_back(
        grad_third, third_unit, third_inv, gain_rows[2]
    )
    grad_cross = grad_out + grad_norm
    cross_branch = grad_cross.astype(jnp.bfloat16)
    grad_mixed = matmul_right_t(cross_branch, cross_full[3]).astype(jnp.bfloat16)
    grad_cq, grad_ck, grad_cv = attend_backward(
        cross_query, cross_keys, cross_values, enc_len, False, grad_mixed, wide_stage[0]
    )
    cross_kind = (
        [second_low, encoded, encoded, cross_mixed],
        [grad_cq, grad_ck, grad_cv, cross_branch],
        rows,
        True,
    )
    cross_other = weight_rows(place_now, [cross_kind])[0]
    grad_second = matmul_right_t(grad_cq, cross_full[0])
    grad_norm, second_gain, second_bias = normalize_back(
        grad_second, second_unit, second_inv, gain_rows[1]
    )
    grad_self = grad_cross + grad_norm
    self_branch = grad_self.astype(jnp.bfloat16)
    grad_mixed = matmul_right_t(self_branch, self_full[3]).astype(jnp.bfloat16)
    wide_stage, wide_token = second_sums(wide_stage, grad_mixed)
    cross_stage = first_sums([cross_kind], [cross_other], wide_token)
    grad_sq, grad_sk, grad_sv = attend_backward(
        query_rows, incoming_keys, incoming_values, dec_len, True, grad_mixed, cross_stage[0]
    )
    self_kind = (
        [first_low, first_low, first_low, attended_values],
        [grad_sq, grad_sk, grad_sv, self_branch],
        rows,
        True,
    )
    self_other = weight_rows(place_now, [self_kind])[0]
    wide_stage = third_sums(wide_stage, self_other)
    cross_stage, cross_token = second_sums(cross_stage, wide_stage[0])
    self_stage = first_sums([self_kind], [self_other], cross_token)
    grad_sq = held_until(grad_sq, self_stage[0])
    grad_states = matmul_right_t(grad_ck, cross_full[1]) + matmul_right_t(grad_cv, cross_full[2])
    grad_first = (
        matmul_right_t(grad_sq, self_full[0])
        + matmul_right_t(grad_sk, self_full[1])
        + matmul_right_t(grad_sv, self_full[2])
    )
    grad_norm, first_gain, first_bias = normalize_back(
        grad_first, first_unit, first_inv, gain_rows[0]
    )
    grad_tokens = grad_self + grad_norm
    def owned(grads_fresh):
        mine, *sent = grads_fresh[1:]
        arrived = [from_chip(sent[turn - 1], turn) for turn in range(1, chips)]
        mine = jnp.concatenate([mine, *arrived])
        return mine, swap(mine)

    def to_both(result):
        other = from_chip(result[1], chips // 2)
        return jnp.stack(
            [jnp.where(is_lower, result[0], other), jnp.where(is_lower, other, result[0])]
        )

    self_stage, self_token = second_sums(self_stage)
    wide_fresh = fresh_blocks(place_now, *wide_stage, wide_moments)
    wide_grads = wide_fresh[0]
    wide_own = owned(wide_fresh)
    cross_stage = third_sums(cross_stage, wide_grads)
    self_stage = third_sums(self_stage)
    to_x, to_y, kept, later = gram_parts(place_now, *wide_own, reps, self_token)
    gram_stage, gram_token = second_sums((kept, later, from_rep(to_x, 1), from_rep(to_y, 2)))
    kept, by_x, by_y, last_x, last_y = gram_stage
    quarter = jnp.concatenate(
        [add_low(kept[0, 0], by_x[0, 0], last_y[0]), add_low(kept[0, 1], by_y[0, 0], last_x[0])]
    )
    quarter_x, quarter_y = from_rep(quarter, 1), from_rep(quarter, 2)
    part = quarter.shape[0] // 2
    quarters = [
        quarter,
        quarter_x,
        quarter_y,
        from_rep(quarter_y[:part], 1),
        from_rep(quarter_x[part:], 2),
    ]
    square_fresh = fresh_blocks(
        place_now,
        jnp.concatenate([self_stage[0], cross_stage[0]]),
        [jnp.concatenate(pair) for pair in zip(self_stage[1], cross_stage[1])],
        square_moments,
    )
    square_grads = square_fresh[0]
    square_own = owned(square_fresh)
    wide_grads_shared = share_pair(wide_grads)
    square_grads_shared = share_pair(square_grads)
    wide_rows = gram_schulz(
        place_now, quarters, *wide_own, rows, wide_grads_shared[1], self_stage[0]
    )
    wide_orth_shared = share_pair(to_both(wide_rows))
    square_rows = square_schulz(
        *square_own, rows, wide_rows, square_grads_shared[1], wide_grads_shared[3]
    )
    square_orth = held_until(
        to_both(square_rows), wide_orth_shared[3], square_grads_shared[3]
    )
    square_orth_shared = share_pair(square_orth)
    norm_local = jnp.stack(
        [
            jnp.stack([first_gain, second_gain, third_gain]),
            jnp.stack([first_bias, second_bias, third_bias]),
        ]
    )
    norm_local = held_until(norm_local, quarters[-1])
    norm_total = norm_local + swap(norm_local)
    norm_total = norm_total + from_rep(norm_total, 1)
    norm_total = norm_total + from_rep(norm_total, 2)
    norm_total = sum([from_chip(norm_total, turn) for turn in range(1, chips)], norm_total)
    width_part = norm_moment.shape[2]
    norm_grad = lax.dynamic_slice_in_dim(norm_total, my_place * width_part, width_part, 2)

    in_shared, out_shared = to_replicas(wide_grads_shared)
    self_shared, cross_shared = to_replicas(square_grads_shared)
    in_orth_shared, out_orth_shared = to_replicas(wide_orth_shared)
    self_orth_shared, cross_orth_shared = to_replicas(square_orth_shared)

    def stacked(pieces):
        return jnp.stack(pieces).astype(jnp.float32)

    def lengthwise(pieces):
        return jnp.concatenate(pieces).astype(jnp.float32)

    self_grad = stacked(self_shared)
    cross_grad = stacked(cross_shared)
    fc_in_grad = in_shard(in_shared).astype(jnp.float32)
    fc_out_grad = lengthwise(out_shared)
    self_orth = stacked(self_orth_shared)
    cross_orth = stacked(cross_orth_shared)
    in_orth = in_shard(in_orth_shared).astype(jnp.float32)
    out_orth = lengthwise(out_orth_shared)

    self_fresh = MOMENTUM_DECAY * self_moment + self_grad
    cross_fresh = MOMENTUM_DECAY * cross_moment + cross_grad
    in_fresh = MOMENTUM_DECAY * fc_in_moment + fc_in_grad
    out_fresh = MOMENTUM_DECAY * fc_out_moment + fc_out_grad
    norm_fresh = MOMENTUM_DECAY * norm_moment + norm_grad
    self_new = self_weights - MATRIX_RATE * stretch((width, width)) * self_orth
    cross_new = cross_weights - MATRIX_RATE * stretch((width, width)) * cross_orth
    in_new = fc_in - MATRIX_RATE * stretch((width, hidden_width)) * in_orth
    out_new = fc_out - MATRIX_RATE * stretch((hidden_width, width)) * out_orth
    own_params = lax.dynamic_slice_in_dim(norm_params, my_place * width_part, width_part, 2)
    total_tokens = reps * shards * tokens.shape[0] * tokens.shape[1]
    norm_new = own_params - VECTOR_RATE * norm_fresh / math.sqrt(total_tokens)
    return (
        block_out[None].astype(jnp.bfloat16),
        grad_tokens[None].astype(jnp.bfloat16),
        grad_states[None].astype(jnp.bfloat16),
        self_grad,
        cross_grad,
        fc_in_grad,
        fc_out_grad,
        norm_grad,
        self_fresh,
        cross_fresh,
        in_fresh,
        out_fresh,
        norm_fresh,
        self_new,
        cross_new,
        in_new,
        out_new,
        norm_new,
        self_new.astype(jnp.bfloat16),
        cross_new.astype(jnp.bfloat16),
        in_new.astype(jnp.bfloat16),
        out_new.astype(jnp.bfloat16),
    )


def solution(mesh):
    placed = (
        P(("rep", "shard"), None, None),
        P(("rep", "shard"), None, None),
        P(("rep", "shard"), None, None),
        P(("rep", "shard")),
        P(("rep", "shard")),
        P(None, "shard", None),
        P(None, "shard", None),
        P("shard", None),
        P("shard", None),
        P(),
        P(None, "shard", None),
        P(None, "shard", None),
        P("shard", None),
        P("shard", None),
        P(None, None, "shard"),
    )
    return jax.shard_map(
        on_device,
        mesh=mesh,
        in_specs=placed,
        out_specs=(
            P(("rep", "shard"), None, None),
            P(("rep", "shard"), None, None),
            P(("rep", "shard"), None, None),
            P(None, "shard", None),
            P(None, "shard", None),
            P("shard", None),
            P("shard", None),
            P(None, None, "shard"),
            P(None, "shard", None),
            P(None, "shard", None),
            P("shard", None),
            P("shard", None),
            P(None, None, "shard"),
            P(None, "shard", None),
            P(None, "shard", None),
            P("shard", None),
            P("shard", None),
            P(None, None, "shard"),
            P(None, "shard", None),
            P(None, "shard", None),
            P("shard", None),
            P("shard", None),
        ),
        check_vma=False,
    )
```

time: 1560 us -> 765 us (0.49)
  waiting for transfers between devices: 1120 us -> 267 us
  Pallas kernels: 0 us -> 250 us
  matrix products: 264 us -> 33.8 us
  starting transfers between devices: 1.53 us -> 107 us
  other arithmetic: 84.7 us -> 47.9 us
    reduce_scatter x8 -> x0, waiting for transfers between devices: 561 us -> none  [the longest x1 90.3 us: on_device(): lax.psum_scatter(cross_local.astype(jnp.bfloat16), 'shard', scatter_dimen...]
    all_gather x8 -> x0, waiting for transfers between devices: 454 us -> none  [the longest x1 82.9 us: on_device(): lax.all_gather(out_fresh.astype(jnp.bfloat16), 'shard', axis=0, tiled=True)]
    ppermute x0 -> x95, waiting for transfers between devices: none -> 267 us  [the longest x32 169 us: from_chip(): return lax.ppermute(values, 'shard', pairs)]
    pallas_call x0 -> x37, Pallas kernels: none -> 250 us  [the longest x4 47.4 us: attention_call(): pl.pallas_call(kernel, out_shape=tuple(out_shapes), in_specs=[pl.BlockSpe...]
    psum x1 -> x0, waiting for transfers between devices: 107 us -> none  [on_device(): lax.psum(reduced[3].astype(jnp.bfloat16), 'rep').astype(jnp.float32)]
    ppermute x0 -> x95, starting transfers between devices: none -> 107 us  [the longest x32 53.3 us: from_chip(): return lax.ppermute(values, 'shard', pairs)]
    dot_general x16 -> x8, matrix products: 121 us -> 17.9 us  [matmul(): return jnp.dot(left, right, preferred_element_type=jnp.float32)]
    dot_general x16 -> x8, matrix products: 95.5 us -> 15.8 us  [matmul_right_t(): lax.dot_general(left, right, (((1,), (1,)), ((), ())), preferred_element_...]
  transfers between devices with their start and end apart: 18 -> 95, of which waited for: 16 -> 45; matrix products, arithmetic and copies ran while one was open for 24% -> 13% of each run, Pallas kernels for 0% -> 22%
where the time goes in v1:
time: 765 us; the launch traced here: 761 us
  waiting for transfers between devices  267 us (35%)
  Pallas kernels  250 us (33%)
  starting transfers between devices  107 us (14%)
  local copies, waits for them, and re-layouts  51.4 us (7%)
  other arithmetic  47.9 us (6%)
  matrix products  33.8 us (4%)
    ppermute x32, waiting for transfers between devices, from_chip(): return lax.ppermute(values, 'shard', pairs)  169 us
    ppermute x48, waiting for transfers between devices, from_rep(): lax.ppermute(values, 'rep', [(index ^ step, index) for index in range(rep...  87.6 us
    ppermute x32, starting transfers between devices, from_chip(): return lax.ppermute(values, 'shard', pairs)  53.3 us
    ppermute x48, starting transfers between devices, from_rep(): lax.ppermute(values, 'rep', [(index ^ step, index) for index in range(rep...  51.1 us
    pallas_call x4, Pallas kernels, attention_call(): pl.pallas_call(kernel, out_shape=tuple(out_shapes), in_specs=[pl.BlockSpe...  47.4 us
    pallas_call x6, Pallas kernels, weight_rows(): pl.pallas_call(kernel, out_shape=tuple(out_shapes), in_specs=[pl.BlockSpe...  43.4 us
    unnamed x273, local copies, waits for them, and re-layouts  33.7 us
    pallas_call x1, Pallas kernels, gram_schulz(): pl.pallas_call(kernel, out_shape=low(2, rows, size), in_specs=[pl.BlockSp...  33.6 us
  transfers between devices with their start and end apart: 95, of which 45 were waited for; matrix products, arithmetic and copies ran while one was open for 13% of the time, Pallas kernels for 22%

profile of v1, /device:TPU:0, one launch (start us, length us, event | category | flops | bytes accessed | tf_op | source)
XLA Modules:
  0.0 760.7 jit_solution(17229854912062891356)
XLA Ops:
  13.1 7.9 %shard_map.318 = (bf16[4,4,128,1024]{3,2,1,0:T(8,128)(2,1)}, bf16[128,1024]{1,0:T(8,128)(2,1)}, bf16[128,1024]{1,0:T(8,128)(2,1)}, bf16[128,1024]{1,0:T(8,128)(2...) custom-call(s32[4]{0:T(128)} %pad_add_fusion.place_ref, f32[4,128,1024]{2,1,0:T(8,128)} %refs_0_.1, ...), custom_call_target="tpu_custom_call" | custom-call | flops 1024 | bytes 1024 | tf_op jit(solution)/shard_map/pallas_call | solution.py:871
  26.1 15.9 %collective-permute-done.1.refs_1_ = bf16[128,1024]{1,0:T(8,128)(2,1)S(1)} collective-permute-done((bf16[128,1024]{1,0:T(8,128)(2,1)S(1)}, bf16[128,1024]{1,0:T(8,128)(2,1)S(1)}, u32[]{:S(2)}, u32[]{:S(2)}) %collective-permute-start.1) | collective-permute-done | bytes 262176 | tf_op jit(solution)/shard_map/ppermute | solution.py:924
  49.9 6.7 collective-permute-done.5.refs_0_
  59.4 13.6 %collective-permute-done.6.refs_1_ = bf16[128,1024]{1,0:T(8,128)(2,1)S(1)} collective-permute-done((bf16[128,1024]{1,0:T(8,128)(2,1)}, bf16[128,1024]{1,0:T(8,128)(2,1)S(1)}, u32[]{:S(2)}, u32[]{:S(2)}) %collective-permute-start.6) | collective-permute-done | bytes 262176 | tf_op jit(solution)/shard_map/ppermute | solution.py:924
  82.4 8.1 %collective-permute-done.13.refs_0_ = bf16[128,1024]{1,0:T(8,128)(2,1)S(1)} collective-permute-done((bf16[128,1024]{1,0:T(8,128)(2,1)}, bf16[128,1024]{1,0:T(8,128)(2,1)S(1)}, u32[]{:S(2)}, u32[]{:S(2)}) %collective-permute-start.13) | collective-permute-done | bytes 262176 | tf_op jit(solution)/shard_map/ppermute | solution.py:924
  90.9 15.0 %collective-permute-done.14.refs_1_ = bf16[128,1024]{1,0:T(8,128)(2,1)S(1)} collective-permute-done((bf16[128,1024]{1,0:T(8,128)(2,1)}, bf16[128,1024]{1,0:T(8,128)(2,1)S(1)}, u32[]{:S(2)}, u32[]{:S(2)}) %collective-permute-start.14) | collective-permute-done | bytes 262176 | tf_op jit(solution)/shard_map/ppermute | solution.py:924
  119.2 8.2 %collective-permute-done.19.refs_0_ = bf16[128,1024]{1,0:T(8,128)(2,1)S(1)} collective-permute-done((bf16[128,1024]{1,0:T(8,128)(2,1)}, bf16[128,1024]{1,0:T(8,128)(2,1)S(1)}, u32[]{:S(2)}, u32[]{:S(2)}) %collective-permute-start.19) | collective-permute-done | bytes 262176 | tf_op jit(solution)/shard_map/ppermute | solution.py:924
  129.4 13.3 %collective-permute-done.20.refs_1_ = bf16[128,1024]{1,0:T(8,128)(2,1)S(1)} collective-permute-done((bf16[128,1024]{1,0:T(8,128)(2,1)}, bf16[128,1024]{1,0:T(8,128)(2,1)S(1)}, u32[]{:S(2)}, u32[]{:S(2)}) %collective-permute-start.20) | collective-permute-done | bytes 262176 | tf_op jit(solution)/shard_map/ppermute | solution.py:924
  160.4 7.8 %shard_map.324 = (bf16[4,2,128,1024]{3,2,1,0:T(8,128)(2,1)}, bf16[4,2,128,1024]{3,2,1,0:T(8,128)(2,1)}, bf16[4,2,128,1024]{3,2,1,0:T(8,128)(2,1)}, bf16[4,2,128,1024]{3,2,1,0:T(8,128)(2,1)}) custom-call(s32[4]{0:T(128)} %pad_add_fusion.place_ref, bf16[4,4,128,1024]{3,2,1,0:T(8,128)(2,1)} %get-tuple-element.115.refs_3_.refs_0_.refs_12_, ...), custom_call_target="tpu_custom_call" | custom-call | flops 1024 | bytes 1024 | tf_op jit(solution)/shard_map/pallas_call | solution.py:740
  175.6 9.6 %shard_map.325.refs_1_ = bf16[256,1024]{1,0:T(8,128)(2,1)} custom-call(s32[1]{0:T(128)S(6)} %copy.80.count_ref, bf16[256,1024]{1,0:T(8,128)(2,1)} %convolution_convert_fusion.7.query_ref, bf16[256,1024]{1,0:T(8,128)(2,1)} %convolution_convert_fusion.6.key_ref, bf16[256,1024]{1,0:T(8,128)(2,1)} %convolution_convert_fusion.5.value_ref), custom_call_target="tpu_custom_call" | custom-call | flops 1024 | bytes 1024 | tf_op jit(solution)/shard_map/pallas_call | solution.py:86
  196.2 7.7 %shard_map.328 = (bf16[4,2,128,1024]{3,2,1,0:T(8,128)(2,1)}, bf16[4,2,128,1024]{3,2,1,0:T(8,128)(2,1)}, bf16[4,2,128,1024]{3,2,1,0:T(8,128)(2,1)}, bf16[4,2,128,1024]{3,2,1,0:T(8,128)(2,1)}) custom-call(s32[4]{0:T(128)} %pad_add_fusion.place_ref, bf16[4,4,128,1024]{3,2,1,0:T(8,128)(2,1)} %get-tuple-element.115.refs_3_.refs_0_.refs_12_, ...), custom_call_target="tpu_custom_call" | custom-call | flops 1024 | bytes 1024 | tf_op jit(solution)/shard_map/pallas_call | solution.py:740
  212.5 10.8 %shard_map.329.refs_2_ = bf16[256,1024]{1,0:T(8,128)(2,1)} custom-call(s32[1]{0:T(128)S(6)} %copy.81.count_ref, bf16[256,1024]{1,0:T(8,128)(2,1)} %convolution_convert_fusion.4.query_ref, bf16[384,1024]{1,0:T(8,128)(2,1)} %fusion.3.key_ref, bf16[384,1024]{1,0:T(8,128)(2,1)} %fusion.4.value_ref), custom_call_target="tpu_custom_call" | custom-call | flops 1024 | bytes 1024 | tf_op jit(solution)/shard_map/pallas_call | solution.py:86
  229.3 17.7 %shard_map.331 = (f32[256,1024]{1,0:T(8,128)}, f32[256,1024]{1,0:T(8,128)}, bf16[256,1024]{1,0:T(8,128)(2,1)}, bf16[256,1024]{1,0:T(8,128)(2,1)}, bf16[256,1024]...) custom-call(s32[4]{0:T(128)} %pad_add_fusion.place_ref, ...), custom_call_target="tpu_custom_call" | custom-call | flops 1024 | bytes 1024 | tf_op jit(solution)/shard_map/pallas_call | solution.py:810
  247.0 7.2 shard_map.332
  267.7 10.5 %shard_map.333 = (bf16[2,2,256,1024]{3,2,1,0:T(8,128)(2,1)}, bf16[2,2,256,1024]{3,2,1,0:T(8,128)(2,1)}, bf16[2,2,256,1024]{3,2,1,0:T(8,128)(2,1)}, bf16[2,2,256,1024]{3,2,1,0:T(8,128)(2,1)}) custom-call(s32[4]{0:T(128)} %pad_add_fusion.place_ref, bf16[256,1024]{1,0:T(8,128)(2,1)} %add_convert_fusion.1.third_ref.refs_0_, ...), custom_call_target="tpu_custom_call" | custom-call | flops 1024 | bytes 1024 | tf_op jit(solution)/shard_map/pallas_call | solution.py:502
  278.2 14.3 %shard_map.334 = (bf16[256,1024]{1,0:T(8,128)(2,1)}, bf16[384,1024]{1,0:T(8,128)(2,1)}, bf16[384,1024]{1,0:T(8,128)(2,1)}) custom-call(s32[1]{0:T(128)S(6)} %copy.81.count_ref, bf16[256,1024]{1,0:T(8,128)(2,1)} %convolution_convert_fusion.4.query_ref, bf16[384,1024]{1,0:T(8,128)(2,1)} %fusion.3.key_ref, bf16[384,1024]{1,0:T(8,128)(2,1)} %fusion.4.value_ref, ...), custom_call_target="tpu_custom_call" | custom-call | flops 1024 | bytes 1024 | tf_op jit(solution)/shard_map/pallas_call | solution.py:86
  306.3 40.5 %collective-permute-done.33.x_ref = bf16[2,2,256,1024]{3,2,1,0:T(8,128)(2,1)S(1)} collective-permute-done((bf16[2,2,256,1024]{3,2,1,0:T(8,128)(2,1)}, bf16[2,2,256,1024]{3,2,1,0:T(8,128)(2,1)S(1)}, u32[]{:S(2)}, u32[]{:S(2)}) %collective-permute-start.33) | collective-permute-done | bytes 2097184 | tf_op jit(solution)/shard_map/ppermute | solution.py:927
  356.3 7.5 shard_map.337
  363.9 12.8 %shard_map.338 = (bf16[256,1024]{1,0:T(8,128)(2,1)}, bf16[256,1024]{1,0:T(8,128)(2,1)}, bf16[256,1024]{1,0:T(8,128)(2,1)}) custom-call(s32[1]{0:T(128)S(6)} %copy.80.count_ref, bf16[256,1024]{1,0:T(8,128)(2,1)} %convolution_convert_fusion.7.query_ref, bf16[256,1024]{1,0:T(8,128)(2,1)} %convolution_convert_fusion.6.key_ref, ...), custom_call_target="tpu_custom_call" | custom-call | flops 1024 | bytes 1024 | tf_op jit(solution)/shard_map/pallas_call | solution.py:86
  399.9 7.0 collective-permute-done.46.refs_0_
  408.3 30.4 %collective-permute-done.47.refs_1_ = bf16[2,128,1024]{2,1,0:T(8,128)(2,1)S(1)} collective-permute-done((bf16[2,128,1024]{2,1,0:T(8,128)(2,1)}, bf16[2,128,1024]{2,1,0:T(8,128)(2,1)S(1)}, u32[]{:S(2)}, u32[]{:S(2)}) %collective-permute-start.47) | collective-permute-done | bytes 524320 | tf_op jit(solution)/shard_map/ppermute | solution.py:924
  455.9 7.1 collective-permute-done.64
  466.5 7.6 collective-permute-done.65
  493.4 7.3 collective-permute-done.62
  523.3 9.6 %collective-permute-done.40.x_ref = bf16[1,2,256,1024]{3,2,1,0:T(8,128)(2,1)S(1)} collective-permute-done((bf16[1,2,256,1024]{3,2,1,0:T(8,128)(2,1)}, bf16[1,2,256,1024]{3,2,1,0:T(8,128)(2,1)S(1)}, u32[]{:S(2)}, u32[]{:S(2)}) %collective-permute-start.40) | collective-permute-done | bytes 1048608 | tf_op jit(solution)/shard_map/ppermute | solution.py:927
  567.6 7.2 collective-permute-done.52
  587.6 8.9 %collective-permute-start.79 = (bf16[128,1024]{1,0:T(8,128)(2,1)}, bf16[128,1024]{1,0:T(8,128)(2,1)S(1)}, u32[]{:S(2)}, u32[]{:S(2)}) collective-permute-start(bf16[128,1024]{1,0:T(8,128)(2,1)} %get-tuple-element.205), channel_id=1, source_target_pairs={{2,0},{3,1},{4,2},{5,3},{6,4},{7,5},{0,6},{1,7},{10,8},{11,9},{12,... | collective-permute-start | bytes 786440 | tf_op jit(solution)/shard_map/ppermute | solution.py:924
  603.5 10.6 %collective-permute-start.81 = (bf16[128,1024]{1,0:T(8,128)(2,1)S(1)}, bf16[128,1024]{1,0:T(8,128)(2,1)S(1)}, u32[]{:S(2)}, u32[]{:S(2)}) collective-permute-start(bf16[128,1024]{1,0:T(8,128)(2,1)S(1)} %copy-done.125), channel_id=1, source_target_pairs={{6,0},{7,1},{0,2},{1,3},{2,4},{3,5},{4,6},{5,7},{14,8},{15,9},{8,1... | collective-permute-start | bytes 786440 | tf_op jit(solution)/shard_map/ppermute | solution.py:924
  621.4 9.6 %collective-permute-done.55 = bf16[2,128,1024]{2,1,0:T(8,128)(2,1)S(1)} collective-permute-done((bf16[2,128,1024]{2,1,0:T(8,128)(2,1)S(1)}, bf16[2,128,1024]{2,1,0:T(8,128)(2,1)S(1)}, u32[]{:S(2)}, u32[]{:S(2)}) %collective-permute-start.55) | collective-permute-done | bytes 524320 | tf_op jit(solution)/shard_map/ppermute | solution.py:927
  636.5 33.6 %shard_map.352.refs_0_ = bf16[2,128,1024]{2,1,0:T(8,128)(2,1)} custom-call(s32[4]{0:T(128)} %pad_add_fusion.place_ref, bf16[256,1024]{1,0:T(8,128)(2,1)} %copy-done.60, bf16[256,1024]{1,0:T(8,128)(2,1)} %copy-done.70, bf16[256,1024]{1,0:T(8,128)(2,1)} %copy-done.71, bf16[128,1024]{1,0:T(8,128)(2,1)} %copy-done.114, bf16[128,1024]{1,0:T(8,128)(2,1)} %copy-done.74, ...), custom_call_target="tpu_custom_call" | custom-call | flops 1024 | bytes 1024 | tf_op jit(solution)/shard_map/pallas_call | solution.py:380
  692.8 25.5 %shard_map.353 = bf16[2,128,1024]{2,1,0:T(8,128)(2,1)} custom-call(bf16[512,1024]{1,0:T(8,128)(2,1)} %copy-done.61, bf16[512,1024]{1,0:T(8,128)(2,1)} %copy-done.92, bf16[2,128,1024]{2,1,0:T(8,128)(2,1)} %shard_map.352.refs_0_, bf16[2,128,1024]{2,1,0:T(8,128)(2,1)} %copy-done.41, bf16[2,128,1024]{2,1,0:T(8,128)(2,1)} %pad_maximum_fusion.9.refs_2_), custom_call_target="tpu_custom_call" | custom-call | flops 1024 | bytes 1024 | tf_op jit(solution)/shard_map/pallas_call | solution.py:233
  721.8 8.9 %collective-permute-done.85 = bf16[128,1024]{1,0:T(8,128)(2,1)S(1)} collective-permute-done((bf16[128,1024]{1,0:T(8,128)(2,1)S(1)}, bf16[128,1024]{1,0:T(8,128)(2,1)S(1)}, u32[]{:S(2)}, u32[]{:S(2)}) %collective-permute-start.85) | collective-permute-done | bytes 262176 | tf_op jit(solution)/shard_map/ppermute | solution.py:924
  (571 shorter events, 348.7 us)
Async XLA Ops:
  21.1 51.9 %collective-permute-start.8 = (bf16[4,4,128,1024]{3,2,1,0:T(8,128)(2,1)}, bf16[4,4,128,1024]{3,2,1,0:T(8,128)(2,1)S(1)}, u32[]{:S(2)}, u32[]{:S(2)}) collective-permute-start(bf16[4,4,128,1024]{3,2,1,0:T(8,128)(2,1)} %get-tuple-element.115.refs_3_.refs_0_.refs_12_), channel_id=1, source_target_pairs={{0,1},{1,0},{2,3},{3,2},{4,5},{5,4},{6,7},{7,6},{8,9},{9,8},{10,11... | collective-permute-start | bytes 12582920 | tf_op jit(solution)/shard_map/ppermute | solution.py:916
  45.5 27.5 %collective-permute-start.3 = (bf16[384,1024]{1,0:T(8,128)(2,1)}, bf16[384,1024]{1,0:T(8,128)(2,1)S(1)}, u32[]{:S(2)}, u32[]{:S(2)}) collective-permute-start(bf16[384,1024]{1,0:T(8,128)(2,1)} %get-tuple-element.119), channel_id=1, source_target_pairs={{8,0},{0,8},{24,16},{16,24},{9,1},{1,9},{25,17},{17,25},{10,2},{2,... | collective-permute-start | bytes 2359304 | tf_op jit(solution)/shard_map/ppermute | solution.py:927
  80.3 28.8 %collective-permute-start.12 = (bf16[1152,1024]{1,0:T(8,128)(2,1)}, bf16[1152,1024]{1,0:T(8,128)(2,1)S(1)}, u32[]{:S(2)}, u32[]{:S(2)}) collective-permute-start(bf16[1152,1024]{1,0:T(8,128)(2,1)} %get-tuple-element.124.refs_1_), channel_id=1, source_target_pairs={{0,1},{1,0},{2,3},{3,2},{4,5},{5,4},{6,7},{7,6},{8,9},{9,8},{10,11... | collective-permute-start | bytes 7077896 | tf_op jit(solution)/shard_map/ppermute | solution.py:916
  80.3 28.6 %collective-permute-start.10 = (bf16[576,1024]{1,0:T(8,128)(2,1)}, bf16[576,1024]{1,0:T(8,128)(2,1)S(1)}, u32[]{:S(2)}, u32[]{:S(2)}) collective-permute-start(bf16[576,1024]{1,0:T(8,128)(2,1)} %get-tuple-element.123), channel_id=1, source_target_pairs={{16,0},{24,8},{0,16},{8,24},{17,1},{25,9},{1,17},{9,25},{18,2},{26... | collective-permute-start | bytes 3538952 | tf_op jit(solution)/shard_map/ppermute | solution.py:927
  80.8 28.3 %collective-permute-start.9 = (bf16[576,1024]{1,0:T(8,128)(2,1)}, bf16[576,1024]{1,0:T(8,128)(2,1)S(1)}, u32[]{:S(2)}, u32[]{:S(2)}) collective-permute-start(bf16[576,1024]{1,0:T(8,128)(2,1)} %get-tuple-element.122), channel_id=1, source_target_pairs={{8,0},{0,8},{24,16},{16,24},{9,1},{1,9},{25,17},{17,25},{10,2},{2,... | collective-permute-start | bytes 3538952 | tf_op jit(solution)/shard_map/ppermute | solution.py:927
  116.2 28.9 %collective-permute-start.16 = (bf16[1536,1024]{1,0:T(8,128)(2,1)}, bf16[1536,1024]{1,0:T(8,128)(2,1)S(1)}, u32[]{:S(2)}, u32[]{:S(2)}) collective-permute-start(bf16[1536,1024]{1,0:T(8,128)(2,1)} %get-tuple-element.125.refs_1_), channel_id=1, source_target_pairs={{0,1},{1,0},{2,3},{3,2},{4,5},{5,4},{6,7},{7,6},{8,9},{9,8},{10,11... | collective-permute-start | bytes 9437192 | tf_op jit(solution)/shard_map/ppermute | solution.py:916
  116.3 28.6 %collective-permute-start.17 = (bf16[576,1024]{1,0:T(8,128)(2,1)}, bf16[576,1024]{1,0:T(8,128)(2,1)S(1)}, u32[]{:S(2)}, u32[]{:S(2)}) collective-permute-start(bf16[576,1024]{1,0:T(8,128)(2,1)} %get-tuple-element.130), channel_id=1, source_target_pairs={{8,0},{0,8},{24,16},{16,24},{9,1},{1,9},{25,17},{17,25},{10,2},{2,... | collective-permute-start | bytes 3538952 | tf_op jit(solution)/shard_map/ppermute | solution.py:927
  116.8 28.3 %collective-permute-start.18 = (bf16[576,1024]{1,0:T(8,128)(2,1)}, bf16[576,1024]{1,0:T(8,128)(2,1)S(1)}, u32[]{:S(2)}, u32[]{:S(2)}) collective-permute-start(bf16[576,1024]{1,0:T(8,128)(2,1)} %get-tuple-element.131), channel_id=1, source_target_pairs={{16,0},{24,8},{0,16},{8,24},{17,1},{25,9},{1,17},{9,25},{18,2},{26... | collective-permute-start | bytes 3538952 | tf_op jit(solution)/shard_map/ppermute | solution.py:927
  152.5 35.6 %collective-permute-start.22 = (bf16[1536,1024]{1,0:T(8,128)(2,1)}, bf16[1536,1024]{1,0:T(8,128)(2,1)S(1)}, u32[]{:S(2)}, u32[]{:S(2)}) collective-permute-start(bf16[1536,1024]{1,0:T(8,128)(2,1)} %get-tuple-element.132), channel_id=1, source_target_pairs={{0,1},{1,0},{2,3},{3,2},{4,5},{5,4},{6,7},{7,6},{8,9},{9,8},{10,11... | collective-permute-start | bytes 9437192 | tf_op jit(solution)/shard_map/ppermute | solution.py:916
  156.4 31.6 %collective-permute-start.23 = (bf16[576,1024]{1,0:T(8,128)(2,1)}, bf16[576,1024]{1,0:T(8,128)(2,1)S(1)}, u32[]{:S(2)}, u32[]{:S(2)}) collective-permute-start(bf16[576,1024]{1,0:T(8,128)(2,1)} %get-tuple-element.137), channel_id=1, source_target_pairs={{8,0},{0,8},{24,16},{16,24},{9,1},{1,9},{25,17},{17,25},{10,2},{2,... | collective-permute-start | bytes 3538952 | tf_op jit(solution)/shard_map/ppermute | solution.py:927
  157.7 30.3 %collective-permute-start.24 = (bf16[576,1024]{1,0:T(8,128)(2,1)}, bf16[576,1024]{1,0:T(8,128)(2,1)S(1)}, u32[]{:S(2)}, u32[]{:S(2)}) collective-permute-start(bf16[576,1024]{1,0:T(8,128)(2,1)} %get-tuple-element.138), channel_id=1, source_target_pairs={{16,0},{24,8},{0,16},{8,24},{17,1},{25,9},{1,17},{9,25},{18,2},{26... | collective-permute-start | bytes 3538952 | tf_op jit(solution)/shard_map/ppermute | solution.py:927
  194.4 33.4 %collective-permute-start.25 = (bf16[1152,1024]{1,0:T(8,128)(2,1)}, bf16[1152,1024]{1,0:T(8,128)(2,1)S(1)}, u32[]{:S(2)}, u32[]{:S(2)}) collective-permute-start(bf16[1152,1024]{1,0:T(8,128)(2,1)} %get-tuple-element.139), channel_id=1, source_target_pairs={{0,1},{1,0},{2,3},{3,2},{4,5},{5,4},{6,7},{7,6},{8,9},{9,8},{10,11... | collective-permute-start | bytes 7077896 | tf_op jit(solution)/shard_map/ppermute | solution.py:916
  194.8 30.6 %collective-permute-start.26 = (bf16[192,1024]{1,0:T(8,128)(2,1)}, bf16[192,1024]{1,0:T(8,128)(2,1)S(1)}, u32[]{:S(2)}, u32[]{:S(2)}) collective-permute-start(bf16[192,1024]{1,0:T(8,128)(2,1)} %get-tuple-element.140), channel_id=1, source_target_pairs={{8,0},{0,8},{24,16},{16,24},{9,1},{1,9},{25,17},{17,25},{10,2},{2,... | collective-permute-start | bytes 1179656 | tf_op jit(solution)/shard_map/ppermute | solution.py:927
  298.6 57.7 %collective-permute-start.32 = (bf16[4,512,1024]{2,1,0:T(8,128)(2,1)}, bf16[4,512,1024]{2,1,0:T(8,128)(2,1)}, u32[]{:S(2)}, u32[]{:S(2)}) collective-permute-start(bf16[4,512,1024]{2,1,0:T(8,128)(2,1)} %shard_map.335), channel_id=1, source_target_pairs={{0,1},{1,0},{2,3},{3,2},{4,5},{5,4},{6,7},{7,6},{8,9},{9,8},{10,11... | collective-permute-start | bytes 12582920 | tf_op jit(solution)/shard_map/ppermute | solution.py:916
  298.8 48.1 %collective-permute-start.33 = (bf16[2,2,256,1024]{3,2,1,0:T(8,128)(2,1)}, bf16[2,2,256,1024]{3,2,1,0:T(8,128)(2,1)S(1)}, u32[]{:S(2)}, u32[]{:S(2)}) collective-permute-start(bf16[2,2,256,1024]{3,2,1,0:T(8,128)(2,1)} %get-tuple-element.159), channel_id=1, source_target_pairs={{8,0},{0,8},{24,16},{16,24},{9,1},{1,9},{25,17},{17,25},{10,2},{2,... | collective-permute-start | bytes 6291464 | tf_op jit(solution)/shard_map/ppermute | solution.py:927
  299.5 47.8 %collective-permute-start.34 = (bf16[2,2,256,1024]{3,2,1,0:T(8,128)(2,1)}, bf16[2,2,256,1024]{3,2,1,0:T(8,128)(2,1)S(1)}, u32[]{:S(2)}, u32[]{:S(2)}) collective-permute-start(bf16[2,2,256,1024]{3,2,1,0:T(8,128)(2,1)} %get-tuple-element.160), channel_id=1, source_target_pairs={{16,0},{24,8},{0,16},{8,24},{17,1},{25,9},{1,17},{9,25},{18,2},{26... | collective-permute-start | bytes 6291464 | tf_op jit(solution)/shard_map/ppermute | solution.py:927
  353.4 29.4 %collective-permute-start.38 = (bf16[2,256,1024]{2,1,0:T(8,128)(2,1)}, bf16[2,256,1024]{2,1,0:T(8,128)(2,1)S(1)}, u32[]{:S(2)}, u32[]{:S(2)}) collective-permute-start(bf16[2,256,1024]{2,1,0:T(8,128)(2,1)} %get-tuple-element.161.refs_8_), channel_id=1, source_target_pairs={{8,0},{0,8},{24,16},{16,24},{9,1},{1,9},{25,17},{17,25},{10,2},{2,... | collective-permute-start | bytes 3145736 | tf_op jit(solution)/shard_map/ppermute | solution.py:927
  354.5 28.4 %collective-permute-start.39 = (bf16[2,256,1024]{2,1,0:T(8,128)(2,1)}, bf16[2,256,1024]{2,1,0:T(8,128)(2,1)S(1)}, u32[]{:S(2)}, u32[]{:S(2)}) collective-permute-start(bf16[2,256,1024]{2,1,0:T(8,128)(2,1)} %get-tuple-element.169), channel_id=1, source_target_pairs={{16,0},{24,8},{0,16},{8,24},{17,1},{25,9},{1,17},{9,25},{18,2},{26... | collective-permute-start | bytes 3145736 | tf_op jit(solution)/shard_map/ppermute | solution.py:927
  382.0 119.8 %collective-permute-start.35 = (bf16[4,512,1024]{2,1,0:T(8,128)(2,1)}, bf16[4,512,1024]{2,1,0:T(8,128)(2,1)}, u32[]{:S(2)}, u32[]{:S(2)}) collective-permute-start(bf16[4,512,1024]{2,1,0:T(8,128)(2,1)} %shard_map.339.refs_0_), channel_id=1, source_target_pairs={{0,1},{1,0},{2,3},{3,2},{4,5},{5,4},{6,7},{7,6},{8,9},{9,8},{10,11... | collective-permute-start | bytes 12582920 | tf_op jit(solution)/shard_map/ppermute | solution.py:916
  391.1 47.6 %collective-permute-start.47 = (bf16[2,128,1024]{2,1,0:T(8,128)(2,1)}, bf16[2,128,1024]{2,1,0:T(8,128)(2,1)S(1)}, u32[]{:S(2)}, u32[]{:S(2)}) collective-permute-start(bf16[2,128,1024]{2,1,0:T(8,128)(2,1)} %get-tuple-element.181), channel_id=1, source_target_pairs={{4,0},{5,1},{6,2},{7,3},{0,4},{1,5},{2,6},{3,7},{12,8},{13,9},{14,... | collective-permute-start | bytes 1572872 | tf_op jit(solution)/shard_map/ppermute | solution.py:924
  392.2 46.5 %collective-permute-start.48 = (bf16[2,128,1024]{2,1,0:T(8,128)(2,1)}, bf16[2,128,1024]{2,1,0:T(8,128)(2,1)S(1)}, u32[]{:S(2)}, u32[]{:S(2)}) collective-permute-start(bf16[2,128,1024]{2,1,0:T(8,128)(2,1)} %get-tuple-element.182), channel_id=1, source_target_pairs={{6,0},{7,1},{0,2},{1,3},{2,4},{3,5},{4,6},{5,7},{14,8},{15,9},{8,1... | collective-permute-start | bytes 1572872 | tf_op jit(solution)/shard_map/ppermute | solution.py:924
  399.0 76.8 %collective-permute-start.36 = (bf16[1,2,256,1024]{3,2,1,0:T(8,128)(2,1)}, bf16[1,2,256,1024]{3,2,1,0:T(8,128)(2,1)S(1)}, u32[]{:S(2)}, u32[]{:S(2)}) collective-permute-start(bf16[1,2,256,1024]{3,2,1,0:T(8,128)(2,1)} %get-tuple-element.167), channel_id=1, source_target_pairs={{8,0},{0,8},{24,16},{16,24},{9,1},{1,9},{25,17},{17,25},{10,2},{2,... | collective-permute-start | bytes 3145736 | tf_op jit(solution)/shard_map/ppermute | solution.py:927
  407.0 68.9 %collective-permute-start.37 = (bf16[1,2,256,1024]{3,2,1,0:T(8,128)(2,1)}, bf16[1,2,256,1024]{3,2,1,0:T(8,128)(2,1)S(1)}, u32[]{:S(2)}, u32[]{:S(2)}) collective-permute-start(bf16[1,2,256,1024]{3,2,1,0:T(8,128)(2,1)} %get-tuple-element.168), channel_id=1, source_target_pairs={{16,0},{24,8},{0,16},{8,24},{17,1},{25,9},{1,17},{9,25},{18,2},{26... | collective-permute-start | bytes 3145736 | tf_op jit(solution)/shard_map/ppermute | solution.py:927
  475.8 64.0 %collective-permute-start.66 = (bf16[512,1024]{1,0:T(8,128)(2,1)}, bf16[512,1024]{1,0:T(8,128)(2,1)}, u32[]{:S(2)}, u32[]{:S(2)}) collective-permute-start(bf16[512,1024]{1,0:T(8,128)(2,1)} %constant_dynamic-update-slice_fusion.mine_ref), channel_id=1, source_target_pairs={{0,1},{1,0},{2,3},{3,2},{4,5},{5,4},{6,7},{7,6},{8,9},{9,8},{10,11... | collective-permute-start | bytes 3145736 | tf_op jit(solution)/shard_map/ppermute | solution.py:916
  480.1 35.4 %collective-permute-start.44 = (bf16[1,256,1024]{2,1,0:T(8,128)(2,1)}, bf16[1,256,1024]{2,1,0:T(8,128)(2,1)}, u32[]{:S(2)}, u32[]{:S(2)}) collective-permute-start(bf16[1,256,1024]{2,1,0:T(8,128)(2,1)} %get-tuple-element.171.refs_7_), channel_id=1, source_target_pairs={{8,0},{0,8},{24,16},{16,24},{9,1},{1,9},{25,17},{17,25},{10,2},{2,... | collective-permute-start | bytes 1572872 | tf_op jit(solution)/shard_map/ppermute | solution.py:927
  481.1 34.4 %collective-permute-start.45 = (bf16[1,256,1024]{2,1,0:T(8,128)(2,1)}, bf16[1,256,1024]{2,1,0:T(8,128)(2,1)}, u32[]{:S(2)}, u32[]{:S(2)}) collective-permute-start(bf16[1,256,1024]{2,1,0:T(8,128)(2,1)} %get-tuple-element.179), channel_id=1, source_target_pairs={{16,0},{24,8},{0,16},{8,24},{17,1},{25,9},{1,17},{9,25},{18,2},{26... | collective-permute-start | bytes 1572872 | tf_op jit(solution)/shard_map/ppermute | solution.py:927
  519.5 39.1 %collective-permute-start.54 = (bf16[1,128,1024]{2,1,0:T(8,128)(2,1)}, bf16[1,128,1024]{2,1,0:T(8,128)(2,1)S(1)}, u32[]{:S(2)}, u32[]{:S(2)}) collective-permute-start(bf16[1,128,1024]{2,1,0:T(8,128)(2,1)} %get-tuple-element.191), channel_id=1, source_target_pairs={{6,0},{7,1},{0,2},{1,3},{2,4},{3,5},{4,6},{5,7},{14,8},{15,9},{8,1... | collective-permute-start | bytes 786440 | tf_op jit(solution)/shard_map/ppermute | solution.py:924
  618.0 73.8 %collective-permute-start.82 = (bf16[512,1024]{1,0:T(8,128)(2,1)S(1)}, bf16[512,1024]{1,0:T(8,128)(2,1)S(1)}, u32[]{:S(2)}, u32[]{:S(2)}) collective-permute-start(bf16[512,1024]{1,0:T(8,128)(2,1)S(1)} %constant_dynamic-update-slice_fusion.4.mine_ref), channel_id=1, source_target_pairs={{0,1},{1,0},{2,3},{3,2},{4,5},{5,4},{6,7},{7,6},{8,9},{9,8},{10,11... | collective-permute-start | bytes 3145736 | tf_op jit(solution)/shard_map/ppermute | solution.py:916
  620.6 50.7 %collective-permute-start.58 = (bf16[128,1024]{1,0:T(8,128)(2,1)S(1)}, bf16[128,1024]{1,0:T(8,128)(2,1)S(1)}, u32[]{:S(2)}, u32[]{:S(2)}) collective-permute-start(bf16[128,1024]{1,0:T(8,128)(2,1)S(1)} %slice_bitcast_fusion.15), channel_id=1, source_target_pairs={{16,0},{24,8},{0,16},{8,24},{17,1},{25,9},{1,17},{9,25},{18,2},{26... | collective-permute-start | bytes 786440 | tf_op jit(solution)/shard_map/ppermute | solution.py:927
  631.1 44.0 %collective-permute-start.56 = (bf16[128,1024]{1,0:T(8,128)(2,1)S(1)}, bf16[128,1024]{1,0:T(8,128)(2,1)S(1)}, u32[]{:S(2)}, u32[]{:S(2)}) collective-permute-start(bf16[128,1024]{1,0:T(8,128)(2,1)S(1)} %slice_bitcast_fusion.16), channel_id=1, source_target_pairs={{8,0},{0,8},{24,16},{16,24},{9,1},{1,9},{25,17},{17,25},{10,2},{2,... | collective-permute-start | bytes 786440 | tf_op jit(solution)/shard_map/ppermute | solution.py:927
  687.0 32.3 %collective-permute-start.89 = (bf16[2,128,1024]{2,1,0:T(8,128)(2,1)S(1)}, bf16[2,128,1024]{2,1,0:T(8,128)(2,1)S(1)}, u32[]{:S(2)}, u32[]{:S(2)}) collective-permute-start(bf16[2,128,1024]{2,1,0:T(8,128)(2,1)S(1)} %pad_maximum_fusion.11), channel_id=1, source_target_pairs={{8,0},{0,8},{24,16},{16,24},{9,1},{1,9},{25,17},{17,25},{10,2},{2,... | collective-permute-start | bytes 1572872 | tf_op jit(solution)/shard_map/ppermute | solution.py:927
  688.9 31.9 %collective-permute-start.87 = (bf16[2,128,1024]{2,1,0:T(8,128)(2,1)S(1)}, bf16[2,128,1024]{2,1,0:T(8,128)(2,1)S(1)}, u32[]{:S(2)}, u32[]{:S(2)}) collective-permute-start(bf16[2,128,1024]{2,1,0:T(8,128)(2,1)S(1)} %pad_maximum_fusion.11), channel_id=1, source_target_pairs={{16,0},{24,8},{0,16},{8,24},{17,1},{25,9},{1,17},{9,25},{18,2},{26... | collective-permute-start | bytes 1572872 | tf_op jit(solution)/shard_map/ppermute | solution.py:927
  (191 other events, 1956.4 us)

commit v2 on v1

--- a/solution.py
+++ b/solution.py
@@ -882,6 +882,48 @@
     return whole, parts, wide_old, square_old
 
 
+def branch_back(grad_query, weights, stream, gain, grad_stream, next_weights, *waited):
+    rows, width = stream.shape
+
+    def kernel(query_ref, weights_ref, stream_ref, gain_ref, grad_ref, next_ref, *refs):
+        total_ref, branch_ref, mixed_ref, gain_grad, bias_grad = refs[len(waited) :]
+        grad_out = matmul_right_t(query_ref[...], weights_ref[...])
+        values = stream_ref[...]
+        centered = values - jnp.mean(values, axis=-1, keepdims=True)
+        inverse = lax.rsqrt(jnp.mean(centered * centered, axis=-1, keepdims=True) + NORM_EPSILON)
+        unit_part = centered * inverse
+        grad_unit = grad_out * gain_ref[...]
+        grad_in = inverse * (
+            grad_unit
+            - jnp.mean(grad_unit, axis=-1, keepdims=True)
+            - unit_part * jnp.mean(grad_unit * unit_part, axis=-1, keepdims=True)
+        )
+        total = grad_ref[...] + grad_in
+        branch = total.astype(jnp.bfloat16)
+        total_ref[...] = total
+        branch_ref[...] = branch
+        mixed_ref[...] = matmul_right_t(branch, next_ref[...]).astype(jnp.bfloat16)
+        gain_grad[...] = jnp.sum(grad_out * unit_part, axis=0, keepdims=True)
+        bias_grad[...] = jnp.sum(grad_out, axis=0, keepdims=True)
+
+    vmem = pl.BlockSpec(memory_space=pltpu.VMEM)
+    line = jax.ShapeDtypeStruct((1, width), jnp.float32)
+    return pl.pallas_call(
+        kernel,
+        out_shape=(
+            jax.ShapeDtypeStruct((rows, width), jnp.float32),
+            low(rows, width),
+            low(rows, width),
+            line,
+            line,
+        ),
+        in_specs=[vmem] * 6 + [pl.BlockSpec(memory_space=pl.ANY)] * len(waited),
+        out_specs=(vmem,) * 5,
+        compiler_params=pltpu.CompilerParams(vmem_limit_bytes=56 * 2**20),
+        cost_estimate=SMALL,
+    )(grad_query, weights, stream, gain, grad_stream, next_weights, *waited)
+
+
 def on_device(
     tokens,
     states,
@@ -936,53 +978,50 @@
     is_lower = my_chip < chips // 2
     place_now = jnp.stack([my_rep, my_chip, my_core, is_lower]).astype(jnp.int32)
 
-    def gather_kinds(quarter, prepare):
-        arrived, by_x, by_y, came = [], [], [], []
-        arrived.append([from_chip(quarter, turn) for turn in range(1, chips)])
-        shards, quarters, *others = prepare(arrived[0][0])
-        count = shards.shape[0]
-        other_shards = swap(shards)
-        for phase in range(count + 1):
-            waited = [came[-1]] if phase > 1 else [shards, *quarters] if phase == 0 else []
-            to_x, to_y, to_core = phase_blocks(
-                arrived[phase] if phase < count else None,
-                by_x[-1] if phase > 0 else None,
-                by_y[-1] if phase > 0 else None,
-                [*waited, other_shards] if phase == 1 else waited,
-            )
-            if phase + 1 < count:
-                quarter = held_until(quarters[phase], to_core)
-                arrived.append([from_chip(quarter, turn) for turn in range(1, chips)])
-            by_x.append(from_rep(to_x, 1))
-            by_y.append(from_rep(to_y, 2))
-            came.append(swap(to_core))
-        came.append((swap(by_x[-1]), swap(by_y[-1])))
-        total = (chips - 1) * rows
-        shares = []
-        for kind in range(count):
-            size = total if kind == 0 else total + total // 2
-            next_size = total // 2 if kind == count - 1 else total + total // 2
-            behind = next_size - total // 2
-            before = 0 if kind == 0 else 2 * (total if kind == 1 else total + total // 2)
-            mine = [
-                shards,
-                (jnp.concatenate(arrived[kind]), 0),
-                (by_x[kind], 0),
-                (by_y[kind], 0),
-                (by_x[kind + 1], behind),
-                (by_y[kind + 1], behind),
-            ]
-            last = came[kind + 2]
-            siblings = [
-                other_shards,
-                (came[kind], before),
-                (came[kind + 1], 0),
-                (came[kind + 1], size),
-                (last[0], behind) if kind == count - 1 else (last, behind),
-                (last[1], behind) if kind == count - 1 else (last, next_size + behind),
-            ]
-            shares.append((mine, siblings))
-        return shares, others
+    def first_blocks(quarter):
+        return [from_chip(quarter, turn) for turn in range(1, chips)]
+
+    total_rows = (chips - 1) * rows
+
+    def run_phase(state, phase, waited):
+        to_x, to_y, to_core = phase_blocks(
+            state["arrived"] if phase < 4 else None,
+            state["by_x"][-1] if phase > 0 else None,
+            state["by_y"][-1] if phase > 0 else None,
+            [*waited, *state["came"][-1:]],
+        )
+        if phase < 3:
+            quarter = held_until(state["quarters"][phase], to_core)
+            state["arrived"] = first_blocks(quarter)
+        state["sent"].append(to_x)
+        state["by_x"].append(from_rep(to_x, 1))
+        state["by_y"].append(from_rep(to_y, 2))
+        state["came"].append(swap(to_core))
+
+    def shares_of(state, kind, last_pair=None):
+        by_x, by_y, came = state["by_x"], state["by_y"], state["came"]
+        size = total_rows if kind == 0 else total_rows + total_rows // 2
+        next_size = total_rows // 2 if kind == 3 else total_rows + total_rows // 2
+        behind = next_size - total_rows // 2
+        before = [0, 2 * total_rows, 3 * total_rows, 3 * total_rows][kind]
+        mine = [
+            state["shards"],
+            (state["sent"][kind], 0),
+            (by_x[kind], 0),
+            (by_y[kind], 0),
+            (by_x[kind + 1], behind),
+            (by_y[kind + 1], behind),
+        ]
+        last = last_pair or (came[kind + 2], came[kind + 2])
+        siblings = [
+            state["other_shards"],
+            (came[kind], before),
+            (came[kind + 1], 0),
+            (came[kind + 1], size),
+            (last[0], behind),
+            (last[1], behind if last_pair else next_size + behind),
+        ]
+        return mine, siblings
 
     def of_rep(values):
         return lax.dynamic_index_in_dim(values, my_rep, 0, keepdims=False)
@@ -996,11 +1035,11 @@
         cut = jnp.stack(pieces).reshape(reps, rows, shards, sub)
         return cut.transpose(1, 2, 0, 3).reshape(rows, hidden_width)
 
-    def prepare(first):
+    def prepare():
         matrices = [self_weights, cross_weights, fc_in, fc_out]
         moments = [self_moment, cross_moment, fc_in_moment, fc_out_moment]
         if sub % 128 == 0:
-            return prepared(place_now, matrices, moments, shards, sub, [first])
+            return prepared(place_now, matrices, moments, shards, sub, [])
         whole = jnp.stack(
             [
                 self_weights.astype(jnp.bfloat16),
@@ -1014,11 +1053,14 @@
         quarters = [of_rep(whole[kind]) for kind in range(1, 4)]
         return whole, quarters, jnp.stack(wide_old), jnp.stack(square_old)
 
-    shares, (wide_moments, square_moments) = gather_kinds(
-        of_rep(self_weights).astype(jnp.bfloat16), prepare
-    )
-    self_full = placed_blocks(place_now, shares[0], 0, chips, [])
-    cross_full = placed_blocks(place_now, shares[1], 1, chips, [])
+    state = {"by_x": [], "by_y": [], "came": [], "sent": []}
+    state["arrived"] = first_blocks(of_rep(self_weights).astype(jnp.bfloat16))
+    state["shards"], state["quarters"], wide_moments, square_moments = prepare()
+    state["other_shards"] = swap(state["shards"])
+    run_phase(state, 0, [state["shards"]])
+    run_phase(state, 1, [state["other_shards"]])
+    run_phase(state, 2, [])
+    self_full = placed_blocks(place_now, shares_of(state, 0), 0, chips, [])
 
     def first_sums(kinds, others, *waited):
         received = [swap(other) for other in others]
@@ -1052,13 +1094,20 @@
     query_rows = matmul(first_low, self_full[0]).astype(jnp.bfloat16)
     incoming_keys = matmul(first_low, self_full[1]).astype(jnp.bfloat16)
     incoming_values = matmul(first_low, self_full[2]).astype(jnp.bfloat16)
+    run_phase(state, 3, [query_rows, incoming_keys, incoming_values])
+    cross_full = placed_blocks(place_now, shares_of(state, 1), 1, chips, [])
     attended_values = attend_forward(query_rows, incoming_keys, incoming_values, dec_len, True)
     after_self = source + matmul(attended_values, self_full[3])
     second, second_unit, second_inv = normalize_parts(after_self, gain_rows[1], bias_rows[1])
     second_low = second.astype(jnp.bfloat16)
-    cross_query = matmul(second_low, cross_full[0]).astype(jnp.bfloat16)
     cross_keys = matmul(encoded, cross_full[1]).astype(jnp.bfloat16)
     cross_values = matmul(encoded, cross_full[2]).astype(jnp.bfloat16)
+    run_phase(state, 4, [cross_keys, cross_values, after_self])
+    hidden_shares = [
+        shares_of(state, 2),
+        shares_of(state, 3, (swap(state["by_x"][-1]), swap(state["by_y"][-1]))),
+    ]
+    cross_query = matmul(second_low, cross_full[0]).astype(jnp.bfloat16)
     cross_mixed = attend_forward(cross_query, cross_keys, cross_values, enc_len, False)
     after_cross = after_self + matmul(cross_mixed, cross_full[3])
     third, third_unit, third_inv = normalize_parts(after_cross, gain_rows[2], bias_rows[2])
@@ -1066,7 +1115,7 @@
     grad_out = cotangent[0].astype(jnp.float32)
     grad_branch = cotangent[0]
     block_out, grad_third, hidden, grad_pre = feed_forward(
-        place_now, shares[2], shares[3], chips, third_low, after_cross, grad_branch
+        place_now, *hidden_shares, chips, third_low, after_cross, grad_branch
     )
     wide_kinds = [
         ([third_low] * reps, grad_pre, rows, False),
@@ -1090,17 +1139,18 @@
         True,
     )
     cross_other = weight_rows(place_now, [cross_kind])[0]
-    grad_second = matmul_right_t(grad_cq, cross_full[0])
-    grad_norm, second_gain, second_bias = normalize_back(
-        grad_second, second_unit, second_inv, gain_rows[1]
-    )
-    grad_self = grad_cross + grad_norm
-    self_branch = grad_self.astype(jnp.bfloat16)
-    grad_mixed = matmul_right_t(self_branch, self_full[3]).astype(jnp.bfloat16)
-    wide_stage, wide_token = second_sums(wide_stage, grad_mixed)
-    cross_stage = first_sums([cross_kind], [cross_other], wide_token)
+    grad_self, self_branch, grad_mixed, second_gain, second_bias = branch_back(
+        grad_cq,
+        cross_full[0],
+        after_self,
+        gain_rows[1:2],
+        grad_cross,
+        self_full[3],
+        cross_other,
+    )
+    second_gain, second_bias = second_gain[0], second_bias[0]
     grad_sq, grad_sk, grad_sv = attend_backward(
-        query_rows, incoming_keys, incoming_values, dec_len, True, grad_mixed, cross_stage[0]
+        query_rows, incoming_keys, incoming_values, dec_len, True, grad_mixed
     )
     self_kind = (
         [first_low, first_low, first_low, attended_values],
@@ -1108,21 +1158,18 @@
         rows,
         True,
     )
-    self_other = weight_rows(place_now, [self_kind])[0]
+    wide_stage, wide_token = second_sums(wide_stage, grad_sq)
+    cross_stage = first_sums([cross_kind], [cross_other], wide_token)
+    self_other = weight_rows(place_now, [self_kind], None, [cross_stage[0]])[0]
     wide_stage = third_sums(wide_stage, self_other)
     cross_stage, cross_token = second_sums(cross_stage, wide_stage[0])
     self_stage = first_sums([self_kind], [self_other], cross_token)
-    grad_sq = held_until(grad_sq, self_stage[0])
-    grad_states = matmul_right_t(grad_ck, cross_full[1]) + matmul_right_t(grad_cv, cross_full[2])
-    grad_first = (
-        matmul_right_t(grad_sq, self_full[0])
-        + matmul_right_t(grad_sk, self_full[1])
-        + matmul_right_t(grad_sv, self_full[2])
-    )
-    grad_norm, first_gain, first_bias = normalize_back(
-        grad_first, first_unit, first_inv, gain_rows[0]
-    )
-    grad_tokens = grad_self + grad_norm
+    cross_stage = third_sums(cross_stage, self_stage[0])
+    self_stage, self_token = second_sums(self_stage, cross_stage[0])
+    wide_fresh = fresh_blocks(place_now, *wide_stage, wide_moments, self_token)
+    wide_grads = wide_fresh[0]
+    self_stage = third_sums(self_stage, wide_grads)
+
     def owned(grads_fresh):
         mine, *sent = grads_fresh[1:]
         arrived = [from_chip(sent[turn - 1], turn) for turn in range(1, chips)]
@@ -1135,13 +1182,10 @@
             [jnp.where(is_lower, result[0], other), jnp.where(is_lower, other, result[0])]
         )
 
-    self_stage, self_token = second_sums(self_stage)
-    wide_fresh = fresh_blocks(place_now, *wide_stage, wide_moments)
-    wide_grads = wide_fresh[0]
     wide_own = owned(wide_fresh)
-    cross_stage = third_sums(cross_stage, wide_grads)
-    self_stage = third_sums(self_stage)
-    to_x, to_y, kept, later = gram_parts(place_now, *wide_own, reps, self_token)
+    to_x, to_y, kept, later = gram_parts(
+        place_now, *wide_own, reps, self_stage[0]
+    )
     gram_stage, gram_token = second_sums((kept, later, from_rep(to_x, 1), from_rep(to_y, 2)))
     kept, by_x, by_y, last_x, last_y = gram_stage
     quarter = jnp.concatenate(
@@ -1167,7 +1211,7 @@
     wide_grads_shared = share_pair(wide_grads)
     square_grads_shared = share_pair(square_grads)
     wide_rows = gram_schulz(
-        place_now, quarters, *wide_own, rows, wide_grads_shared[1], self_stage[0]
+        place_now, quarters, *wide_own, rows, wide_grads_shared[1]
     )
     wide_orth_shared = share_pair(to_both(wide_rows))
     square_rows = square_schulz(
@@ -1177,6 +1221,18 @@
         to_both(square_rows), wide_orth_shared[3], square_grads_shared[3]
     )
     square_orth_shared = share_pair(square_orth)
+    late_sq = held_until(grad_sq, gram_token)
+    late_ck = held_until(grad_ck, gram_token)
+    grad_states = matmul_right_t(late_ck, cross_full[1]) + matmul_right_t(grad_cv, cross_full[2])
+    grad_first = (
+        matmul_right_t(late_sq, self_full[0])
+        + matmul_right_t(grad_sk, self_full[1])
+        + matmul_right_t(grad_sv, self_full[2])
+    )
+    grad_norm, first_gain, first_bias = normalize_back(
+        grad_first, first_unit, first_inv, gain_rows[0]
+    )
+    grad_tokens = grad_self + grad_norm
     norm_local = jnp.stack(
         [
             jnp.stack([first_gain, second_gain, third_gain]),
@@ -1191,6 +1247,7 @@
     width_part = norm_moment.shape[2]
     norm_grad = lax.dynamic_slice_in_dim(norm_total, my_place * width_part, width_part, 2)
 
+    wide_grads_shared[0] = held_until(wide_grads_shared[0], wide_rows)
     in_shared, out_shared = to_replicas(wide_grads_shared)
     self_shared, cross_shared = to_replicas(square_grads_shared)
     in_orth_shared, out_orth_shared = to_replicas(wide_orth_shared)

time: 765 us -> 779 us (1.018)
  waiting for transfers between devices: 267 us -> 286 us
    ppermute x48, waiting for transfers between devices: 87.6 us -> 133 us  [from_rep(): lax.ppermute(values, 'rep', [(index ^ step, index) for index in range(rep...]
    ppermute x32, waiting for transfers between devices: 169 us -> 140 us  [from_chip(): return lax.ppermute(values, 'shard', pairs)]
    unnamed x273 -> x245, local copies, waits for them, and re-layouts: 33.7 us -> 27.5 us
    dot_general x8 -> x6, matrix products: 15.8 us -> 13.6 us  [matmul_right_t(): lax.dot_general(left, right, (((1,), (1,)), ((), ())), preferred_element_...]
  transfers between devices with their start and end apart: 95 -> 95, of which waited for: 45 -> 45; matrix products, arithmetic and copies ran while one was open for 13% -> 13% of each run, Pallas kernels for 22% -> 21%
where the time goes in v2:
time: 779 us; the launch traced here: 774 us
  waiting for transfers between devices  286 us (37%)
  Pallas kernels  256 us (33%)
  starting transfers between devices  103 us (13%)
  other arithmetic  47.5 us (6%)
  local copies, waits for them, and re-layouts  46.4 us (6%)
  matrix products  31.6 us (4%)
    ppermute x32, waiting for transfers between devices, from_chip(): return lax.ppermute(values, 'shard', pairs)  140 us
    ppermute x48, waiting for transfers between devices, from_rep(): lax.ppermute(values, 'rep', [(index ^ step, index) for index in range(rep...  133 us
    ppermute x48, starting transfers between devices, from_rep(): lax.ppermute(values, 'rep', [(index ^ step, index) for index in range(rep...  53.6 us
    ppermute x32, starting transfers between devices, from_chip(): return lax.ppermute(values, 'shard', pairs)  47.9 us
    pallas_call x4, Pallas kernels, attention_call(): pl.pallas_call(kernel, out_shape=tuple(out_shapes), in_specs=[pl.BlockSpe...  47.1 us
    pallas_call x6, Pallas kernels, weight_rows(): pl.pallas_call(kernel, out_shape=tuple(out_shapes), in_specs=[pl.BlockSpe...  43.6 us
    pallas_call x1, Pallas kernels, gram_schulz(): pl.pallas_call(kernel, out_shape=low(2, rows, size), in_specs=[pl.BlockSp...  33.7 us
    unnamed x245, local copies, waits for them, and re-layouts  27.5 us
  transfers between devices with their start and end apart: 95, of which 45 were waited for; matrix products, arithmetic and copies ran while one was open for 13% of the time, Pallas kernels for 21%

profile of v2, /device:TPU:0, one launch (start us, length us, event | category | flops | bytes accessed | tf_op | source)
XLA Modules:
  0.0 773.7 jit_solution(7300861440772014741)
XLA Ops:
  1.3 7.9 %shard_map.318 = (bf16[4,4,128,1024]{3,2,1,0:T(8,128)(2,1)}, bf16[128,1024]{1,0:T(8,128)(2,1)}, bf16[128,1024]{1,0:T(8,128)(2,1)}, bf16[128,1024]{1,0:T(8,128)(2...) custom-call(s32[4]{0:T(128)} %pad_add_fusion.place_ref, f32[4,128,1024]{2,1,0:T(8,128)} %refs_0_.1, ...), custom_call_target="tpu_custom_call" | custom-call | flops 1024 | bytes 1024 | tf_op jit(solution)/shard_map/pallas_call | solution.py:871
  22.2 16.3 %collective-permute-done.1.refs_1_ = bf16[128,1024]{1,0:T(8,128)(2,1)S(1)} collective-permute-done((bf16[128,1024]{1,0:T(8,128)(2,1)S(1)}, bf16[128,1024]{1,0:T(8,128)(2,1)S(1)}, u32[]{:S(2)}, u32[]{:S(2)}) %collective-permute-start.1) | collective-permute-done | bytes 262176 | tf_op jit(solution)/shard_map/ppermute | solution.py:966
  52.5 12.0 %collective-permute-done.6.refs_1_ = bf16[128,1024]{1,0:T(8,128)(2,1)S(1)} collective-permute-done((bf16[128,1024]{1,0:T(8,128)(2,1)}, bf16[128,1024]{1,0:T(8,128)(2,1)S(1)}, u32[]{:S(2)}, u32[]{:S(2)}) %collective-permute-start.6) | collective-permute-done | bytes 262176 | tf_op jit(solution)/shard_map/ppermute | solution.py:966
  64.4 10.2 %collective-permute-done.7.refs_2_ = bf16[128,1024]{1,0:T(8,128)(2,1)S(1)} collective-permute-done((bf16[128,1024]{1,0:T(8,128)(2,1)}, bf16[128,1024]{1,0:T(8,128)(2,1)S(1)}, u32[]{:S(2)}, u32[]{:S(2)}) %collective-permute-start.7) | collective-permute-done | bytes 262176 | tf_op jit(solution)/shard_map/ppermute | solution.py:966
  83.7 8.8 %collective-permute-done.13.refs_0_ = bf16[128,1024]{1,0:T(8,128)(2,1)S(1)} collective-permute-done((bf16[128,1024]{1,0:T(8,128)(2,1)}, bf16[128,1024]{1,0:T(8,128)(2,1)S(1)}, u32[]{:S(2)}, u32[]{:S(2)}) %collective-permute-start.13) | collective-permute-done | bytes 262176 | tf_op jit(solution)/shard_map/ppermute | solution.py:966
  92.6 13.7 %collective-permute-done.14.refs_1_ = bf16[128,1024]{1,0:T(8,128)(2,1)S(1)} collective-permute-done((bf16[128,1024]{1,0:T(8,128)(2,1)}, bf16[128,1024]{1,0:T(8,128)(2,1)S(1)}, u32[]{:S(2)}, u32[]{:S(2)}) %collective-permute-start.14) | collective-permute-done | bytes 262176 | tf_op jit(solution)/shard_map/ppermute | solution.py:966
  124.5 7.7 %shard_map.324 = (bf16[4,2,128,1024]{3,2,1,0:T(8,128)(2,1)}, bf16[4,2,128,1024]{3,2,1,0:T(8,128)(2,1)}, bf16[4,2,128,1024]{3,2,1,0:T(8,128)(2,1)}, bf16[4,2,128,1024]{3,2,1,0:T(8,128)(2,1)}) custom-call(s32[4]{0:T(128)} %pad_add_fusion.place_ref, bf16[4,4,128,1024]{3,2,1,0:T(8,128)(2,1)} %get-tuple-element.120.refs_3_.refs_0_.refs_12_, ...), custom_call_target="tpu_custom_call" | custom-call | flops 1024 | bytes 1024 | tf_op jit(solution)/shard_map/pallas_call | solution.py:740
  156.0 9.6 %shard_map.325.refs_1_ = bf16[256,1024]{1,0:T(8,128)(2,1)} custom-call(s32[1]{0:T(128)S(6)} %copy.84.count_ref, bf16[256,1024]{1,0:T(8,128)(2,1)} %convolution_convert_fusion.6.query_ref.refs_5_, bf16[256,1024]{1,0:T(8,128)(2,1)} %convolution_convert_fusion.5.key_ref.refs_6_, bf16[256,1024]{1,0:T(8,128)(2,1)} %convolution_convert_fusion.4.value_ref.refs_7_), custom_call_target="tpu_custom_call" | custom-call | flops 1024 | bytes 1024 | tf_op jit(solution)/shard_map/pallas_call | solution.py:86
  170.0 7.7 %shard_map.328 = (bf16[4,2,128,1024]{3,2,1,0:T(8,128)(2,1)}, bf16[4,2,128,1024]{3,2,1,0:T(8,128)(2,1)}, bf16[4,2,128,1024]{3,2,1,0:T(8,128)(2,1)}, bf16[4,2,128,1024]{3,2,1,0:T(8,128)(2,1)}) custom-call(s32[4]{0:T(128)} %pad_add_fusion.place_ref, bf16[4,4,128,1024]{3,2,1,0:T(8,128)(2,1)} %get-tuple-element.120.refs_3_.refs_0_.refs_12_, ...), custom_call_target="tpu_custom_call" | custom-call | flops 1024 | bytes 1024 | tf_op jit(solution)/shard_map/pallas_call | solution.py:740
  192.0 10.5 %shard_map.329.refs_2_ = bf16[256,1024]{1,0:T(8,128)(2,1)} custom-call(s32[1]{0:T(128)S(6)} %copy.85.count_ref, bf16[256,1024]{1,0:T(8,128)(2,1)} %convolution_convert_fusion.3.query_ref, bf16[384,1024]{1,0:T(8,128)(2,1)} %fusion.3.key_ref.refs_2_, bf16[384,1024]{1,0:T(8,128)(2,1)} %fusion.4.value_ref.refs_3_), custom_call_target="tpu_custom_call" | custom-call | flops 1024 | bytes 1024 | tf_op jit(solution)/shard_map/pallas_call | solution.py:86
  208.8 17.7 %shard_map.331 = (f32[256,1024]{1,0:T(8,128)}, f32[256,1024]{1,0:T(8,128)}, bf16[256,1024]{1,0:T(8,128)(2,1)}, bf16[256,1024]{1,0:T(8,128)(2,1)}, bf16[256,1024]...) custom-call(s32[4]{0:T(128)} %pad_add_fusion.place_ref, ...), custom_call_target="tpu_custom_call" | custom-call | flops 1024 | bytes 1024 | tf_op jit(solution)/shard_map/pallas_call | solution.py:810
  226.5 7.5 shard_map.332
  247.5 10.5 %shard_map.333 = (bf16[2,2,256,1024]{3,2,1,0:T(8,128)(2,1)}, bf16[2,2,256,1024]{3,2,1,0:T(8,128)(2,1)}, bf16[2,2,256,1024]{3,2,1,0:T(8,128)(2,1)}, bf16[2,2,256,1024]{3,2,1,0:T(8,128)(2,1)}) custom-call(s32[4]{0:T(128)} %pad_add_fusion.place_ref, bf16[256,1024]{1,0:T(8,128)(2,1)} %add_convert_fusion.1.third_ref.refs_0_, ...), custom_call_target="tpu_custom_call" | custom-call | flops 1024 | bytes 1024 | tf_op jit(solution)/shard_map/pallas_call | solution.py:502
  258.0 14.2 %shard_map.334 = (bf16[256,1024]{1,0:T(8,128)(2,1)}, bf16[384,1024]{1,0:T(8,128)(2,1)}, bf16[384,1024]{1,0:T(8,128)(2,1)}) custom-call(s32[1]{0:T(128)S(6)} %copy.85.count_ref, bf16[256,1024]{1,0:T(8,128)(2,1)} %convolution_convert_fusion.3.query_ref, bf16[384,1024]{1,0:T(8,128)(2,1)} %fusion.3.key_ref.refs_2_, bf16[384,1024]{1,0:T(8,128)(2,1)} %fusion.4.value_ref.refs_3_, ...), custom_call_target="tpu_custom_call" | custom-call | flops 1024 | bytes 1024 | tf_op jit(solution)/shard_map/pallas_call | solution.py:86
  288.0 12.8 %shard_map.337 = (bf16[256,1024]{1,0:T(8,128)(2,1)}, bf16[256,1024]{1,0:T(8,128)(2,1)}, bf16[256,1024]{1,0:T(8,128)(2,1)}) custom-call(s32[1]{0:T(128)S(6)} %copy.84.count_ref, bf16[256,1024]{1,0:T(8,128)(2,1)} %convolution_convert_fusion.6.query_ref.refs_5_, bf16[256,1024]{1,0:T(8,128)(2,1)} %convolution_convert_fusion.5.key_ref.refs_6_, ...), custom_call_target="tpu_custom_call" | custom-call | flops 1024 | bytes 1024 | tf_op jit(solution)/shard_map/pallas_call | solution.py:86
  300.8 26.0 %collective-permute-done.32.x_ref = bf16[2,2,256,1024]{3,2,1,0:T(8,128)(2,1)S(1)} collective-permute-done((bf16[2,2,256,1024]{3,2,1,0:T(8,128)(2,1)}, bf16[2,2,256,1024]{3,2,1,0:T(8,128)(2,1)S(1)}, u32[]{:S(2)}, u32[]{:S(2)}) %collective-permute-start.32) | collective-permute-done | bytes 2097184 | tf_op jit(solution)/shard_map/ppermute | solution.py:969
  333.3 7.5 shard_map.339
  350.2 21.9 %collective-permute-done.34.last_x_ref = bf16[2,256,1024]{2,1,0:T(8,128)(2,1)S(1)} collective-permute-done((bf16[2,256,1024]{2,1,0:T(8,128)(2,1)S(1)}, bf16[2,256,1024]{2,1,0:T(8,128)(2,1)S(1)}, u32[]{:S(2)}, u32[]{:S(2)}) %collective-permute-start.34) | collective-permute-done | bytes 1048608 | tf_op jit(solution)/shard_map/ppermute | solution.py:969
  379.9 14.2 %collective-permute-done.41.x_ref = bf16[1,2,256,1024]{3,2,1,0:T(8,128)(2,1)S(1)} collective-permute-done((bf16[1,2,256,1024]{3,2,1,0:T(8,128)(2,1)}, bf16[1,2,256,1024]{3,2,1,0:T(8,128)(2,1)S(1)}, u32[]{:S(2)}, u32[]{:S(2)}) %collective-permute-start.41) | collective-permute-done | bytes 1048608 | tf_op jit(solution)/shard_map/ppermute | solution.py:969
  403.4 6.6 shard_map.343
  424.9 10.1 %collective-permute-done.43.x_ref = bf16[1,2,256,1024]{3,2,1,0:T(8,128)(2,1)S(1)} collective-permute-done((bf16[1,2,256,1024]{3,2,1,0:T(8,128)(2,1)}, bf16[1,2,256,1024]{3,2,1,0:T(8,128)(2,1)S(1)}, u32[]{:S(2)}, u32[]{:S(2)}) %collective-permute-start.43) | collective-permute-done | bytes 1048608 | tf_op jit(solution)/shard_map/ppermute | solution.py:969
  442.0 15.1 %collective-permute-done.38.refs_1_ = bf16[2,128,1024]{2,1,0:T(8,128)(2,1)S(1)} collective-permute-done((bf16[2,128,1024]{2,1,0:T(8,128)(2,1)}, bf16[2,128,1024]{2,1,0:T(8,128)(2,1)S(1)}, u32[]{:S(2)}, u32[]{:S(2)}) %collective-permute-start.38) | collective-permute-done | bytes 524320 | tf_op jit(solution)/shard_map/ppermute | solution.py:966
  472.2 15.3 %collective-permute-done.48 = bf16[128,1024]{1,0:T(8,128)(2,1)S(1)} collective-permute-done((bf16[128,1024]{1,0:T(8,128)(2,1)}, bf16[128,1024]{1,0:T(8,128)(2,1)S(1)}, u32[]{:S(2)}, u32[]{:S(2)}) %collective-permute-start.48) | collective-permute-done | bytes 262176 | tf_op jit(solution)/shard_map/ppermute | solution.py:966
  503.3 13.4 %collective-permute-done.59 = bf16[1,128,1024]{2,1,0:T(8,128)(2,1)S(1)} collective-permute-done((bf16[1,128,1024]{2,1,0:T(8,128)(2,1)}, bf16[1,128,1024]{2,1,0:T(8,128)(2,1)S(1)}, u32[]{:S(2)}, u32[]{:S(2)}) %collective-permute-start.59) | collective-permute-done | bytes 262176 | tf_op jit(solution)/shard_map/ppermute | solution.py:966
  520.0 11.8 %collective-permute-done.57 = bf16[1,128,1024]{2,1,0:T(8,128)(2,1)S(1)} collective-permute-done((bf16[1,128,1024]{2,1,0:T(8,128)(2,1)}, bf16[1,128,1024]{2,1,0:T(8,128)(2,1)S(1)}, u32[]{:S(2)}, u32[]{:S(2)}) %collective-permute-start.57) | collective-permute-done | bytes 262176 | tf_op jit(solution)/shard_map/ppermute | solution.py:966
  550.8 12.0 %collective-permute-start.83 = (bf16[128,1024]{1,0:T(8,128)(2,1)S(1)}, bf16[128,1024]{1,0:T(8,128)(2,1)S(1)}, u32[]{:S(2)}, u32[]{:S(2)}) collective-permute-start(bf16[128,1024]{1,0:T(8,128)(2,1)S(1)} %copy-done.110), channel_id=1, source_target_pairs={{6,0},{7,1},{0,2},{1,3},{2,4},{3,5},{4,6},{5,7},{14,8},{15,9},{8,1... | collective-permute-start | bytes 786440 | tf_op jit(solution)/shard_map/ppermute | solution.py:966
  570.5 6.5 shard_map.348
  583.3 13.9 %collective-permute-done.62 = bf16[128,1024]{1,0:T(8,128)(2,1)S(1)} collective-permute-done((bf16[128,1024]{1,0:T(8,128)(2,1)S(1)}, bf16[128,1024]{1,0:T(8,128)(2,1)S(1)}, u32[]{:S(2)}, u32[]{:S(2)}) %collective-permute-start.62) | collective-permute-done | bytes 262176 | tf_op jit(solution)/shard_map/ppermute | solution.py:969
  620.4 6.8 collective-permute-done.71.y_ref
  635.5 33.7 %shard_map.353.refs_1_.refs_0_ = bf16[2,128,1024]{2,1,0:T(8,128)(2,1)} custom-call(s32[4]{0:T(128)} %pad_add_fusion.place_ref, bf16[256,1024]{1,0:T(8,128)(2,1)} %copy-done.56, bf16[256,1024]{1,0:T(8,128)(2,1)} %copy-done.67, bf16[256,1024]{1,0:T(8,128)(2,1)} %copy-done.66, bf16[128,1024]{1,0:T(8,128)(2,1)} %copy-done.99, bf16[128,1024]{1,0:T(8,128)(2,1)} %copy-done.76, ...), custom_call_target="tpu_custom_call" | custom-call | flops 1024 | bytes 1024 | tf_op jit(solution)/shard_map/pallas_call | solution.py:380
  692.1 25.5 %shard_map.356 = bf16[2,128,1024]{2,1,0:T(8,128)(2,1)} custom-call(bf16[512,1024]{1,0:T(8,128)(2,1)} %constant_dynamic-update-slice_fusion.4.mine_ref, bf16[512,1024]{1,0:T(8,128)(2,1)} %collective-permute-done.84.sibling_ref, bf16[2,128,1024]{2,1,0:T(8,128)(2,1)} %shard_map.353.refs_1_.refs_0_, bf16[2,128,1024]{2,1,0:T(8,128)(2,1)} %copy-done.44, ...), custom_call_target="tpu_custom_call" | custom-call | flops 1024 | bytes 1024 | tf_op jit(solution)/shard_map/pallas_call | solution.py:233
  730.0 7.4 collective-permute-done.87
  (537 shorter events, 355.6 us)
Async XLA Ops:
  9.2 65.4 %collective-permute-start.8 = (bf16[4,4,128,1024]{3,2,1,0:T(8,128)(2,1)}, bf16[4,4,128,1024]{3,2,1,0:T(8,128)(2,1)}, u32[]{:S(2)}, u32[]{:S(2)}) collective-permute-start(bf16[4,4,128,1024]{3,2,1,0:T(8,128)(2,1)} %get-tuple-element.120.refs_3_.refs_0_.refs_12_), channel_id=1, source_target_pairs={{0,1},{1,0},{2,3},{3,2},{4,5},{5,4},{6,7},{7,6},{8,9},{9,8},{10,11... | collective-permute-start | bytes 12582920 | tf_op jit(solution)/shard_map/ppermute | solution.py:958
  42.5 32.1 %collective-permute-start.9 = (bf16[384,1024]{1,0:T(8,128)(2,1)}, bf16[384,1024]{1,0:T(8,128)(2,1)S(1)}, u32[]{:S(2)}, u32[]{:S(2)}) collective-permute-start(bf16[384,1024]{1,0:T(8,128)(2,1)} %get-tuple-element.124.refs_1_), channel_id=1, source_target_pairs={{0,1},{1,0},{2,3},{3,2},{4,5},{5,4},{6,7},{7,6},{8,9},{9,8},{10,11... | collective-permute-start | bytes 2359304 | tf_op jit(solution)/shard_map/ppermute | solution.py:958
  42.5 32.1 %collective-permute-start.3 = (bf16[384,1024]{1,0:T(8,128)(2,1)}, bf16[384,1024]{1,0:T(8,128)(2,1)S(1)}, u32[]{:S(2)}, u32[]{:S(2)}) collective-permute-start(bf16[384,1024]{1,0:T(8,128)(2,1)} %get-tuple-element.121.refs_1_), channel_id=1, source_target_pairs={{8,0},{0,8},{24,16},{16,24},{9,1},{1,9},{25,17},{17,25},{10,2},{2,... | collective-permute-start | bytes 2359304 | tf_op jit(solution)/shard_map/ppermute | solution.py:969
  44.1 30.6 %collective-permute-start.4 = (bf16[384,1024]{1,0:T(8,128)(2,1)}, bf16[384,1024]{1,0:T(8,128)(2,1)S(1)}, u32[]{:S(2)}, u32[]{:S(2)}) collective-permute-start(bf16[384,1024]{1,0:T(8,128)(2,1)} %get-tuple-element.122), channel_id=1, source_target_pairs={{16,0},{24,8},{0,16},{8,24},{17,1},{25,9},{1,17},{9,25},{18,2},{26... | collective-permute-start | bytes 2359304 | tf_op jit(solution)/shard_map/ppermute | solution.py:969
  80.1 29.8 %collective-permute-start.12 = (bf16[1152,1024]{1,0:T(8,128)(2,1)}, bf16[1152,1024]{1,0:T(8,128)(2,1)S(1)}, u32[]{:S(2)}, u32[]{:S(2)}) collective-permute-start(bf16[1152,1024]{1,0:T(8,128)(2,1)} %get-tuple-element.127.refs_1_), channel_id=1, source_target_pairs={{0,1},{1,0},{2,3},{3,2},{4,5},{5,4},{6,7},{7,6},{8,9},{9,8},{10,11... | collective-permute-start | bytes 7077896 | tf_op jit(solution)/shard_map/ppermute | solution.py:958
  80.1 28.6 %collective-permute-start.10 = (bf16[576,1024]{1,0:T(8,128)(2,1)}, bf16[576,1024]{1,0:T(8,128)(2,1)S(1)}, u32[]{:S(2)}, u32[]{:S(2)}) collective-permute-start(bf16[576,1024]{1,0:T(8,128)(2,1)} %get-tuple-element.125.refs_1_), channel_id=1, source_target_pairs={{8,0},{0,8},{24,16},{16,24},{9,1},{1,9},{25,17},{17,25},{10,2},{2,... | collective-permute-start | bytes 3538952 | tf_op jit(solution)/shard_map/ppermute | solution.py:969
  81.6 28.3 %collective-permute-start.11 = (bf16[576,1024]{1,0:T(8,128)(2,1)}, bf16[576,1024]{1,0:T(8,128)(2,1)S(1)}, u32[]{:S(2)}, u32[]{:S(2)}) collective-permute-start(bf16[576,1024]{1,0:T(8,128)(2,1)} %get-tuple-element.126), channel_id=1, source_target_pairs={{16,0},{24,8},{0,16},{8,24},{17,1},{25,9},{1,17},{9,25},{18,2},{26... | collective-permute-start | bytes 3538952 | tf_op jit(solution)/shard_map/ppermute | solution.py:969
  117.4 28.7 %collective-permute-start.17 = (bf16[576,1024]{1,0:T(8,128)(2,1)}, bf16[576,1024]{1,0:T(8,128)(2,1)S(1)}, u32[]{:S(2)}, u32[]{:S(2)}) collective-permute-start(bf16[576,1024]{1,0:T(8,128)(2,1)} %get-tuple-element.134.refs_1_), channel_id=1, source_target_pairs={{8,0},{0,8},{24,16},{16,24},{9,1},{1,9},{25,17},{17,25},{10,2},{2,... | collective-permute-start | bytes 3538952 | tf_op jit(solution)/shard_map/ppermute | solution.py:969
  118.1 28.3 %collective-permute-start.18 = (bf16[576,1024]{1,0:T(8,128)(2,1)}, bf16[576,1024]{1,0:T(8,128)(2,1)S(1)}, u32[]{:S(2)}, u32[]{:S(2)}) collective-permute-start(bf16[576,1024]{1,0:T(8,128)(2,1)} %get-tuple-element.135), channel_id=1, source_target_pairs={{16,0},{24,8},{0,16},{8,24},{17,1},{25,9},{1,17},{9,25},{18,2},{26... | collective-permute-start | bytes 3538952 | tf_op jit(solution)/shard_map/ppermute | solution.py:969
  152.5 30.8 %collective-permute-start.23 = (bf16[576,1024]{1,0:T(8,128)(2,1)}, bf16[576,1024]{1,0:T(8,128)(2,1)S(1)}, u32[]{:S(2)}, u32[]{:S(2)}) collective-permute-start(bf16[576,1024]{1,0:T(8,128)(2,1)} %get-tuple-element.142.refs_13_), channel_id=1, source_target_pairs={{8,0},{0,8},{24,16},{16,24},{9,1},{1,9},{25,17},{17,25},{10,2},{2,... | collective-permute-start | bytes 3538952 | tf_op jit(solution)/shard_map/ppermute | solution.py:969
  153.2 30.1 %collective-permute-start.24 = (bf16[576,1024]{1,0:T(8,128)(2,1)}, bf16[576,1024]{1,0:T(8,128)(2,1)S(1)}, u32[]{:S(2)}, u32[]{:S(2)}) collective-permute-start(bf16[576,1024]{1,0:T(8,128)(2,1)} %get-tuple-element.143), channel_id=1, source_target_pairs={{16,0},{24,8},{0,16},{8,24},{17,1},{25,9},{1,17},{9,25},{18,2},{26... | collective-permute-start | bytes 3538952 | tf_op jit(solution)/shard_map/ppermute | solution.py:969
  278.5 54.8 %collective-permute-start.36 = (bf16[4,512,1024]{2,1,0:T(8,128)(2,1)}, bf16[4,512,1024]{2,1,0:T(8,128)(2,1)}, u32[]{:S(2)}, u32[]{:S(2)}) collective-permute-start(bf16[4,512,1024]{2,1,0:T(8,128)(2,1)} %shard_map.335.refs_0_), channel_id=1, source_target_pairs={{0,1},{1,0},{2,3},{3,2},{4,5},{5,4},{6,7},{7,6},{8,9},{9,8},{10,11... | collective-permute-start | bytes 12582920 | tf_op jit(solution)/shard_map/ppermute | solution.py:958
  278.7 48.1 %collective-permute-start.32 = (bf16[2,2,256,1024]{3,2,1,0:T(8,128)(2,1)}, bf16[2,2,256,1024]{3,2,1,0:T(8,128)(2,1)S(1)}, u32[]{:S(2)}, u32[]{:S(2)}) collective-permute-start(bf16[2,2,256,1024]{3,2,1,0:T(8,128)(2,1)} %get-tuple-element.166), channel_id=1, source_target_pairs={{8,0},{0,8},{24,16},{16,24},{9,1},{1,9},{25,17},{17,25},{10,2},{2,... | collective-permute-start | bytes 6291464 | tf_op jit(solution)/shard_map/ppermute | solution.py:969
  279.8 47.6 %collective-permute-start.33 = (bf16[2,2,256,1024]{3,2,1,0:T(8,128)(2,1)S(1)}, bf16[2,2,256,1024]{3,2,1,0:T(8,128)(2,1)S(1)}, u32[]{:S(2)}, u32[]{:S(2)}) collective-permute-start(bf16[2,2,256,1024]{3,2,1,0:T(8,128)(2,1)S(1)} %copy-done.108), channel_id=1, source_target_pairs={{16,0},{24,8},{0,16},{8,24},{17,1},{25,9},{1,17},{9,25},{18,2},{26... | collective-permute-start | bytes 6291464 | tf_op jit(solution)/shard_map/ppermute | solution.py:969
  346.1 55.3 %collective-permute-start.40 = (bf16[4,512,1024]{2,1,0:T(8,128)(2,1)}, bf16[4,512,1024]{2,1,0:T(8,128)(2,1)S(1)}, u32[]{:S(2)}, u32[]{:S(2)}) collective-permute-start(bf16[4,512,1024]{2,1,0:T(8,128)(2,1)} %shard_map.340.refs_0_), channel_id=1, source_target_pairs={{0,1},{1,0},{2,3},{3,2},{4,5},{5,4},{6,7},{7,6},{8,9},{9,8},{10,11... | collective-permute-start | bytes 12582920 | tf_op jit(solution)/shard_map/ppermute | solution.py:958
  348.7 45.4 %collective-permute-start.41 = (bf16[1,2,256,1024]{3,2,1,0:T(8,128)(2,1)}, bf16[1,2,256,1024]{3,2,1,0:T(8,128)(2,1)S(1)}, u32[]{:S(2)}, u32[]{:S(2)}) collective-permute-start(bf16[1,2,256,1024]{3,2,1,0:T(8,128)(2,1)} %get-tuple-element.181), channel_id=1, source_target_pairs={{8,0},{0,8},{24,16},{16,24},{9,1},{1,9},{25,17},{17,25},{10,2},{2,... | collective-permute-start | bytes 3145736 | tf_op jit(solution)/shard_map/ppermute | solution.py:969
  349.6 45.6 %collective-permute-start.42 = (bf16[1,2,256,1024]{3,2,1,0:T(8,128)(2,1)}, bf16[1,2,256,1024]{3,2,1,0:T(8,128)(2,1)S(1)}, u32[]{:S(2)}, u32[]{:S(2)}) collective-permute-start(bf16[1,2,256,1024]{3,2,1,0:T(8,128)(2,1)} %get-tuple-element.182), channel_id=1, source_target_pairs={{16,0},{24,8},{0,16},{8,24},{17,1},{25,9},{1,17},{9,25},{18,2},{26... | collective-permute-start | bytes 3145736 | tf_op jit(solution)/shard_map/ppermute | solution.py:969
  411.8 30.3 %collective-permute-start.37 = (bf16[2,128,1024]{2,1,0:T(8,128)(2,1)}, bf16[2,128,1024]{2,1,0:T(8,128)(2,1)S(1)}, u32[]{:S(2)}, u32[]{:S(2)}) collective-permute-start(bf16[2,128,1024]{2,1,0:T(8,128)(2,1)} %get-tuple-element.176), channel_id=1, source_target_pairs={{2,0},{3,1},{4,2},{5,3},{6,4},{7,5},{0,6},{1,7},{10,8},{11,9},{12,... | collective-permute-start | bytes 1572872 | tf_op jit(solution)/shard_map/ppermute | solution.py:966
  413.5 43.7 %collective-permute-start.38 = (bf16[2,128,1024]{2,1,0:T(8,128)(2,1)}, bf16[2,128,1024]{2,1,0:T(8,128)(2,1)S(1)}, u32[]{:S(2)}, u32[]{:S(2)}) collective-permute-start(bf16[2,128,1024]{2,1,0:T(8,128)(2,1)} %get-tuple-element.177), channel_id=1, source_target_pairs={{4,0},{5,1},{6,2},{7,3},{0,4},{1,5},{2,6},{3,7},{12,8},{13,9},{14,... | collective-permute-start | bytes 1572872 | tf_op jit(solution)/shard_map/ppermute | solution.py:966
  415.2 42.0 %collective-permute-start.39 = (bf16[2,128,1024]{2,1,0:T(8,128)(2,1)}, bf16[2,128,1024]{2,1,0:T(8,128)(2,1)S(1)}, u32[]{:S(2)}, u32[]{:S(2)}) collective-permute-start(bf16[2,128,1024]{2,1,0:T(8,128)(2,1)} %get-tuple-element.178), channel_id=1, source_target_pairs={{6,0},{7,1},{0,2},{1,3},{2,4},{3,5},{4,6},{5,7},{14,8},{15,9},{8,1... | collective-permute-start | bytes 1572872 | tf_op jit(solution)/shard_map/ppermute | solution.py:966
  439.5 49.0 %collective-permute-start.51 = (bf16[1,256,1024]{2,1,0:T(8,128)(2,1)}, bf16[1,256,1024]{2,1,0:T(8,128)(2,1)S(1)}, u32[]{:S(2)}, u32[]{:S(2)}) collective-permute-start(bf16[1,256,1024]{2,1,0:T(8,128)(2,1)} %get-tuple-element.190.refs_4_), channel_id=1, source_target_pairs={{8,0},{0,8},{24,16},{16,24},{9,1},{1,9},{25,17},{17,25},{10,2},{2,... | collective-permute-start | bytes 1572872 | tf_op jit(solution)/shard_map/ppermute | solution.py:969
  440.6 48.0 %collective-permute-start.52 = (bf16[1,256,1024]{2,1,0:T(8,128)(2,1)}, bf16[1,256,1024]{2,1,0:T(8,128)(2,1)S(1)}, u32[]{:S(2)}, u32[]{:S(2)}) collective-permute-start(bf16[1,256,1024]{2,1,0:T(8,128)(2,1)} %get-tuple-element.195), channel_id=1, source_target_pairs={{16,0},{24,8},{0,16},{8,24},{17,1},{25,9},{1,17},{9,25},{18,2},{26... | collective-permute-start | bytes 1572872 | tf_op jit(solution)/shard_map/ppermute | solution.py:969
  464.0 32.4 %collective-permute-start.65 = (bf16[2,128,1024]{2,1,0:T(8,128)(2,1)}, bf16[2,128,1024]{2,1,0:T(8,128)(2,1)S(1)}, u32[]{:S(2)}, u32[]{:S(2)}) collective-permute-start(bf16[2,128,1024]{2,1,0:T(8,128)(2,1)} %get-tuple-element.196.refs_0_), channel_id=1, source_target_pairs={{16,0},{24,8},{0,16},{8,24},{17,1},{25,9},{1,17},{9,25},{18,2},{26... | collective-permute-start | bytes 1572872 | tf_op jit(solution)/shard_map/ppermute | solution.py:969
  488.5 30.4 %collective-permute-start.58 = (bf16[1,128,1024]{2,1,0:T(8,128)(2,1)S(1)}, bf16[1,128,1024]{2,1,0:T(8,128)(2,1)S(1)}, u32[]{:S(2)}, u32[]{:S(2)}) collective-permute-start(bf16[1,128,1024]{2,1,0:T(8,128)(2,1)S(1)} %copy-done.109), channel_id=1, source_target_pairs={{4,0},{5,1},{6,2},{7,3},{0,4},{1,5},{2,6},{3,7},{12,8},{13,9},{14,... | collective-permute-start | bytes 786440 | tf_op jit(solution)/shard_map/ppermute | solution.py:966
  488.6 45.4 %collective-permute-start.56 = (bf16[1,128,1024]{2,1,0:T(8,128)(2,1)}, bf16[1,128,1024]{2,1,0:T(8,128)(2,1)S(1)}, u32[]{:S(2)}, u32[]{:S(2)}) collective-permute-start(bf16[1,128,1024]{2,1,0:T(8,128)(2,1)} %get-tuple-element.203), channel_id=1, source_target_pairs={{2,0},{3,1},{4,2},{5,3},{6,4},{7,5},{0,6},{1,7},{10,8},{11,9},{12,... | collective-permute-start | bytes 786440 | tf_op jit(solution)/shard_map/ppermute | solution.py:966
  500.7 31.1 %collective-permute-start.57 = (bf16[1,128,1024]{2,1,0:T(8,128)(2,1)}, bf16[1,128,1024]{2,1,0:T(8,128)(2,1)S(1)}, u32[]{:S(2)}, u32[]{:S(2)}) collective-permute-start(bf16[1,128,1024]{2,1,0:T(8,128)(2,1)} %get-tuple-element.204), channel_id=1, source_target_pairs={{4,0},{5,1},{6,2},{7,3},{0,4},{1,5},{2,6},{3,7},{12,8},{13,9},{14,... | collective-permute-start | bytes 786440 | tf_op jit(solution)/shard_map/ppermute | solution.py:966
  500.8 33.3 %collective-permute-start.55 = (bf16[1,128,1024]{2,1,0:T(8,128)(2,1)}, bf16[1,128,1024]{2,1,0:T(8,128)(2,1)S(1)}, u32[]{:S(2)}, u32[]{:S(2)}) collective-permute-start(bf16[1,128,1024]{2,1,0:T(8,128)(2,1)} %get-tuple-element.202), channel_id=1, source_target_pairs={{2,0},{3,1},{4,2},{5,3},{6,4},{7,5},{0,6},{1,7},{10,8},{11,9},{12,... | collective-permute-start | bytes 786440 | tf_op jit(solution)/shard_map/ppermute | solution.py:966
  516.7 52.9 %collective-permute-start.50 = (bf16[512,1024]{1,0:T(8,128)(2,1)S(1)}, bf16[512,1024]{1,0:T(8,128)(2,1)S(1)}, u32[]{:S(2)}, u32[]{:S(2)}) collective-permute-start(bf16[512,1024]{1,0:T(8,128)(2,1)S(1)} %constant_dynamic-update-slice_fusion.mine_ref), channel_id=1, source_target_pairs={{0,1},{1,0},{2,3},{3,2},{4,5},{5,4},{6,7},{7,6},{8,9},{9,8},{10,11... | collective-permute-start | bytes 3145736 | tf_op jit(solution)/shard_map/ppermute | solution.py:958
  547.1 31.5 %collective-permute-start.61 = (bf16[2,128,1024]{2,1,0:T(8,128)(2,1)}, bf16[2,128,1024]{2,1,0:T(8,128)(2,1)S(1)}, u32[]{:S(2)}, u32[]{:S(2)}) collective-permute-start(bf16[2,128,1024]{2,1,0:T(8,128)(2,1)} %get-tuple-element.209), channel_id=1, source_target_pairs={{16,0},{24,8},{0,16},{8,24},{17,1},{25,9},{1,17},{9,25},{18,2},{26... | collective-permute-start | bytes 1572872 | tf_op jit(solution)/shard_map/ppermute | solution.py:969
  569.5 122.6 %collective-permute-start.84 = (bf16[512,1024]{1,0:T(8,128)(2,1)}, bf16[512,1024]{1,0:T(8,128)(2,1)}, u32[]{:S(2)}, u32[]{:S(2)}) collective-permute-start(bf16[512,1024]{1,0:T(8,128)(2,1)} %constant_dynamic-update-slice_fusion.4.mine_ref), channel_id=1, source_target_pairs={{0,1},{1,0},{2,3},{3,2},{4,5},{5,4},{6,7},{7,6},{8,9},{9,8},{10,11... | collective-permute-start | bytes 3145736 | tf_op jit(solution)/shard_map/ppermute | solution.py:958
  686.8 30.8 %collective-permute-start.77 = (f32[2,3,1024]{2,1,0:T(4,128)S(1)}, f32[2,3,1024]{2,1,0:T(4,128)S(1)}, u32[]{:S(2)}, u32[]{:S(2)}) collective-permute-start(f32[2,3,1024]{2,1,0:T(4,128)S(1)} %add.171), channel_id=1, source_target_pairs={{16,0},{24,8},{0,16},{8,24},{17,1},{25,9},{1,17},{9,25},{18,2},{26... | collective-permute-start | bytes 73736 | tf_op jit(solution)/shard_map/ppermute | solution.py:969
  688.4 39.5 %collective-permute-start.89 = (bf16[2,128,1024]{2,1,0:T(8,128)(2,1)S(1)}, bf16[2,128,1024]{2,1,0:T(8,128)(2,1)S(1)}, u32[]{:S(2)}, u32[]{:S(2)}) collective-permute-start(bf16[2,128,1024]{2,1,0:T(8,128)(2,1)S(1)} %pad_maximum_fusion.7), channel_id=1, source_target_pairs={{8,0},{0,8},{24,16},{16,24},{9,1},{1,9},{25,17},{17,25},{10,2},{2,... | collective-permute-start | bytes 1572872 | tf_op jit(solution)/shard_map/ppermute | solution.py:969
  (177 other events, 1802.3 us)

commit v3 on v2

--- a/solution.py
+++ b/solution.py
@@ -1058,8 +1058,8 @@
     state["shards"], state["quarters"], wide_moments, square_moments = prepare()
     state["other_shards"] = swap(state["shards"])
     run_phase(state, 0, [state["shards"]])
-    run_phase(state, 1, [state["other_shards"]])
-    run_phase(state, 2, [])
+    run_phase(state, 1, [])
+    run_phase(state, 2, [state["other_shards"]])
     self_full = placed_blocks(place_now, shares_of(state, 0), 0, chips, [])
 
     def first_sums(kinds, others, *waited):
@@ -1121,8 +1121,8 @@
         ([third_low] * reps, grad_pre, rows, False),
         (hidden, [grad_branch] * reps, sub, False),
     ]
-    wide_other = weight_rows(place_now, wide_kinds)
-    wide_stage = first_sums(wide_kinds, wide_other)
+    in_other = weight_rows(place_now, wide_kinds[:1])[0]
+    out_other = weight_rows(place_now, wide_kinds[1:], None, [in_other])[0]
     grad_norm, third_gain, third_bias = normalize_back(
         grad_third, third_unit, third_inv, gain_rows[2]
     )
@@ -1130,15 +1130,16 @@
     cross_branch = grad_cross.astype(jnp.bfloat16)
     grad_mixed = matmul_right_t(cross_branch, cross_full[3]).astype(jnp.bfloat16)
     grad_cq, grad_ck, grad_cv = attend_backward(
-        cross_query, cross_keys, cross_values, enc_len, False, grad_mixed, wide_stage[0]
-    )
+        cross_query, cross_keys, cross_values, enc_len, False, grad_mixed
+    )
+    wide_stage = first_sums(wide_kinds, [in_other, out_other], grad_cq)
     cross_kind = (
         [second_low, encoded, encoded, cross_mixed],
         [grad_cq, grad_ck, grad_cv, cross_branch],
         rows,
         True,
     )
-    cross_other = weight_rows(place_now, [cross_kind])[0]
+    cross_other = weight_rows(place_now, [cross_kind], None, [wide_stage[0]])[0]
     grad_self, self_branch, grad_mixed, second_gain, second_bias = branch_back(
         grad_cq,
         cross_full[0],
@@ -1164,6 +1165,7 @@
     wide_stage = third_sums(wide_stage, self_other)
     cross_stage, cross_token = second_sums(cross_stage, wide_stage[0])
     self_stage = first_sums([self_kind], [self_other], cross_token)
+    first_sums_done = self_stage[0]
     cross_stage = third_sums(cross_stage, self_stage[0])
     self_stage, self_token = second_sums(self_stage, cross_stage[0])
     wide_fresh = fresh_blocks(place_now, *wide_stage, wide_moments, self_token)
@@ -1205,24 +1207,24 @@
         jnp.concatenate([self_stage[0], cross_stage[0]]),
         [jnp.concatenate(pair) for pair in zip(self_stage[1], cross_stage[1])],
         square_moments,
+        gram_token,
     )
     square_grads = square_fresh[0]
     square_own = owned(square_fresh)
-    wide_grads_shared = share_pair(wide_grads)
-    square_grads_shared = share_pair(square_grads)
-    wide_rows = gram_schulz(
-        place_now, quarters, *wide_own, rows, wide_grads_shared[1]
-    )
-    wide_orth_shared = share_pair(to_both(wide_rows))
-    square_rows = square_schulz(
-        *square_own, rows, wide_rows, square_grads_shared[1], wide_grads_shared[3]
-    )
+    grads = jnp.concatenate([wide_grads, square_grads])
+    grads_x, grads_y = from_rep(grads, 1), from_rep(grads, 2)
+    wide_rows = gram_schulz(place_now, quarters, *wide_own, rows, square_grads)
+    wide_orth = to_both(wide_rows)
+    wide_orth_shared = share_pair(wide_orth)
+    square_rows = square_schulz(*square_own, rows, wide_orth, grads_x, grads_y)
+    grads_across = [from_rep(grads_y[:2], 1), from_rep(grads_x[2:], 2)]
     square_orth = held_until(
-        to_both(square_rows), wide_orth_shared[3], square_grads_shared[3]
+        to_both(square_rows), wide_orth_shared[1], wide_orth_shared[2], *grads_across
     )
     square_orth_shared = share_pair(square_orth)
-    late_sq = held_until(grad_sq, gram_token)
-    late_ck = held_until(grad_ck, gram_token)
+
+    late_sq = held_until(grad_sq, first_sums_done)
+    late_ck = held_until(grad_ck, first_sums_done)
     grad_states = matmul_right_t(late_ck, cross_full[1]) + matmul_right_t(grad_cv, cross_full[2])
     grad_first = (
         matmul_right_t(late_sq, self_full[0])
@@ -1239,7 +1241,7 @@
             jnp.stack([first_bias, second_bias, third_bias]),
         ]
     )
-    norm_local = held_until(norm_local, quarters[-1])
+    norm_local = held_until(norm_local, square_orth)
     norm_total = norm_local + swap(norm_local)
     norm_total = norm_total + from_rep(norm_total, 1)
     norm_total = norm_total + from_rep(norm_total, 2)
@@ -1247,7 +1249,10 @@
     width_part = norm_moment.shape[2]
     norm_grad = lax.dynamic_slice_in_dim(norm_total, my_place * width_part, width_part, 2)
 
-    wide_grads_shared[0] = held_until(wide_grads_shared[0], wide_rows)
+    late_grads = held_until(grads, square_orth)
+    wide_grads_shared = [late_grads[:2], grads_x[:2], grads_y[:2], grads_across[0]]
+    square_grads_shared = [late_grads[2:], grads_x[2:], grads_y[2:], grads_across[1]]
+    wide_orth_shared[0] = held_until(wide_orth_shared[0], square_orth)
     in_shared, out_shared = to_replicas(wide_grads_shared)
     self_shared, cross_shared = to_replicas(square_grads_shared)
     in_orth_shared, out_orth_shared = to_replicas(wide_orth_shared)

time: 779 us -> 798 us (1.024)
  waiting for transfers between devices: 286 us -> 304 us
    ppermute x32, waiting for transfers between devices: 140 us -> 159 us  [from_chip(): return lax.ppermute(values, 'shard', pairs)]
    ppermute x15, waiting for transfers between devices: 12.4 us -> 4.43 us  [swap(): lax.ppermute(values, 'shard', [(index, index ^ 1) for index in range(shar...]
    ppermute x48 -> x44, waiting for transfers between devices: 133 us -> 141 us  [from_rep(): lax.ppermute(values, 'rep', [(index ^ step, index) for index in range(rep...]
    ppermute x48 -> x44, starting transfers between devices: 53.6 us -> 47.2 us  [from_rep(): lax.ppermute(values, 'rep', [(index ^ step, index) for index in range(rep...]
    unnamed x245 -> x276, local copies, waits for them, and re-layouts: 27.5 us -> 33.3 us
    pallas_call x6 -> x7, Pallas kernels: 43.6 us -> 47 us  [weight_rows(): pl.pallas_call(kernel, out_shape=tuple(out_shapes), in_specs=[pl.BlockSpe...]
  transfers between devices with their start and end apart: 95 -> 91, of which waited for: 45 -> 46; matrix products, arithmetic and copies ran while one was open for 13% -> 12% of each run, Pallas kernels for 21% -> 17%
where the time goes in v3:
time: 798 us; the launch traced here: 793 us
  waiting for transfers between devices  304 us (38%)
  Pallas kernels  259 us (32%)
  starting transfers between devices  95.4 us (12%)
  local copies, waits for them, and re-layouts  52.7 us (7%)
  other arithmetic  46 us (6%)
  matrix products  32.5 us (4%)
    ppermute x32, waiting for transfers between devices, from_chip(): return lax.ppermute(values, 'shard', pairs)  159 us
    ppermute x44, waiting for transfers between devices, from_rep(): lax.ppermute(values, 'rep', [(index ^ step, index) for index in range(rep...  141 us
    ppermute x44, starting transfers between devices, from_rep(): lax.ppermute(values, 'rep', [(index ^ step, index) for index in range(rep...  47.2 us
    pallas_call x7, Pallas kernels, weight_rows(): pl.pallas_call(kernel, out_shape=tuple(out_shapes), in_specs=[pl.BlockSpe...  47 us
    pallas_call x4, Pallas kernels, attention_call(): pl.pallas_call(kernel, out_shape=tuple(out_shapes), in_specs=[pl.BlockSpe...  47 us
    ppermute x32, starting transfers between devices, from_chip(): return lax.ppermute(values, 'shard', pairs)  46.3 us
    pallas_call x1, Pallas kernels, gram_schulz(): pl.pallas_call(kernel, out_shape=low(2, rows, size), in_specs=[pl.BlockSp...  33.7 us
    unnamed x276, local copies, waits for them, and re-layouts  33.3 us
  transfers between devices with their start and end apart: 91, of which 46 were waited for; matrix products, arithmetic and copies ran while one was open for 12% of the time, Pallas kernels for 17%

profile of v3, /device:TPU:0, one launch (start us, length us, event | category | flops | bytes accessed | tf_op | source)
XLA Modules:
  0.0 793.2 jit_solution(16310567654442862863)
XLA Ops:
  1.2 7.9 %shard_map.318 = (bf16[4,4,128,1024]{3,2,1,0:T(8,128)(2,1)}, bf16[128,1024]{1,0:T(8,128)(2,1)}, bf16[128,1024]{1,0:T(8,128)(2,1)}, bf16[128,1024]{1,0:T(8,128)(2...) custom-call(s32[4]{0:T(128)} %pad_add_fusion.place_ref, f32[4,128,1024]{2,1,0:T(8,128)} %refs_0_.1, ...), custom_call_target="tpu_custom_call" | custom-call | flops 1024 | bytes 1024 | tf_op jit(solution)/shard_map/pallas_call | solution.py:871
  22.2 16.3 %collective-permute-done.1.refs_1_ = bf16[128,1024]{1,0:T(8,128)(2,1)S(1)} collective-permute-done((bf16[128,1024]{1,0:T(8,128)(2,1)S(1)}, bf16[128,1024]{1,0:T(8,128)(2,1)S(1)}, u32[]{:S(2)}, u32[]{:S(2)}) %collective-permute-start.1) | collective-permute-done | bytes 262176 | tf_op jit(solution)/shard_map/ppermute | solution.py:966
  52.4 12.0 %collective-permute-done.6.refs_1_ = bf16[128,1024]{1,0:T(8,128)(2,1)S(1)} collective-permute-done((bf16[128,1024]{1,0:T(8,128)(2,1)}, bf16[128,1024]{1,0:T(8,128)(2,1)S(1)}, u32[]{:S(2)}, u32[]{:S(2)}) %collective-permute-start.6) | collective-permute-done | bytes 262176 | tf_op jit(solution)/shard_map/ppermute | solution.py:966
  64.4 10.2 %collective-permute-done.7.refs_2_ = bf16[128,1024]{1,0:T(8,128)(2,1)S(1)} collective-permute-done((bf16[128,1024]{1,0:T(8,128)(2,1)}, bf16[128,1024]{1,0:T(8,128)(2,1)S(1)}, u32[]{:S(2)}, u32[]{:S(2)}) %collective-permute-start.7) | collective-permute-done | bytes 262176 | tf_op jit(solution)/shard_map/ppermute | solution.py:966
  84.3 7.8 collective-permute-done.13.refs_0_
  92.1 13.8 %collective-permute-done.14.refs_1_ = bf16[128,1024]{1,0:T(8,128)(2,1)S(1)} collective-permute-done((bf16[128,1024]{1,0:T(8,128)(2,1)}, bf16[128,1024]{1,0:T(8,128)(2,1)S(1)}, u32[]{:S(2)}, u32[]{:S(2)}) %collective-permute-start.14) | collective-permute-done | bytes 262176 | tf_op jit(solution)/shard_map/ppermute | solution.py:966
  105.8 10.2 %collective-permute-done.15.refs_2_ = bf16[128,1024]{1,0:T(8,128)(2,1)S(1)} collective-permute-done((bf16[128,1024]{1,0:T(8,128)(2,1)}, bf16[128,1024]{1,0:T(8,128)(2,1)S(1)}, u32[]{:S(2)}, u32[]{:S(2)}) %collective-permute-start.15) | collective-permute-done | bytes 262176 | tf_op jit(solution)/shard_map/ppermute | solution.py:966
  130.3 7.7 shard_map.324
  161.0 9.5 %shard_map.325.refs_1_ = bf16[256,1024]{1,0:T(8,128)(2,1)} custom-call(s32[1]{0:T(128)S(6)} %copy.87.count_ref, bf16[256,1024]{1,0:T(8,128)(2,1)} %convolution_convert_fusion.6.query_ref.refs_5_, bf16[256,1024]{1,0:T(8,128)(2,1)} %convolution_convert_fusion.5.key_ref.refs_6_, bf16[256,1024]{1,0:T(8,128)(2,1)} %convolution_convert_fusion.4.value_ref.refs_7_), custom_call_target="tpu_custom_call" | custom-call | flops 1024 | bytes 1024 | tf_op jit(solution)/shard_map/pallas_call | solution.py:86
  174.9 7.7 shard_map.328
  198.4 10.4 %shard_map.329.refs_2_ = bf16[256,1024]{1,0:T(8,128)(2,1)} custom-call(s32[1]{0:T(128)S(6)} %copy.88.count_ref, bf16[256,1024]{1,0:T(8,128)(2,1)} %convolution_convert_fusion.3.query_ref, bf16[384,1024]{1,0:T(8,128)(2,1)} %fusion.3.key_ref.refs_2_, bf16[384,1024]{1,0:T(8,128)(2,1)} %fusion.4.value_ref.refs_3_), custom_call_target="tpu_custom_call" | custom-call | flops 1024 | bytes 1024 | tf_op jit(solution)/shard_map/pallas_call | solution.py:86
  215.6 17.7 %shard_map.331 = (f32[256,1024]{1,0:T(8,128)}, f32[256,1024]{1,0:T(8,128)}, bf16[256,1024]{1,0:T(8,128)(2,1)}, bf16[256,1024]{1,0:T(8,128)(2,1)}, bf16[256,1024]...) custom-call(s32[4]{0:T(128)} %pad_add_fusion.place_ref, ...), custom_call_target="tpu_custom_call" | custom-call | flops 1024 | bytes 1024 | tf_op jit(solution)/shard_map/pallas_call | solution.py:810
  248.5 14.2 %shard_map.332 = (bf16[256,1024]{1,0:T(8,128)(2,1)}, bf16[384,1024]{1,0:T(8,128)(2,1)}, bf16[384,1024]{1,0:T(8,128)(2,1)}) custom-call(s32[1]{0:T(128)S(6)} %copy.88.count_ref, bf16[256,1024]{1,0:T(8,128)(2,1)} %convolution_convert_fusion.3.query_ref, bf16[384,1024]{1,0:T(8,128)(2,1)} %fusion.3.key_ref.refs_2_, bf16[384,1024]{1,0:T(8,128)(2,1)} %fusion.4.value_ref.refs_3_, ...), custom_call_target="tpu_custom_call" | custom-call | flops 1024 | bytes 1024 | tf_op jit(solution)/shard_map/pallas_call | solution.py:86
  262.8 10.5 %shard_map.335 = (bf16[2,2,256,1024]{3,2,1,0:T(8,128)(2,1)}, bf16[2,2,256,1024]{3,2,1,0:T(8,128)(2,1)}, bf16[2,2,256,1024]{3,2,1,0:T(8,128)(2,1)}, bf16[2,2,256,1024]{3,2,1,0:T(8,128)(2,1)}) custom-call(s32[4]{0:T(128)} %pad_add_fusion.place_ref, bf16[256,1024]{1,0:T(8,128)(2,1)} %add_convert_fusion.1.third_ref.refs_0_, ...), custom_call_target="tpu_custom_call" | custom-call | flops 1024 | bytes 1024 | tf_op jit(solution)/shard_map/pallas_call | solution.py:502
  273.3 6.3 shard_map.336.refs_0_
  287.9 12.8 %shard_map.338 = (bf16[256,1024]{1,0:T(8,128)(2,1)}, bf16[256,1024]{1,0:T(8,128)(2,1)}, bf16[256,1024]{1,0:T(8,128)(2,1)}) custom-call(s32[1]{0:T(128)S(6)} %copy.87.count_ref, bf16[256,1024]{1,0:T(8,128)(2,1)} %convolution_convert_fusion.6.query_ref.refs_5_, bf16[256,1024]{1,0:T(8,128)(2,1)} %convolution_convert_fusion.5.key_ref.refs_6_, ...), custom_call_target="tpu_custom_call" | custom-call | flops 1024 | bytes 1024 | tf_op jit(solution)/shard_map/pallas_call | solution.py:86
  300.7 27.1 %collective-permute-done.33.x_ref = bf16[2,2,256,1024]{3,2,1,0:T(8,128)(2,1)S(1)} collective-permute-done((bf16[2,2,256,1024]{3,2,1,0:T(8,128)(2,1)}, bf16[2,2,256,1024]{3,2,1,0:T(8,128)(2,1)S(1)}, u32[]{:S(2)}, u32[]{:S(2)}) %collective-permute-start.33) | collective-permute-done | bytes 2097184 | tf_op jit(solution)/shard_map/ppermute | solution.py:969
  334.4 7.5 shard_map.340
  351.4 21.9 %collective-permute-done.38.last_x_ref = bf16[2,256,1024]{2,1,0:T(8,128)(2,1)S(1)} collective-permute-done((bf16[2,256,1024]{2,1,0:T(8,128)(2,1)S(1)}, bf16[2,256,1024]{2,1,0:T(8,128)(2,1)S(1)}, u32[]{:S(2)}, u32[]{:S(2)}) %collective-permute-start.38) | collective-permute-done | bytes 1048608 | tf_op jit(solution)/shard_map/ppermute | solution.py:969
  380.8 14.4 %collective-permute-done.36.x_ref = bf16[1,2,256,1024]{3,2,1,0:T(8,128)(2,1)S(1)} collective-permute-done((bf16[1,2,256,1024]{3,2,1,0:T(8,128)(2,1)}, bf16[1,2,256,1024]{3,2,1,0:T(8,128)(2,1)S(1)}, u32[]{:S(2)}, u32[]{:S(2)}) %collective-permute-start.36) | collective-permute-done | bytes 1048608 | tf_op jit(solution)/shard_map/ppermute | solution.py:969
  402.1 6.7 shard_map.344
  412.9 31.8 %collective-permute-done.45.last_x_ref = bf16[1,256,1024]{2,1,0:T(8,128)(2,1)S(1)} collective-permute-done((bf16[1,256,1024]{2,1,0:T(8,128)(2,1)S(1)}, bf16[1,256,1024]{2,1,0:T(8,128)(2,1)S(1)}, u32[]{:S(2)}, u32[]{:S(2)}) %collective-permute-start.45) | collective-permute-done | bytes 524320 | tf_op jit(solution)/shard_map/ppermute | solution.py:969
  454.4 24.0 %collective-permute-done.41.refs_1_ = bf16[2,128,1024]{2,1,0:T(8,128)(2,1)S(1)} collective-permute-done((bf16[2,128,1024]{2,1,0:T(8,128)(2,1)}, bf16[2,128,1024]{2,1,0:T(8,128)(2,1)S(1)}, u32[]{:S(2)}, u32[]{:S(2)}) %collective-permute-start.41) | collective-permute-done | bytes 524320 | tf_op jit(solution)/shard_map/ppermute | solution.py:966
  493.0 13.2 %collective-permute-done.56 = bf16[128,1024]{1,0:T(8,128)(2,1)S(1)} collective-permute-done((bf16[128,1024]{1,0:T(8,128)(2,1)}, bf16[128,1024]{1,0:T(8,128)(2,1)S(1)}, u32[]{:S(2)}, u32[]{:S(2)}) %collective-permute-start.56) | collective-permute-done | bytes 262176 | tf_op jit(solution)/shard_map/ppermute | solution.py:966
  514.5 10.2 %collective-permute-done.47.last_x_ref = bf16[1,256,1024]{2,1,0:T(8,128)(2,1)S(1)} collective-permute-done((bf16[1,256,1024]{2,1,0:T(8,128)(2,1)S(1)}, bf16[1,256,1024]{2,1,0:T(8,128)(2,1)S(1)}, u32[]{:S(2)}, u32[]{:S(2)}) %collective-permute-start.47) | collective-permute-done | bytes 524320 | tf_op jit(solution)/shard_map/ppermute | solution.py:969
  562.3 19.9 %collective-permute-start.51 = (bf16[1,128,1024]{2,1,0:T(8,128)(2,1)S(1)}, bf16[1,128,1024]{2,1,0:T(8,128)(2,1)S(1)}, u32[]{:S(2)}, u32[]{:S(2)}) collective-permute-start(bf16[1,128,1024]{2,1,0:T(8,128)(2,1)S(1)} %copy-done.128), channel_id=1, source_target_pairs={{4,0},{5,1},{6,2},{7,3},{0,4},{1,5},{2,6},{3,7},{12,8},{13,9},{14,... | collective-permute-start | bytes 786440 | tf_op jit(solution)/shard_map/ppermute | solution.py:966
  605.0 10.4 %collective-permute-done.65 = bf16[128,1024]{1,0:T(8,128)(2,1)S(1)} collective-permute-done((bf16[128,1024]{1,0:T(8,128)(2,1)}, bf16[128,1024]{1,0:T(8,128)(2,1)S(1)}, u32[]{:S(2)}, u32[]{:S(2)}) %collective-permute-start.65) | collective-permute-done | bytes 262176 | tf_op jit(solution)/shard_map/ppermute | solution.py:966
  616.2 7.8 collective-permute-done.72.a_ref
  625.4 33.7 %shard_map.354 = bf16[2,128,1024]{2,1,0:T(8,128)(2,1)} custom-call(s32[4]{0:T(128)} %pad_add_fusion.place_ref, bf16[256,1024]{1,0:T(8,128)(2,1)} %copy-done.74, bf16[256,1024]{1,0:T(8,128)(2,1)} %copy-done.79, bf16[256,1024]{1,0:T(8,128)(2,1)} %copy-done.78, bf16[128,1024]{1,0:T(8,128)(2,1)} %copy-done.114, bf16[128,1024]{1,0:T(8,128)(2,1)} %copy-done.115, ...), custom_call_target="tpu_custom_call" | custom-call | flops 1024 | bytes 1024 | tf_op jit(solution)/shard_map/pallas_call | solution.py:380
  661.7 8.5 %collective-permute-done.74 = bf16[128,1024]{1,0:T(8,128)(2,1)S(1)} collective-permute-done((bf16[128,1024]{1,0:T(8,128)(2,1)S(1)}, bf16[128,1024]{1,0:T(8,128)(2,1)S(1)}, u32[]{:S(2)}, u32[]{:S(2)}) %collective-permute-start.74) | collective-permute-done | bytes 262176 | tf_op jit(solution)/shard_map/ppermute | solution.py:966
  673.4 25.5 %shard_map.355 = bf16[2,128,1024]{2,1,0:T(8,128)(2,1)} custom-call(bf16[512,1024]{1,0:T(8,128)(2,1)} %copy-done.75, bf16[512,1024]{1,0:T(8,128)(2,1)} %collective-permute-done.67.sibling_ref, bf16[2,128,1024]{2,1,0:T(8,128)(2,1)} %pad_maximum_fusion.5.refs_0_, bf16[4,128,1024]{2,1,0:T(8,128)(2,1)} %copy-done.11, bf16[4,128,1024]{2,1,0:T(8,128)(2,1)} %copy-done.13), custom_call_target="tpu_custom_call" | custom-call | flops 1024 | bytes 1024 | tf_op jit(solution)/shard_map/pallas_call | solution.py:233
  714.9 9.4 %collective-permute-done.76.refs_1_ = bf16[2,128,1024]{2,1,0:T(8,128)(2,1)S(1)} collective-permute-done((bf16[2,128,1024]{2,1,0:T(8,128)(2,1)S(1)}, bf16[2,128,1024]{2,1,0:T(8,128)(2,1)S(1)}, u32[]{:S(2)}, u32[]{:S(2)}) %collective-permute-start.76) | collective-permute-done | bytes 524320 | tf_op jit(solution)/shard_map/ppermute | solution.py:969
  (558 shorter events, 342.7 us)
Async XLA Ops:
  9.2 106.9 %collective-permute-start.11 = (bf16[4,4,128,1024]{3,2,1,0:T(8,128)(2,1)}, bf16[4,4,128,1024]{3,2,1,0:T(8,128)(2,1)}, u32[]{:S(2)}, u32[]{:S(2)}) collective-permute-start(bf16[4,4,128,1024]{3,2,1,0:T(8,128)(2,1)} %get-tuple-element.118.refs_3_.refs_0_.refs_12_), channel_id=1, source_target_pairs={{0,1},{1,0},{2,3},{3,2},{4,5},{5,4},{6,7},{7,6},{8,9},{9,8},{10,11... | collective-permute-start | bytes 12582920 | tf_op jit(solution)/shard_map/ppermute | solution.py:958
  42.5 32.1 %collective-permute-start.8 = (bf16[384,1024]{1,0:T(8,128)(2,1)}, bf16[384,1024]{1,0:T(8,128)(2,1)S(1)}, u32[]{:S(2)}, u32[]{:S(2)}) collective-permute-start(bf16[384,1024]{1,0:T(8,128)(2,1)} %get-tuple-element.122.refs_1_), channel_id=1, source_target_pairs={{0,1},{1,0},{2,3},{3,2},{4,5},{5,4},{6,7},{7,6},{8,9},{9,8},{10,11... | collective-permute-start | bytes 2359304 | tf_op jit(solution)/shard_map/ppermute | solution.py:958
  42.5 32.1 %collective-permute-start.3 = (bf16[384,1024]{1,0:T(8,128)(2,1)}, bf16[384,1024]{1,0:T(8,128)(2,1)S(1)}, u32[]{:S(2)}, u32[]{:S(2)}) collective-permute-start(bf16[384,1024]{1,0:T(8,128)(2,1)} %get-tuple-element.119.refs_1_), channel_id=1, source_target_pairs={{8,0},{0,8},{24,16},{16,24},{9,1},{1,9},{25,17},{17,25},{10,2},{2,... | collective-permute-start | bytes 2359304 | tf_op jit(solution)/shard_map/ppermute | solution.py:969
  44.0 30.6 %collective-permute-start.4 = (bf16[384,1024]{1,0:T(8,128)(2,1)}, bf16[384,1024]{1,0:T(8,128)(2,1)S(1)}, u32[]{:S(2)}, u32[]{:S(2)}) collective-permute-start(bf16[384,1024]{1,0:T(8,128)(2,1)} %get-tuple-element.120), channel_id=1, source_target_pairs={{16,0},{24,8},{0,16},{8,24},{17,1},{25,9},{1,17},{9,25},{18,2},{26... | collective-permute-start | bytes 2359304 | tf_op jit(solution)/shard_map/ppermute | solution.py:969
  80.7 35.4 %collective-permute-start.12 = (bf16[1152,1024]{1,0:T(8,128)(2,1)}, bf16[1152,1024]{1,0:T(8,128)(2,1)S(1)}, u32[]{:S(2)}, u32[]{:S(2)}) collective-permute-start(bf16[1152,1024]{1,0:T(8,128)(2,1)} %get-tuple-element.125.refs_1_), channel_id=1, source_target_pairs={{0,1},{1,0},{2,3},{3,2},{4,5},{5,4},{6,7},{7,6},{8,9},{9,8},{10,11... | collective-permute-start | bytes 7077896 | tf_op jit(solution)/shard_map/ppermute | solution.py:958
  80.7 35.4 %collective-permute-start.10 = (bf16[576,1024]{1,0:T(8,128)(2,1)}, bf16[576,1024]{1,0:T(8,128)(2,1)S(1)}, u32[]{:S(2)}, u32[]{:S(2)}) collective-permute-start(bf16[576,1024]{1,0:T(8,128)(2,1)} %get-tuple-element.124), channel_id=1, source_target_pairs={{16,0},{24,8},{0,16},{8,24},{17,1},{25,9},{1,17},{9,25},{18,2},{26... | collective-permute-start | bytes 3538952 | tf_op jit(solution)/shard_map/ppermute | solution.py:969
  82.2 33.9 %collective-permute-start.9 = (bf16[576,1024]{1,0:T(8,128)(2,1)}, bf16[576,1024]{1,0:T(8,128)(2,1)S(1)}, u32[]{:S(2)}, u32[]{:S(2)}) collective-permute-start(bf16[576,1024]{1,0:T(8,128)(2,1)} %get-tuple-element.123.refs_1_), channel_id=1, source_target_pairs={{8,0},{0,8},{24,16},{16,24},{9,1},{1,9},{25,17},{17,25},{10,2},{2,... | collective-permute-start | bytes 3538952 | tf_op jit(solution)/shard_map/ppermute | solution.py:969
  123.2 28.7 %collective-permute-start.17 = (bf16[576,1024]{1,0:T(8,128)(2,1)}, bf16[576,1024]{1,0:T(8,128)(2,1)S(1)}, u32[]{:S(2)}, u32[]{:S(2)}) collective-permute-start(bf16[576,1024]{1,0:T(8,128)(2,1)} %get-tuple-element.132.refs_1_), channel_id=1, source_target_pairs={{8,0},{0,8},{24,16},{16,24},{9,1},{1,9},{25,17},{17,25},{10,2},{2,... | collective-permute-start | bytes 3538952 | tf_op jit(solution)/shard_map/ppermute | solution.py:969
  123.8 28.3 %collective-permute-start.18 = (bf16[576,1024]{1,0:T(8,128)(2,1)}, bf16[576,1024]{1,0:T(8,128)(2,1)S(1)}, u32[]{:S(2)}, u32[]{:S(2)}) collective-permute-start(bf16[576,1024]{1,0:T(8,128)(2,1)} %get-tuple-element.133), channel_id=1, source_target_pairs={{16,0},{24,8},{0,16},{8,24},{17,1},{25,9},{1,17},{9,25},{18,2},{26... | collective-permute-start | bytes 3538952 | tf_op jit(solution)/shard_map/ppermute | solution.py:969
  158.5 29.8 %collective-permute-start.23 = (bf16[576,1024]{1,0:T(8,128)(2,1)}, bf16[576,1024]{1,0:T(8,128)(2,1)S(1)}, u32[]{:S(2)}, u32[]{:S(2)}) collective-permute-start(bf16[576,1024]{1,0:T(8,128)(2,1)} %get-tuple-element.140.refs_13_), channel_id=1, source_target_pairs={{8,0},{0,8},{24,16},{16,24},{9,1},{1,9},{25,17},{17,25},{10,2},{2,... | collective-permute-start | bytes 3538952 | tf_op jit(solution)/shard_map/ppermute | solution.py:969
  159.2 29.0 %collective-permute-start.24 = (bf16[576,1024]{1,0:T(8,128)(2,1)}, bf16[576,1024]{1,0:T(8,128)(2,1)S(1)}, u32[]{:S(2)}, u32[]{:S(2)}) collective-permute-start(bf16[576,1024]{1,0:T(8,128)(2,1)} %get-tuple-element.141), channel_id=1, source_target_pairs={{16,0},{24,8},{0,16},{8,24},{17,1},{25,9},{1,17},{9,25},{18,2},{26... | collective-permute-start | bytes 3538952 | tf_op jit(solution)/shard_map/ppermute | solution.py:969
  279.6 54.8 %collective-permute-start.32 = (bf16[4,512,1024]{2,1,0:T(8,128)(2,1)}, bf16[4,512,1024]{2,1,0:T(8,128)(2,1)}, u32[]{:S(2)}, u32[]{:S(2)}) collective-permute-start(bf16[4,512,1024]{2,1,0:T(8,128)(2,1)} %shard_map.336.refs_0_), channel_id=1, source_target_pairs={{0,1},{1,0},{2,3},{3,2},{4,5},{5,4},{6,7},{7,6},{8,9},{9,8},{10,11... | collective-permute-start | bytes 12582920 | tf_op jit(solution)/shard_map/ppermute | solution.py:958
  279.7 48.1 %collective-permute-start.33 = (bf16[2,2,256,1024]{3,2,1,0:T(8,128)(2,1)}, bf16[2,2,256,1024]{3,2,1,0:T(8,128)(2,1)S(1)}, u32[]{:S(2)}, u32[]{:S(2)}) collective-permute-start(bf16[2,2,256,1024]{3,2,1,0:T(8,128)(2,1)} %get-tuple-element.166), channel_id=1, source_target_pairs={{8,0},{0,8},{24,16},{16,24},{9,1},{1,9},{25,17},{17,25},{10,2},{2,... | collective-permute-start | bytes 6291464 | tf_op jit(solution)/shard_map/ppermute | solution.py:969
  280.7 47.6 %collective-permute-start.34 = (bf16[2,2,256,1024]{3,2,1,0:T(8,128)(2,1)S(1)}, bf16[2,2,256,1024]{3,2,1,0:T(8,128)(2,1)S(1)}, u32[]{:S(2)}, u32[]{:S(2)}) collective-permute-start(bf16[2,2,256,1024]{3,2,1,0:T(8,128)(2,1)S(1)} %copy-done.121), channel_id=1, source_target_pairs={{16,0},{24,8},{0,16},{8,24},{17,1},{25,9},{1,17},{9,25},{18,2},{26... | collective-permute-start | bytes 6291464 | tf_op jit(solution)/shard_map/ppermute | solution.py:969
  347.2 52.8 %collective-permute-start.35 = (bf16[4,512,1024]{2,1,0:T(8,128)(2,1)}, bf16[4,512,1024]{2,1,0:T(8,128)(2,1)S(1)}, u32[]{:S(2)}, u32[]{:S(2)}) collective-permute-start(bf16[4,512,1024]{2,1,0:T(8,128)(2,1)} %shard_map.341.refs_0_), channel_id=1, source_target_pairs={{0,1},{1,0},{2,3},{3,2},{4,5},{5,4},{6,7},{7,6},{8,9},{9,8},{10,11... | collective-permute-start | bytes 12582920 | tf_op jit(solution)/shard_map/ppermute | solution.py:958
  348.7 46.5 %collective-permute-start.36 = (bf16[1,2,256,1024]{3,2,1,0:T(8,128)(2,1)}, bf16[1,2,256,1024]{3,2,1,0:T(8,128)(2,1)S(1)}, u32[]{:S(2)}, u32[]{:S(2)}) collective-permute-start(bf16[1,2,256,1024]{3,2,1,0:T(8,128)(2,1)} %get-tuple-element.171), channel_id=1, source_target_pairs={{8,0},{0,8},{24,16},{16,24},{9,1},{1,9},{25,17},{17,25},{10,2},{2,... | collective-permute-start | bytes 3145736 | tf_op jit(solution)/shard_map/ppermute | solution.py:969
  349.8 46.3 %collective-permute-start.37 = (bf16[1,2,256,1024]{3,2,1,0:T(8,128)(2,1)}, bf16[1,2,256,1024]{3,2,1,0:T(8,128)(2,1)S(1)}, u32[]{:S(2)}, u32[]{:S(2)}) collective-permute-start(bf16[1,2,256,1024]{3,2,1,0:T(8,128)(2,1)} %get-tuple-element.172), channel_id=1, source_target_pairs={{16,0},{24,8},{0,16},{8,24},{17,1},{25,9},{1,17},{9,25},{18,2},{26... | collective-permute-start | bytes 3145736 | tf_op jit(solution)/shard_map/ppermute | solution.py:969
  408.8 41.4 %collective-permute-start.43 = (bf16[1,2,256,1024]{3,2,1,0:T(8,128)(2,1)}, bf16[1,2,256,1024]{3,2,1,0:T(8,128)(2,1)S(1)}, u32[]{:S(2)}, u32[]{:S(2)}) collective-permute-start(bf16[1,2,256,1024]{3,2,1,0:T(8,128)(2,1)} %get-tuple-element.182), channel_id=1, source_target_pairs={{8,0},{0,8},{24,16},{16,24},{9,1},{1,9},{25,17},{17,25},{10,2},{2,... | collective-permute-start | bytes 3145736 | tf_op jit(solution)/shard_map/ppermute | solution.py:969
  409.9 40.3 %collective-permute-start.44 = (bf16[1,2,256,1024]{3,2,1,0:T(8,128)(2,1)}, bf16[1,2,256,1024]{3,2,1,0:T(8,128)(2,1)S(1)}, u32[]{:S(2)}, u32[]{:S(2)}) collective-permute-start(bf16[1,2,256,1024]{3,2,1,0:T(8,128)(2,1)} %get-tuple-element.183), channel_id=1, source_target_pairs={{16,0},{24,8},{0,16},{8,24},{17,1},{25,9},{1,17},{9,25},{18,2},{26... | collective-permute-start | bytes 3145736 | tf_op jit(solution)/shard_map/ppermute | solution.py:969
  410.4 34.2 %collective-permute-start.45 = (bf16[1,256,1024]{2,1,0:T(8,128)(2,1)S(1)}, bf16[1,256,1024]{2,1,0:T(8,128)(2,1)S(1)}, u32[]{:S(2)}, u32[]{:S(2)}) collective-permute-start(bf16[1,256,1024]{2,1,0:T(8,128)(2,1)S(1)} %copy-done.86), channel_id=1, source_target_pairs={{8,0},{0,8},{24,16},{16,24},{9,1},{1,9},{25,17},{17,25},{10,2},{2,... | collective-permute-start | bytes 1572872 | tf_op jit(solution)/shard_map/ppermute | solution.py:969
  411.3 34.1 %collective-permute-start.46 = (bf16[1,256,1024]{2,1,0:T(8,128)(2,1)}, bf16[1,256,1024]{2,1,0:T(8,128)(2,1)S(1)}, u32[]{:S(2)}, u32[]{:S(2)}) collective-permute-start(bf16[1,256,1024]{2,1,0:T(8,128)(2,1)} %get-tuple-element.184), channel_id=1, source_target_pairs={{16,0},{24,8},{0,16},{8,24},{17,1},{25,9},{1,17},{9,25},{18,2},{26... | collective-permute-start | bytes 1572872 | tf_op jit(solution)/shard_map/ppermute | solution.py:969
  412.9 41.5 %collective-permute-start.40 = (bf16[2,128,1024]{2,1,0:T(8,128)(2,1)}, bf16[2,128,1024]{2,1,0:T(8,128)(2,1)S(1)}, u32[]{:S(2)}, u32[]{:S(2)}) collective-permute-start(bf16[2,128,1024]{2,1,0:T(8,128)(2,1)} %get-tuple-element.177), channel_id=1, source_target_pairs={{2,0},{3,1},{4,2},{5,3},{6,4},{7,5},{0,6},{1,7},{10,8},{11,9},{12,... | collective-permute-start | bytes 1572872 | tf_op jit(solution)/shard_map/ppermute | solution.py:966
  444.7 33.7 %collective-permute-start.41 = (bf16[2,128,1024]{2,1,0:T(8,128)(2,1)}, bf16[2,128,1024]{2,1,0:T(8,128)(2,1)S(1)}, u32[]{:S(2)}, u32[]{:S(2)}) collective-permute-start(bf16[2,128,1024]{2,1,0:T(8,128)(2,1)} %get-tuple-element.178), channel_id=1, source_target_pairs={{4,0},{5,1},{6,2},{7,3},{0,4},{1,5},{2,6},{3,7},{12,8},{13,9},{14,... | collective-permute-start | bytes 1572872 | tf_op jit(solution)/shard_map/ppermute | solution.py:966
  445.5 32.9 %collective-permute-start.42 = (bf16[2,128,1024]{2,1,0:T(8,128)(2,1)S(1)}, bf16[2,128,1024]{2,1,0:T(8,128)(2,1)S(1)}, u32[]{:S(2)}, u32[]{:S(2)}) collective-permute-start(bf16[2,128,1024]{2,1,0:T(8,128)(2,1)S(1)} %copy-done.123), channel_id=1, source_target_pairs={{6,0},{7,1},{0,2},{1,3},{2,4},{3,5},{4,6},{5,7},{14,8},{15,9},{8,1... | collective-permute-start | bytes 1572872 | tf_op jit(solution)/shard_map/ppermute | solution.py:966
  543.5 41.5 %collective-permute-start.52 = (bf16[1,128,1024]{2,1,0:T(8,128)(2,1)}, bf16[1,128,1024]{2,1,0:T(8,128)(2,1)S(1)}, u32[]{:S(2)}, u32[]{:S(2)}) collective-permute-start(bf16[1,128,1024]{2,1,0:T(8,128)(2,1)} %get-tuple-element.193), channel_id=1, source_target_pairs={{4,0},{5,1},{6,2},{7,3},{0,4},{1,5},{2,6},{3,7},{12,8},{13,9},{14,... | collective-permute-start | bytes 786440 | tf_op jit(solution)/shard_map/ppermute | solution.py:966
  553.5 29.5 %collective-permute-start.68 = (bf16[1,128,1024]{2,1,0:T(8,128)(2,1)}, bf16[1,128,1024]{2,1,0:T(8,128)(2,1)S(1)}, u32[]{:S(2)}, u32[]{:S(2)}) collective-permute-start(bf16[1,128,1024]{2,1,0:T(8,128)(2,1)} %get-tuple-element.211), channel_id=1, source_target_pairs={{16,0},{24,8},{0,16},{8,24},{17,1},{25,9},{1,17},{9,25},{18,2},{26... | collective-permute-start | bytes 786440 | tf_op jit(solution)/shard_map/ppermute | solution.py:969
  554.9 28.2 %collective-permute-start.69 = (bf16[1,128,1024]{2,1,0:T(8,128)(2,1)}, bf16[1,128,1024]{2,1,0:T(8,128)(2,1)S(1)}, u32[]{:S(2)}, u32[]{:S(2)}) collective-permute-start(bf16[1,128,1024]{2,1,0:T(8,128)(2,1)} %get-tuple-element.204.refs_4_), channel_id=1, source_target_pairs={{8,0},{0,8},{24,16},{16,24},{9,1},{1,9},{25,17},{17,25},{10,2},{2,... | collective-permute-start | bytes 786440 | tf_op jit(solution)/shard_map/ppermute | solution.py:969
  599.8 72.2 %collective-permute-start.61 = (bf16[4,128,1024]{2,1,0:T(8,128)(2,1)S(1)}, bf16[4,128,1024]{2,1,0:T(8,128)(2,1)S(1)}, u32[]{:S(2)}, u32[]{:S(2)}) collective-permute-start(bf16[4,128,1024]{2,1,0:T(8,128)(2,1)S(1)} %constant_dynamic-update-slice_fusion.4.refs_0_), channel_id=1, source_target_pairs={{8,0},{0,8},{24,16},{16,24},{9,1},{1,9},{25,17},{17,25},{10,2},{2,... | collective-permute-start | bytes 3145736 | tf_op jit(solution)/shard_map/ppermute | solution.py:969
  615.4 56.7 %collective-permute-start.63 = (bf16[4,128,1024]{2,1,0:T(8,128)(2,1)S(1)}, bf16[4,128,1024]{2,1,0:T(8,128)(2,1)S(1)}, u32[]{:S(2)}, u32[]{:S(2)}) collective-permute-start(bf16[4,128,1024]{2,1,0:T(8,128)(2,1)S(1)} %constant_dynamic-update-slice_fusion.4.refs_0_), channel_id=1, source_target_pairs={{16,0},{24,8},{0,16},{8,24},{17,1},{25,9},{1,17},{9,25},{18,2},{26... | collective-permute-start | bytes 3145736 | tf_op jit(solution)/shard_map/ppermute | solution.py:969
  616.1 56.0 %collective-permute-start.67 = (bf16[512,1024]{1,0:T(8,128)(2,1)S(1)}, bf16[512,1024]{1,0:T(8,128)(2,1)}, u32[]{:S(2)}, u32[]{:S(2)}) collective-permute-start(bf16[512,1024]{1,0:T(8,128)(2,1)S(1)} %constant_dynamic-update-slice_fusion.6.mine_ref), channel_id=1, source_target_pairs={{0,1},{1,0},{2,3},{3,2},{4,5},{5,4},{6,7},{7,6},{8,9},{9,8},{10,11... | collective-permute-start | bytes 3145736 | tf_op jit(solution)/shard_map/ppermute | solution.py:958
  726.6 51.3 %collective-permute-start.87 = (bf16[2,128,1024]{2,1,0:T(8,128)(2,1)}, bf16[2,128,1024]{2,1,0:T(8,128)(2,1)}, u32[]{:S(2)}, u32[]{:S(2)}) collective-permute-start(bf16[2,128,1024]{2,1,0:T(8,128)(2,1)} %shard_map.356.refs_1_), channel_id=1, source_target_pairs={{8,0},{0,8},{24,16},{16,24},{9,1},{1,9},{25,17},{17,25},{10,2},{2,... | collective-permute-start | bytes 1572872 | tf_op jit(solution)/shard_map/ppermute | solution.py:969
  728.5 37.1 %collective-permute-start.89 = (bf16[128,1024]{1,0:T(8,128)(2,1)}, bf16[128,1024]{1,0:T(8,128)(2,1)}, u32[]{:S(2)}, u32[]{:S(2)}) collective-permute-start(bf16[128,1024]{1,0:T(8,128)(2,1)} %slice_bitcast_fusion.2), channel_id=1, source_target_pairs={{8,0},{0,8},{24,16},{16,24},{9,1},{1,9},{25,17},{17,25},{10,2},{2,... | collective-permute-start | bytes 786440 | tf_op jit(solution)/shard_map/ppermute | solution.py:969
  (188 other events, 1803.0 us)

commit v4 on v3

--- a/solution.py
+++ b/solution.py
@@ -1058,8 +1058,8 @@
     state["shards"], state["quarters"], wide_moments, square_moments = prepare()
     state["other_shards"] = swap(state["shards"])
     run_phase(state, 0, [state["shards"]])
-    run_phase(state, 1, [])
-    run_phase(state, 2, [state["other_shards"]])
+    run_phase(state, 1, [state["other_shards"]])
+    run_phase(state, 2, [])
     self_full = placed_blocks(place_now, shares_of(state, 0), 0, chips, [])
 
     def first_sums(kinds, others, *waited):
@@ -1164,13 +1164,11 @@
     self_other = weight_rows(place_now, [self_kind], None, [cross_stage[0]])[0]
     wide_stage = third_sums(wide_stage, self_other)
     cross_stage, cross_token = second_sums(cross_stage, wide_stage[0])
-    self_stage = first_sums([self_kind], [self_other], cross_token)
-    first_sums_done = self_stage[0]
-    cross_stage = third_sums(cross_stage, self_stage[0])
+    self_stage = first_sums([self_kind], [self_other], cross_token, *cross_stage[3:])
+    wide_fresh = fresh_blocks(place_now, *wide_stage, wide_moments, self_stage[0])
+    wide_grads = wide_fresh[0]
+    cross_stage = third_sums(cross_stage, wide_grads)
     self_stage, self_token = second_sums(self_stage, cross_stage[0])
-    wide_fresh = fresh_blocks(place_now, *wide_stage, wide_moments, self_token)
-    wide_grads = wide_fresh[0]
-    self_stage = third_sums(self_stage, wide_grads)
 
     def owned(grads_fresh):
         mine, *sent = grads_fresh[1:]
@@ -1185,9 +1183,8 @@
         )
 
     wide_own = owned(wide_fresh)
-    to_x, to_y, kept, later = gram_parts(
-        place_now, *wide_own, reps, self_stage[0]
-    )
+    to_x, to_y, kept, later = gram_parts(place_now, *wide_own, reps, self_token)
+    self_stage = third_sums(self_stage, kept, *cross_stage[1])
     gram_stage, gram_token = second_sums((kept, later, from_rep(to_x, 1), from_rep(to_y, 2)))
     kept, by_x, by_y, last_x, last_y = gram_stage
     quarter = jnp.concatenate(
@@ -1218,13 +1215,8 @@
     wide_orth_shared = share_pair(wide_orth)
     square_rows = square_schulz(*square_own, rows, wide_orth, grads_x, grads_y)
     grads_across = [from_rep(grads_y[:2], 1), from_rep(grads_x[2:], 2)]
-    square_orth = held_until(
-        to_both(square_rows), wide_orth_shared[1], wide_orth_shared[2], *grads_across
-    )
-    square_orth_shared = share_pair(square_orth)
-
-    late_sq = held_until(grad_sq, first_sums_done)
-    late_ck = held_until(grad_ck, first_sums_done)
+    late_sq = held_until(grad_sq, square_rows)
+    late_ck = held_until(grad_ck, square_rows)
     grad_states = matmul_right_t(late_ck, cross_full[1]) + matmul_right_t(grad_cv, cross_full[2])
     grad_first = (
         matmul_right_t(late_sq, self_full[0])
@@ -1241,7 +1233,7 @@
             jnp.stack([first_bias, second_bias, third_bias]),
         ]
     )
-    norm_local = held_until(norm_local, square_orth)
+    norm_local = held_until(norm_local, square_rows)
     norm_total = norm_local + swap(norm_local)
     norm_total = norm_total + from_rep(norm_total, 1)
     norm_total = norm_total + from_rep(norm_total, 2)
@@ -1249,14 +1241,11 @@
     width_part = norm_moment.shape[2]
     norm_grad = lax.dynamic_slice_in_dim(norm_total, my_place * width_part, width_part, 2)
 
-    late_grads = held_until(grads, square_orth)
+    late_grads = held_until(grads, square_rows)
     wide_grads_shared = [late_grads[:2], grads_x[:2], grads_y[:2], grads_across[0]]
     square_grads_shared = [late_grads[2:], grads_x[2:], grads_y[2:], grads_across[1]]
-    wide_orth_shared[0] = held_until(wide_orth_shared[0], square_orth)
     in_shared, out_shared = to_replicas(wide_grads_shared)
     self_shared, cross_shared = to_replicas(square_grads_shared)
-    in_orth_shared, out_orth_shared = to_replicas(wide_orth_shared)
-    self_orth_shared, cross_orth_shared = to_replicas(square_orth_shared)
 
     def stacked(pieces):
         return jnp.stack(pieces).astype(jnp.float32)
@@ -1268,15 +1257,28 @@
     cross_grad = stacked(cross_shared)
     fc_in_grad = in_shard(in_shared).astype(jnp.float32)
     fc_out_grad = lengthwise(out_shared)
+    self_fresh = MOMENTUM_DECAY * self_moment + self_grad
+    cross_fresh = MOMENTUM_DECAY * cross_moment + cross_grad
+    in_fresh = MOMENTUM_DECAY * fc_in_moment + fc_in_grad
+    out_fresh = MOMENTUM_DECAY * fc_out_moment + fc_out_grad
+
+    square_orth = held_until(
+        to_both(square_rows),
+        wide_orth_shared[1],
+        wide_orth_shared[2],
+        self_fresh,
+        cross_fresh,
+        in_fresh,
+        out_fresh,
+    )
+    square_orth_shared = share_pair(square_orth)
+    wide_orth_shared[0] = held_until(wide_orth_shared[0], *square_orth_shared[1:3])
+    in_orth_shared, out_orth_shared = to_replicas(wide_orth_shared)
+    self_orth_shared, cross_orth_shared = to_replicas(square_orth_shared)
     self_orth = stacked(self_orth_shared)
     cross_orth = stacked(cross_orth_shared)
     in_orth = in_shard(in_orth_shared).astype(jnp.float32)
     out_orth = lengthwise(out_orth_shared)
-
-    self_fresh = MOMENTUM_DECAY * self_moment + self_grad
-    cross_fresh = MOMENTUM_DECAY * cross_moment + cross_grad
-    in_fresh = MOMENTUM_DECAY * fc_in_moment + fc_in_grad
-    out_fresh = MOMENTUM_DECAY * fc_out_moment + fc_out_grad
     norm_fresh = MOMENTUM_DECAY * norm_moment + norm_grad
     self_new = self_weights - MATRIX_RATE * stretch((width, width)) * self_orth
     cross_new = cross_weights - MATRIX_RATE * stretch((width, width)) * cross_orth

time: 798 us -> 761 us (0.954)
  waiting for transfers between devices: 304 us -> 281 us
  starting transfers between devices: 95.4 us -> 79.2 us
    ppermute x44, waiting for transfers between devices: 141 us -> 122 us  [from_rep(): lax.ppermute(values, 'rep', [(index ^ step, index) for index in range(rep...]
    ppermute x32, starting transfers between devices: 46.3 us -> 30.1 us  [from_chip(): return lax.ppermute(values, 'shard', pairs)]
    unnamed x276 -> x258, local copies, waits for them, and re-layouts: 33.3 us -> 33.4 us
  transfers between devices with their start and end apart: 91 -> 91, of which waited for: 46 -> 39; matrix products, arithmetic and copies ran while one was open for 12% -> 13% of each run, Pallas kernels for 17% -> 23%
where the time goes in v4:
time: 761 us; the launch traced here: 756 us
  waiting for transfers between devices  281 us (37%)
  Pallas kernels  260 us (34%)
  starting transfers between devices  79.2 us (10%)
  local copies, waits for them, and re-layouts  52.9 us (7%)
  other arithmetic  46 us (6%)
  matrix products  33.7 us (4%)
    ppermute x32, waiting for transfers between devices, from_chip(): return lax.ppermute(values, 'shard', pairs)  157 us
    ppermute x44, waiting for transfers between devices, from_rep(): lax.ppermute(values, 'rep', [(index ^ step, index) for index in range(rep...  122 us
    ppermute x44, starting transfers between devices, from_rep(): lax.ppermute(values, 'rep', [(index ^ step, index) for index in range(rep...  47.3 us
    pallas_call x7, Pallas kernels, weight_rows(): pl.pallas_call(kernel, out_shape=tuple(out_shapes), in_specs=[pl.BlockSpe...  47 us
    pallas_call x4, Pallas kernels, attention_call(): pl.pallas_call(kernel, out_shape=tuple(out_shapes), in_specs=[pl.BlockSpe...  46.9 us
    pallas_call x1, Pallas kernels, gram_schulz(): pl.pallas_call(kernel, out_shape=low(2, rows, size), in_specs=[pl.BlockSp...  33.9 us
    unnamed x258, local copies, waits for them, and re-layouts  33.4 us
    ppermute x32, starting transfers between devices, from_chip(): return lax.ppermute(values, 'shard', pairs)  30.1 us
  transfers between devices with their start and end apart: 91, of which 39 were waited for; matrix products, arithmetic and copies ran while one was open for 13% of the time, Pallas kernels for 23%

profile of v4, /device:TPU:0, one launch (start us, length us, event | category | flops | bytes accessed | tf_op | source)
XLA Modules:
  0.0 756.2 jit_solution(15697298301027774967)
XLA Ops:
  1.3 7.9 %shard_map.318 = (bf16[4,4,128,1024]{3,2,1,0:T(8,128)(2,1)}, bf16[128,1024]{1,0:T(8,128)(2,1)}, bf16[128,1024]{1,0:T(8,128)(2,1)}, bf16[128,1024]{1,0:T(8,128)(2...) custom-call(s32[4]{0:T(128)} %pad_add_fusion.place_ref, f32[4,128,1024]{2,1,0:T(8,128)} %refs_0_.1, ...), custom_call_target="tpu_custom_call" | custom-call | flops 1024 | bytes 1024 | tf_op jit(solution)/shard_map/pallas_call | solution.py:871
  22.2 16.3 %collective-permute-done.1.refs_1_ = bf16[128,1024]{1,0:T(8,128)(2,1)S(1)} collective-permute-done((bf16[128,1024]{1,0:T(8,128)(2,1)S(1)}, bf16[128,1024]{1,0:T(8,128)(2,1)S(1)}, u32[]{:S(2)}, u32[]{:S(2)}) %collective-permute-start.1) | collective-permute-done | bytes 262176 | tf_op jit(solution)/shard_map/ppermute | solution.py:966
  52.5 12.0 %collective-permute-done.6.refs_1_ = bf16[128,1024]{1,0:T(8,128)(2,1)S(1)} collective-permute-done((bf16[128,1024]{1,0:T(8,128)(2,1)}, bf16[128,1024]{1,0:T(8,128)(2,1)S(1)}, u32[]{:S(2)}, u32[]{:S(2)}) %collective-permute-start.6) | collective-permute-done | bytes 262176 | tf_op jit(solution)/shard_map/ppermute | solution.py:966
  64.4 10.2 %collective-permute-done.7.refs_2_ = bf16[128,1024]{1,0:T(8,128)(2,1)S(1)} collective-permute-done((bf16[128,1024]{1,0:T(8,128)(2,1)}, bf16[128,1024]{1,0:T(8,128)(2,1)S(1)}, u32[]{:S(2)}, u32[]{:S(2)}) %collective-permute-start.7) | collective-permute-done | bytes 262176 | tf_op jit(solution)/shard_map/ppermute | solution.py:966
  83.8 8.8 %collective-permute-done.13.refs_0_ = bf16[128,1024]{1,0:T(8,128)(2,1)S(1)} collective-permute-done((bf16[128,1024]{1,0:T(8,128)(2,1)}, bf16[128,1024]{1,0:T(8,128)(2,1)S(1)}, u32[]{:S(2)}, u32[]{:S(2)}) %collective-permute-start.13) | collective-permute-done | bytes 262176 | tf_op jit(solution)/shard_map/ppermute | solution.py:966
  92.6 13.7 %collective-permute-done.14.refs_1_ = bf16[128,1024]{1,0:T(8,128)(2,1)S(1)} collective-permute-done((bf16[128,1024]{1,0:T(8,128)(2,1)}, bf16[128,1024]{1,0:T(8,128)(2,1)S(1)}, u32[]{:S(2)}, u32[]{:S(2)}) %collective-permute-start.14) | collective-permute-done | bytes 262176 | tf_op jit(solution)/shard_map/ppermute | solution.py:966
  124.5 7.8 %shard_map.324 = (bf16[4,2,128,1024]{3,2,1,0:T(8,128)(2,1)}, bf16[4,2,128,1024]{3,2,1,0:T(8,128)(2,1)}, bf16[4,2,128,1024]{3,2,1,0:T(8,128)(2,1)}, bf16[4,2,128,1024]{3,2,1,0:T(8,128)(2,1)}) custom-call(s32[4]{0:T(128)} %pad_add_fusion.place_ref, bf16[4,4,128,1024]{3,2,1,0:T(8,128)(2,1)} %get-tuple-element.118.refs_3_.refs_0_.refs_12_, ...), custom_call_target="tpu_custom_call" | custom-call | flops 1024 | bytes 1024 | tf_op jit(solution)/shard_map/pallas_call | solution.py:740
  156.1 9.5 %shard_map.325.refs_1_ = bf16[256,1024]{1,0:T(8,128)(2,1)} custom-call(s32[1]{0:T(128)S(6)} %copy.87.count_ref, bf16[256,1024]{1,0:T(8,128)(2,1)} %convolution_convert_fusion.6.query_ref.refs_5_, bf16[256,1024]{1,0:T(8,128)(2,1)} %convolution_convert_fusion.5.key_ref.refs_6_, bf16[256,1024]{1,0:T(8,128)(2,1)} %convolution_convert_fusion.4.value_ref.refs_7_), custom_call_target="tpu_custom_call" | custom-call | flops 1024 | bytes 1024 | tf_op jit(solution)/shard_map/pallas_call | solution.py:86
  170.0 7.7 %shard_map.328 = (bf16[4,2,128,1024]{3,2,1,0:T(8,128)(2,1)}, bf16[4,2,128,1024]{3,2,1,0:T(8,128)(2,1)}, bf16[4,2,128,1024]{3,2,1,0:T(8,128)(2,1)}, bf16[4,2,128,1024]{3,2,1,0:T(8,128)(2,1)}) custom-call(s32[4]{0:T(128)} %pad_add_fusion.place_ref, bf16[4,4,128,1024]{3,2,1,0:T(8,128)(2,1)} %get-tuple-element.118.refs_3_.refs_0_.refs_12_, ...), custom_call_target="tpu_custom_call" | custom-call | flops 1024 | bytes 1024 | tf_op jit(solution)/shard_map/pallas_call | solution.py:740
  192.4 10.4 %shard_map.329.refs_2_ = bf16[256,1024]{1,0:T(8,128)(2,1)} custom-call(s32[1]{0:T(128)S(6)} %copy.88.count_ref, bf16[256,1024]{1,0:T(8,128)(2,1)} %convolution_convert_fusion.3.query_ref, bf16[384,1024]{1,0:T(8,128)(2,1)} %fusion.3.key_ref.refs_2_, bf16[384,1024]{1,0:T(8,128)(2,1)} %fusion.4.value_ref.refs_3_), custom_call_target="tpu_custom_call" | custom-call | flops 1024 | bytes 1024 | tf_op jit(solution)/shard_map/pallas_call | solution.py:86
  209.6 17.7 %shard_map.331 = (f32[256,1024]{1,0:T(8,128)}, f32[256,1024]{1,0:T(8,128)}, bf16[256,1024]{1,0:T(8,128)(2,1)}, bf16[256,1024]{1,0:T(8,128)(2,1)}, bf16[256,1024]...) custom-call(s32[4]{0:T(128)} %pad_add_fusion.place_ref, ...), custom_call_target="tpu_custom_call" | custom-call | flops 1024 | bytes 1024 | tf_op jit(solution)/shard_map/pallas_call | solution.py:810
  242.6 14.2 %shard_map.332 = (bf16[256,1024]{1,0:T(8,128)(2,1)}, bf16[384,1024]{1,0:T(8,128)(2,1)}, bf16[384,1024]{1,0:T(8,128)(2,1)}) custom-call(s32[1]{0:T(128)S(6)} %copy.88.count_ref, bf16[256,1024]{1,0:T(8,128)(2,1)} %convolution_convert_fusion.3.query_ref, bf16[384,1024]{1,0:T(8,128)(2,1)} %fusion.3.key_ref.refs_2_, bf16[384,1024]{1,0:T(8,128)(2,1)} %fusion.4.value_ref.refs_3_, ...), custom_call_target="tpu_custom_call" | custom-call | flops 1024 | bytes 1024 | tf_op jit(solution)/shard_map/pallas_call | solution.py:86
  256.8 10.5 %shard_map.335 = (bf16[2,2,256,1024]{3,2,1,0:T(8,128)(2,1)}, bf16[2,2,256,1024]{3,2,1,0:T(8,128)(2,1)}, bf16[2,2,256,1024]{3,2,1,0:T(8,128)(2,1)}, bf16[2,2,256,1024]{3,2,1,0:T(8,128)(2,1)}) custom-call(s32[4]{0:T(128)} %pad_add_fusion.place_ref, bf16[256,1024]{1,0:T(8,128)(2,1)} %add_convert_fusion.1.third_ref.refs_0_, ...), custom_call_target="tpu_custom_call" | custom-call | flops 1024 | bytes 1024 | tf_op jit(solution)/shard_map/pallas_call | solution.py:502
  267.2 6.3 shard_map.336.refs_0_
  282.9 12.8 %shard_map.338 = (bf16[256,1024]{1,0:T(8,128)(2,1)}, bf16[256,1024]{1,0:T(8,128)(2,1)}, bf16[256,1024]{1,0:T(8,128)(2,1)}) custom-call(s32[1]{0:T(128)S(6)} %copy.87.count_ref, bf16[256,1024]{1,0:T(8,128)(2,1)} %convolution_convert_fusion.6.query_ref.refs_5_, bf16[256,1024]{1,0:T(8,128)(2,1)} %convolution_convert_fusion.5.key_ref.refs_6_, ...), custom_call_target="tpu_custom_call" | custom-call | flops 1024 | bytes 1024 | tf_op jit(solution)/shard_map/pallas_call | solution.py:86
  295.7 26.1 %collective-permute-done.33.x_ref = bf16[2,2,256,1024]{3,2,1,0:T(8,128)(2,1)S(1)} collective-permute-done((bf16[2,2,256,1024]{3,2,1,0:T(8,128)(2,1)}, bf16[2,2,256,1024]{3,2,1,0:T(8,128)(2,1)S(1)}, u32[]{:S(2)}, u32[]{:S(2)}) %collective-permute-start.33) | collective-permute-done | bytes 2097184 | tf_op jit(solution)/shard_map/ppermute | solution.py:969
  328.3 7.6 %shard_map.340 = (bf16[1,2,256,1024]{3,2,1,0:T(8,128)(2,1)}, bf16[1,2,256,1024]{3,2,1,0:T(8,128)(2,1)}, bf16[1,2,256,1024]{3,2,1,0:T(8,128)(2,1)}, bf16[1,2,256,1024]{3,2,1,0:T(8,128)(2,1)}) custom-call(s32[4]{0:T(128)} %pad_add_fusion.place_ref, bf16[256,1024]{1,0:T(8,128)(2,1)} %copy-done.41, bf16[384,1024]{1,0:T(8,128)(2,1)} %bitcast.336, ...), custom_call_target="tpu_custom_call" | custom-call | flops 1024 | bytes 1024 | tf_op jit(solution)/shard_map/pallas_call | solution.py:502
  345.4 21.9 %collective-permute-done.38.last_x_ref = bf16[2,256,1024]{2,1,0:T(8,128)(2,1)S(1)} collective-permute-done((bf16[2,256,1024]{2,1,0:T(8,128)(2,1)S(1)}, bf16[2,256,1024]{2,1,0:T(8,128)(2,1)S(1)}, u32[]{:S(2)}, u32[]{:S(2)}) %collective-permute-start.38) | collective-permute-done | bytes 1048608 | tf_op jit(solution)/shard_map/ppermute | solution.py:969
  368.6 6.3 shard_map.342
  374.9 14.4 %collective-permute-done.36.x_ref = bf16[1,2,256,1024]{3,2,1,0:T(8,128)(2,1)S(1)} collective-permute-done((bf16[1,2,256,1024]{3,2,1,0:T(8,128)(2,1)}, bf16[1,2,256,1024]{3,2,1,0:T(8,128)(2,1)S(1)}, u32[]{:S(2)}, u32[]{:S(2)}) %collective-permute-start.36) | collective-permute-done | bytes 1048608 | tf_op jit(solution)/shard_map/ppermute | solution.py:969
  397.3 10.1 %collective-permute-done.40.refs_8_.last_x_ref = bf16[1,256,1024]{2,1,0:T(8,128)(2,1)S(1)} collective-permute-done((bf16[1,256,1024]{2,1,0:T(8,128)(2,1)}, bf16[1,256,1024]{2,1,0:T(8,128)(2,1)S(1)}, u32[]{:S(2)}, u32[]{:S(2)}) %collective-permute-start.40) | collective-permute-done | bytes 524320 | tf_op jit(solution)/shard_map/ppermute | solution.py:969
  411.4 6.6 shard_map.344
  418.0 23.6 %collective-permute-done.45.refs_1_ = bf16[2,128,1024]{2,1,0:T(8,128)(2,1)S(1)} collective-permute-done((bf16[2,128,1024]{2,1,0:T(8,128)(2,1)}, bf16[2,128,1024]{2,1,0:T(8,128)(2,1)S(1)}, u32[]{:S(2)}, u32[]{:S(2)}) %collective-permute-start.45) | collective-permute-done | bytes 524320 | tf_op jit(solution)/shard_map/ppermute | solution.py:966
  453.5 18.0 %collective-permute-done.50 = bf16[128,1024]{1,0:T(8,128)(2,1)S(1)} collective-permute-done((bf16[128,1024]{1,0:T(8,128)(2,1)}, bf16[128,1024]{1,0:T(8,128)(2,1)S(1)}, u32[]{:S(2)}, u32[]{:S(2)}) %collective-permute-start.50) | collective-permute-done | bytes 262176 | tf_op jit(solution)/shard_map/ppermute | solution.py:966
  484.7 6.3 shard_map.348
  492.1 7.3 collective-permute-done.54.refs_2_
  521.6 8.8 %collective-permute-done.57 = bf16[1,128,1024]{2,1,0:T(8,128)(2,1)S(1)} collective-permute-done((bf16[1,128,1024]{2,1,0:T(8,128)(2,1)}, bf16[1,128,1024]{2,1,0:T(8,128)(2,1)S(1)}, u32[]{:S(2)}, u32[]{:S(2)}) %collective-permute-start.57) | collective-permute-done | bytes 262176 | tf_op jit(solution)/shard_map/ppermute | solution.py:966
  550.6 16.0 %collective-permute-done.62 = bf16[128,1024]{1,0:T(8,128)(2,1)S(1)} collective-permute-done((bf16[128,1024]{1,0:T(8,128)(2,1)}, bf16[128,1024]{1,0:T(8,128)(2,1)S(1)}, u32[]{:S(2)}, u32[]{:S(2)}) %collective-permute-start.62) | collective-permute-done | bytes 262176 | tf_op jit(solution)/shard_map/ppermute | solution.py:966
  572.0 13.4 %collective-permute-done.69.a_ref = bf16[128,1024]{1,0:T(8,128)(2,1)S(1)} collective-permute-done((bf16[128,1024]{1,0:T(8,128)(2,1)S(1)}, bf16[128,1024]{1,0:T(8,128)(2,1)S(1)}, u32[]{:S(2)}, u32[]{:S(2)}) %collective-permute-start.69) | collective-permute-done | bytes 262176 | tf_op jit(solution)/shard_map/ppermute | solution.py:969
  585.4 11.0 %collective-permute-done.70.b_ref = bf16[128,1024]{1,0:T(8,128)(2,1)S(1)} collective-permute-done((bf16[128,1024]{1,0:T(8,128)(2,1)S(1)}, bf16[128,1024]{1,0:T(8,128)(2,1)S(1)}, u32[]{:S(2)}, u32[]{:S(2)}) %collective-permute-start.70) | collective-permute-done | bytes 262176 | tf_op jit(solution)/shard_map/ppermute | solution.py:969
  597.2 33.9 %shard_map.352 = bf16[2,128,1024]{2,1,0:T(8,128)(2,1)} custom-call(s32[4]{0:T(128)} %pad_add_fusion.place_ref, bf16[256,1024]{1,0:T(8,128)(2,1)} %copy-done.68, bf16[256,1024]{1,0:T(8,128)(2,1)} %copy-done.76, bf16[256,1024]{1,0:T(8,128)(2,1)} %copy-done.75, bf16[128,1024]{1,0:T(8,128)(2,1)} %copy-done.106, bf16[128,1024]{1,0:T(8,128)(2,1)} %copy-done.108, ...), custom_call_target="tpu_custom_call" | custom-call | flops 1024 | bytes 1024 | tf_op jit(solution)/shard_map/pallas_call | solution.py:380
  641.0 25.5 %shard_map.353.refs_1_ = bf16[2,128,1024]{2,1,0:T(8,128)(2,1)} custom-call(bf16[512,1024]{1,0:T(8,128)(2,1)} %constant_dynamic-update-slice_fusion.4.mine_ref, bf16[512,1024]{1,0:T(8,128)(2,1)} %collective-permute-done.64.sibling_ref, bf16[2,128,1024]{2,1,0:T(8,128)(2,1)} %pad_maximum_fusion.5.refs_0_, bf16[4,128,1024]{2,1,0:T(8,128)(2,1)} %copy-done.11, ...), custom_call_target="tpu_custom_call" | custom-call | flops 1024 | bytes 1024 | tf_op jit(solution)/shard_map/pallas_call | solution.py:233
  (540 shorter events, 330.1 us)
Async XLA Ops:
  9.2 65.4 %collective-permute-start.8 = (bf16[4,4,128,1024]{3,2,1,0:T(8,128)(2,1)}, bf16[4,4,128,1024]{3,2,1,0:T(8,128)(2,1)}, u32[]{:S(2)}, u32[]{:S(2)}) collective-permute-start(bf16[4,4,128,1024]{3,2,1,0:T(8,128)(2,1)} %get-tuple-element.118.refs_3_.refs_0_.refs_12_), channel_id=1, source_target_pairs={{0,1},{1,0},{2,3},{3,2},{4,5},{5,4},{6,7},{7,6},{8,9},{9,8},{10,11... | collective-permute-start | bytes 12582920 | tf_op jit(solution)/shard_map/ppermute | solution.py:958
  42.5 32.1 %collective-permute-start.9 = (bf16[384,1024]{1,0:T(8,128)(2,1)}, bf16[384,1024]{1,0:T(8,128)(2,1)S(1)}, u32[]{:S(2)}, u32[]{:S(2)}) collective-permute-start(bf16[384,1024]{1,0:T(8,128)(2,1)} %get-tuple-element.122.refs_1_), channel_id=1, source_target_pairs={{0,1},{1,0},{2,3},{3,2},{4,5},{5,4},{6,7},{7,6},{8,9},{9,8},{10,11... | collective-permute-start | bytes 2359304 | tf_op jit(solution)/shard_map/ppermute | solution.py:958
  42.5 32.1 %collective-permute-start.3 = (bf16[384,1024]{1,0:T(8,128)(2,1)}, bf16[384,1024]{1,0:T(8,128)(2,1)S(1)}, u32[]{:S(2)}, u32[]{:S(2)}) collective-permute-start(bf16[384,1024]{1,0:T(8,128)(2,1)} %get-tuple-element.119.refs_1_), channel_id=1, source_target_pairs={{8,0},{0,8},{24,16},{16,24},{9,1},{1,9},{25,17},{17,25},{10,2},{2,... | collective-permute-start | bytes 2359304 | tf_op jit(solution)/shard_map/ppermute | solution.py:969
  44.1 30.6 %collective-permute-start.4 = (bf16[384,1024]{1,0:T(8,128)(2,1)}, bf16[384,1024]{1,0:T(8,128)(2,1)S(1)}, u32[]{:S(2)}, u32[]{:S(2)}) collective-permute-start(bf16[384,1024]{1,0:T(8,128)(2,1)} %get-tuple-element.120), channel_id=1, source_target_pairs={{16,0},{24,8},{0,16},{8,24},{17,1},{25,9},{1,17},{9,25},{18,2},{26... | collective-permute-start | bytes 2359304 | tf_op jit(solution)/shard_map/ppermute | solution.py:969
  80.1 29.8 %collective-permute-start.12 = (bf16[1152,1024]{1,0:T(8,128)(2,1)}, bf16[1152,1024]{1,0:T(8,128)(2,1)S(1)}, u32[]{:S(2)}, u32[]{:S(2)}) collective-permute-start(bf16[1152,1024]{1,0:T(8,128)(2,1)} %get-tuple-element.125.refs_1_), channel_id=1, source_target_pairs={{0,1},{1,0},{2,3},{3,2},{4,5},{5,4},{6,7},{7,6},{8,9},{9,8},{10,11... | collective-permute-start | bytes 7077896 | tf_op jit(solution)/shard_map/ppermute | solution.py:958
  80.2 28.6 %collective-permute-start.10 = (bf16[576,1024]{1,0:T(8,128)(2,1)}, bf16[576,1024]{1,0:T(8,128)(2,1)S(1)}, u32[]{:S(2)}, u32[]{:S(2)}) collective-permute-start(bf16[576,1024]{1,0:T(8,128)(2,1)} %get-tuple-element.123.refs_1_), channel_id=1, source_target_pairs={{8,0},{0,8},{24,16},{16,24},{9,1},{1,9},{25,17},{17,25},{10,2},{2,... | collective-permute-start | bytes 3538952 | tf_op jit(solution)/shard_map/ppermute | solution.py:969
  81.6 28.3 %collective-permute-start.11 = (bf16[576,1024]{1,0:T(8,128)(2,1)}, bf16[576,1024]{1,0:T(8,128)(2,1)S(1)}, u32[]{:S(2)}, u32[]{:S(2)}) collective-permute-start(bf16[576,1024]{1,0:T(8,128)(2,1)} %get-tuple-element.124), channel_id=1, source_target_pairs={{16,0},{24,8},{0,16},{8,24},{17,1},{25,9},{1,17},{9,25},{18,2},{26... | collective-permute-start | bytes 3538952 | tf_op jit(solution)/shard_map/ppermute | solution.py:969
  117.4 28.7 %collective-permute-start.17 = (bf16[576,1024]{1,0:T(8,128)(2,1)}, bf16[576,1024]{1,0:T(8,128)(2,1)S(1)}, u32[]{:S(2)}, u32[]{:S(2)}) collective-permute-start(bf16[576,1024]{1,0:T(8,128)(2,1)} %get-tuple-element.132.refs_1_), channel_id=1, source_target_pairs={{8,0},{0,8},{24,16},{16,24},{9,1},{1,9},{25,17},{17,25},{10,2},{2,... | collective-permute-start | bytes 3538952 | tf_op jit(solution)/shard_map/ppermute | solution.py:969
  118.1 28.3 %collective-permute-start.18 = (bf16[576,1024]{1,0:T(8,128)(2,1)}, bf16[576,1024]{1,0:T(8,128)(2,1)S(1)}, u32[]{:S(2)}, u32[]{:S(2)}) collective-permute-start(bf16[576,1024]{1,0:T(8,128)(2,1)} %get-tuple-element.133), channel_id=1, source_target_pairs={{16,0},{24,8},{0,16},{8,24},{17,1},{25,9},{1,17},{9,25},{18,2},{26... | collective-permute-start | bytes 3538952 | tf_op jit(solution)/shard_map/ppermute | solution.py:969
  152.5 30.8 %collective-permute-start.23 = (bf16[576,1024]{1,0:T(8,128)(2,1)}, bf16[576,1024]{1,0:T(8,128)(2,1)S(1)}, u32[]{:S(2)}, u32[]{:S(2)}) collective-permute-start(bf16[576,1024]{1,0:T(8,128)(2,1)} %get-tuple-element.140.refs_13_), channel_id=1, source_target_pairs={{8,0},{0,8},{24,16},{16,24},{9,1},{1,9},{25,17},{17,25},{10,2},{2,... | collective-permute-start | bytes 3538952 | tf_op jit(solution)/shard_map/ppermute | solution.py:969
  153.2 30.1 %collective-permute-start.24 = (bf16[576,1024]{1,0:T(8,128)(2,1)}, bf16[576,1024]{1,0:T(8,128)(2,1)S(1)}, u32[]{:S(2)}, u32[]{:S(2)}) collective-permute-start(bf16[576,1024]{1,0:T(8,128)(2,1)} %get-tuple-element.141), channel_id=1, source_target_pairs={{16,0},{24,8},{0,16},{8,24},{17,1},{25,9},{1,17},{9,25},{18,2},{26... | collective-permute-start | bytes 3538952 | tf_op jit(solution)/shard_map/ppermute | solution.py:969
  273.5 54.8 %collective-permute-start.32 = (bf16[4,512,1024]{2,1,0:T(8,128)(2,1)}, bf16[4,512,1024]{2,1,0:T(8,128)(2,1)}, u32[]{:S(2)}, u32[]{:S(2)}) collective-permute-start(bf16[4,512,1024]{2,1,0:T(8,128)(2,1)} %shard_map.336.refs_0_), channel_id=1, source_target_pairs={{0,1},{1,0},{2,3},{3,2},{4,5},{5,4},{6,7},{7,6},{8,9},{9,8},{10,11... | collective-permute-start | bytes 12582920 | tf_op jit(solution)/shard_map/ppermute | solution.py:958
  273.7 48.1 %collective-permute-start.33 = (bf16[2,2,256,1024]{3,2,1,0:T(8,128)(2,1)}, bf16[2,2,256,1024]{3,2,1,0:T(8,128)(2,1)S(1)}, u32[]{:S(2)}, u32[]{:S(2)}) collective-permute-start(bf16[2,2,256,1024]{3,2,1,0:T(8,128)(2,1)} %get-tuple-element.166), channel_id=1, source_target_pairs={{8,0},{0,8},{24,16},{16,24},{9,1},{1,9},{25,17},{17,25},{10,2},{2,... | collective-permute-start | bytes 6291464 | tf_op jit(solution)/shard_map/ppermute | solution.py:969
  274.6 47.6 %collective-permute-start.34 = (bf16[2,2,256,1024]{3,2,1,0:T(8,128)(2,1)S(1)}, bf16[2,2,256,1024]{3,2,1,0:T(8,128)(2,1)S(1)}, u32[]{:S(2)}, u32[]{:S(2)}) collective-permute-start(bf16[2,2,256,1024]{3,2,1,0:T(8,128)(2,1)S(1)} %copy-done.115), channel_id=1, source_target_pairs={{16,0},{24,8},{0,16},{8,24},{17,1},{25,9},{1,17},{9,25},{18,2},{26... | collective-permute-start | bytes 6291464 | tf_op jit(solution)/shard_map/ppermute | solution.py:969
  341.2 67.3 %collective-permute-start.35 = (bf16[4,512,1024]{2,1,0:T(8,128)(2,1)}, bf16[4,512,1024]{2,1,0:T(8,128)(2,1)S(1)}, u32[]{:S(2)}, u32[]{:S(2)}) collective-permute-start(bf16[4,512,1024]{2,1,0:T(8,128)(2,1)} %shard_map.341.refs_0_), channel_id=1, source_target_pairs={{0,1},{1,0},{2,3},{3,2},{4,5},{5,4},{6,7},{7,6},{8,9},{9,8},{10,11... | collective-permute-start | bytes 12582920 | tf_op jit(solution)/shard_map/ppermute | solution.py:958
  341.3 26.0 %collective-permute-start.38 = (bf16[2,256,1024]{2,1,0:T(8,128)(2,1)S(1)}, bf16[2,256,1024]{2,1,0:T(8,128)(2,1)S(1)}, u32[]{:S(2)}, u32[]{:S(2)}) collective-permute-start(bf16[2,256,1024]{2,1,0:T(8,128)(2,1)S(1)} %copy-done.78), channel_id=1, source_target_pairs={{8,0},{0,8},{24,16},{16,24},{9,1},{1,9},{25,17},{17,25},{10,2},{2,... | collective-permute-start | bytes 3145736 | tf_op jit(solution)/shard_map/ppermute | solution.py:969
  342.2 26.3 %collective-permute-start.39 = (bf16[2,256,1024]{2,1,0:T(8,128)(2,1)}, bf16[2,256,1024]{2,1,0:T(8,128)(2,1)}, u32[]{:S(2)}, u32[]{:S(2)}) collective-permute-start(bf16[2,256,1024]{2,1,0:T(8,128)(2,1)} %get-tuple-element.173), channel_id=1, source_target_pairs={{16,0},{24,8},{0,16},{8,24},{17,1},{25,9},{1,17},{9,25},{18,2},{26... | collective-permute-start | bytes 3145736 | tf_op jit(solution)/shard_map/ppermute | solution.py:969
  343.8 45.5 %collective-permute-start.36 = (bf16[1,2,256,1024]{3,2,1,0:T(8,128)(2,1)}, bf16[1,2,256,1024]{3,2,1,0:T(8,128)(2,1)S(1)}, u32[]{:S(2)}, u32[]{:S(2)}) collective-permute-start(bf16[1,2,256,1024]{3,2,1,0:T(8,128)(2,1)} %get-tuple-element.171), channel_id=1, source_target_pairs={{8,0},{0,8},{24,16},{16,24},{9,1},{1,9},{25,17},{17,25},{10,2},{2,... | collective-permute-start | bytes 3145736 | tf_op jit(solution)/shard_map/ppermute | solution.py:969
  344.9 45.3 %collective-permute-start.37 = (bf16[1,2,256,1024]{3,2,1,0:T(8,128)(2,1)}, bf16[1,2,256,1024]{3,2,1,0:T(8,128)(2,1)S(1)}, u32[]{:S(2)}, u32[]{:S(2)}) collective-permute-start(bf16[1,2,256,1024]{3,2,1,0:T(8,128)(2,1)} %get-tuple-element.172), channel_id=1, source_target_pairs={{16,0},{24,8},{0,16},{8,24},{17,1},{25,9},{1,17},{9,25},{18,2},{26... | collective-permute-start | bytes 3145736 | tf_op jit(solution)/shard_map/ppermute | solution.py:969
  397.3 44.3 %collective-permute-start.45 = (bf16[2,128,1024]{2,1,0:T(8,128)(2,1)}, bf16[2,128,1024]{2,1,0:T(8,128)(2,1)S(1)}, u32[]{:S(2)}, u32[]{:S(2)}) collective-permute-start(bf16[2,128,1024]{2,1,0:T(8,128)(2,1)} %get-tuple-element.182), channel_id=1, source_target_pairs={{4,0},{5,1},{6,2},{7,3},{0,4},{1,5},{2,6},{3,7},{12,8},{13,9},{14,... | collective-permute-start | bytes 1572872 | tf_op jit(solution)/shard_map/ppermute | solution.py:966
  407.4 34.1 %collective-permute-start.46 = (bf16[2,128,1024]{2,1,0:T(8,128)(2,1)}, bf16[2,128,1024]{2,1,0:T(8,128)(2,1)S(1)}, u32[]{:S(2)}, u32[]{:S(2)}) collective-permute-start(bf16[2,128,1024]{2,1,0:T(8,128)(2,1)} %get-tuple-element.183), channel_id=1, source_target_pairs={{6,0},{7,1},{0,2},{1,3},{2,4},{3,5},{4,6},{5,7},{14,8},{15,9},{8,1... | collective-permute-start | bytes 1572872 | tf_op jit(solution)/shard_map/ppermute | solution.py:966
  446.2 25.3 %collective-permute-start.50 = (bf16[128,1024]{1,0:T(8,128)(2,1)}, bf16[128,1024]{1,0:T(8,128)(2,1)S(1)}, u32[]{:S(2)}, u32[]{:S(2)}) collective-permute-start(bf16[128,1024]{1,0:T(8,128)(2,1)} %get-tuple-element.191), channel_id=1, source_target_pairs={{4,0},{5,1},{6,2},{7,3},{0,4},{1,5},{2,6},{3,7},{12,8},{13,9},{14,... | collective-permute-start | bytes 786440 | tf_op jit(solution)/shard_map/ppermute | solution.py:966
  544.3 25.3 %collective-permute-start.67 = (bf16[256,1024]{1,0:T(8,128)(2,1)S(1)}, bf16[256,1024]{1,0:T(8,128)(2,1)S(1)}, u32[]{:S(2)}, u32[]{:S(2)}) collective-permute-start(bf16[256,1024]{1,0:T(8,128)(2,1)S(1)} %pad_maximum_fusion.4.q_ref), channel_id=1, source_target_pairs={{8,0},{0,8},{24,16},{16,24},{9,1},{1,9},{25,17},{17,25},{10,2},{2,... | collective-permute-start | bytes 1572872 | tf_op jit(solution)/shard_map/ppermute | solution.py:969
  549.0 87.5 %collective-permute-start.72 = (bf16[4,128,1024]{2,1,0:T(8,128)(2,1)S(1)}, bf16[4,128,1024]{2,1,0:T(8,128)(2,1)S(1)}, u32[]{:S(2)}, u32[]{:S(2)}) collective-permute-start(bf16[4,128,1024]{2,1,0:T(8,128)(2,1)S(1)} %constant_dynamic-update-slice_fusion.8.refs_0_), channel_id=1, source_target_pairs={{8,0},{0,8},{24,16},{16,24},{9,1},{1,9},{25,17},{17,25},{10,2},{2,... | collective-permute-start | bytes 3145736 | tf_op jit(solution)/shard_map/ppermute | solution.py:969
  566.6 67.9 %collective-permute-start.73 = (bf16[4,128,1024]{2,1,0:T(8,128)(2,1)S(1)}, bf16[4,128,1024]{2,1,0:T(8,128)(2,1)S(1)}, u32[]{:S(2)}, u32[]{:S(2)}) collective-permute-start(bf16[4,128,1024]{2,1,0:T(8,128)(2,1)S(1)} %constant_dynamic-update-slice_fusion.8.refs_0_), channel_id=1, source_target_pairs={{16,0},{24,8},{0,16},{8,24},{17,1},{25,9},{1,17},{9,25},{18,2},{26... | collective-permute-start | bytes 3145736 | tf_op jit(solution)/shard_map/ppermute | solution.py:969
  568.6 72.4 %collective-permute-start.64 = (bf16[512,1024]{1,0:T(8,128)(2,1)}, bf16[512,1024]{1,0:T(8,128)(2,1)}, u32[]{:S(2)}, u32[]{:S(2)}) collective-permute-start(bf16[512,1024]{1,0:T(8,128)(2,1)} %constant_dynamic-update-slice_fusion.4.mine_ref), channel_id=1, source_target_pairs={{0,1},{1,0},{2,3},{3,2},{4,5},{5,4},{6,7},{7,6},{8,9},{9,8},{10,11... | collective-permute-start | bytes 3145736 | tf_op jit(solution)/shard_map/ppermute | solution.py:958
  569.7 26.8 %collective-permute-start.70 = (bf16[128,1024]{1,0:T(8,128)(2,1)S(1)}, bf16[128,1024]{1,0:T(8,128)(2,1)S(1)}, u32[]{:S(2)}, u32[]{:S(2)}) collective-permute-start(bf16[128,1024]{1,0:T(8,128)(2,1)S(1)} %slice.231), channel_id=1, source_target_pairs={{16,0},{24,8},{0,16},{8,24},{17,1},{25,9},{1,17},{9,25},{18,2},{26... | collective-permute-start | bytes 786440 | tf_op jit(solution)/shard_map/ppermute | solution.py:969
  635.4 51.6 %collective-permute-start.75 = (bf16[2,128,1024]{2,1,0:T(8,128)(2,1)}, bf16[2,128,1024]{2,1,0:T(8,128)(2,1)S(1)}, u32[]{:S(2)}, u32[]{:S(2)}) collective-permute-start(bf16[2,128,1024]{2,1,0:T(8,128)(2,1)} %slice.241), channel_id=1, source_target_pairs={{8,0},{0,8},{24,16},{16,24},{9,1},{1,9},{25,17},{17,25},{10,2},{2,... | collective-permute-start | bytes 1572872 | tf_op jit(solution)/shard_map/ppermute | solution.py:969
  666.5 35.8 %collective-permute-start.74 = (bf16[2,128,1024]{2,1,0:T(8,128)(2,1)}, bf16[2,128,1024]{2,1,0:T(8,128)(2,1)}, u32[]{:S(2)}, u32[]{:S(2)}) collective-permute-start(bf16[2,128,1024]{2,1,0:T(8,128)(2,1)} %slice.234), channel_id=1, source_target_pairs={{16,0},{24,8},{0,16},{8,24},{17,1},{25,9},{1,17},{9,25},{18,2},{26... | collective-permute-start | bytes 1572872 | tf_op jit(solution)/shard_map/ppermute | solution.py:969
  670.3 46.3 %collective-permute-start.83 = (bf16[2,128,1024]{2,1,0:T(8,128)(2,1)S(1)}, bf16[2,128,1024]{2,1,0:T(8,128)(2,1)}, u32[]{:S(2)}, u32[]{:S(2)}) collective-permute-start(bf16[2,128,1024]{2,1,0:T(8,128)(2,1)S(1)} %copy-done.35), channel_id=1, source_target_pairs={{8,0},{0,8},{24,16},{16,24},{9,1},{1,9},{25,17},{17,25},{10,2},{2,... | collective-permute-start | bytes 1572872 | tf_op jit(solution)/shard_map/ppermute | solution.py:969
  685.1 31.5 %collective-permute-start.84 = (bf16[2,128,1024]{2,1,0:T(8,128)(2,1)S(1)}, bf16[2,128,1024]{2,1,0:T(8,128)(2,1)}, u32[]{:S(2)}, u32[]{:S(2)}) collective-permute-start(bf16[2,128,1024]{2,1,0:T(8,128)(2,1)S(1)} %copy-done.35), channel_id=1, source_target_pairs={{16,0},{24,8},{0,16},{8,24},{17,1},{25,9},{1,17},{9,25},{18,2},{26... | collective-permute-start | bytes 1572872 | tf_op jit(solution)/shard_map/ppermute | solution.py:969
  687.1 33.3 %collective-permute-start.79 = (f32[2,3,1024]{2,1,0:T(4,128)S(1)}, f32[2,3,1024]{2,1,0:T(4,128)S(1)}, u32[]{:S(2)}, u32[]{:S(2)}) collective-permute-start(f32[2,3,1024]{2,1,0:T(4,128)S(1)} %add.172), channel_id=1, source_target_pairs={{2,0},{3,1},{4,2},{5,3},{6,4},{7,5},{0,6},{1,7},{10,8},{11,9},{12,... | collective-permute-start | bytes 73736 | tf_op jit(solution)/shard_map/ppermute | solution.py:966
  (179 other events, 1701.0 us)

commit v5 on v4

--- a/solution.py
+++ b/solution.py
@@ -1170,9 +1170,11 @@
     cross_stage = third_sums(cross_stage, wide_grads)
     self_stage, self_token = second_sums(self_stage, cross_stage[0])
 
-    def owned(grads_fresh):
+    def owned(grads_fresh, *waited):
         mine, *sent = grads_fresh[1:]
         arrived = [from_chip(sent[turn - 1], turn) for turn in range(1, chips)]
+        if waited:
+            mine = held_until(mine, *waited)
         mine = jnp.concatenate([mine, *arrived])
         return mine, swap(mine)
 
@@ -1207,13 +1209,13 @@
         gram_token,
     )
     square_grads = square_fresh[0]
-    square_own = owned(square_fresh)
-    grads = jnp.concatenate([wide_grads, square_grads])
+    square_own = owned(square_fresh, *quarters[3:])
+    grads = held_until(jnp.concatenate([wide_grads, square_grads]), *quarters[3:])
     grads_x, grads_y = from_rep(grads, 1), from_rep(grads, 2)
     wide_rows = gram_schulz(place_now, quarters, *wide_own, rows, square_grads)
     wide_orth = to_both(wide_rows)
     wide_orth_shared = share_pair(wide_orth)
-    square_rows = square_schulz(*square_own, rows, wide_orth, grads_x, grads_y)
+    square_rows = square_schulz(*square_own, rows, wide_orth)
     grads_across = [from_rep(grads_y[:2], 1), from_rep(grads_x[2:], 2)]
     late_sq = held_until(grad_sq, square_rows)
     late_ck = held_until(grad_ck, square_rows)

time: 761 us -> 769 us (1.011)
    ppermute x44, waiting for transfers between devices: 122 us -> 132 us  [from_rep(): lax.ppermute(values, 'rep', [(index ^ step, index) for index in range(rep...]
    unnamed x258 -> x276, local copies, waits for them, and re-layouts: 33.4 us -> 32.3 us
  transfers between devices with their start and end apart: 91 -> 91, of which waited for: 39 -> 40; matrix products, arithmetic and copies ran while one was open for 13% -> 13% of each run, Pallas kernels for 23% -> 22%
where the time goes in v5:
time: 769 us; the launch traced here: 764 us
  waiting for transfers between devices  286 us (37%)
  Pallas kernels  260 us (34%)
  starting transfers between devices  85.4 us (11%)
  local copies, waits for them, and re-layouts  49.9 us (6%)
  other arithmetic  43.9 us (6%)
  matrix products  35.5 us (5%)
    ppermute x32, waiting for transfers between devices, from_chip(): return lax.ppermute(values, 'shard', pairs)  150 us
    ppermute x44, waiting for transfers between devices, from_rep(): lax.ppermute(values, 'rep', [(index ^ step, index) for index in range(rep...  132 us
    ppermute x44, starting transfers between devices, from_rep(): lax.ppermute(values, 'rep', [(index ^ step, index) for index in range(rep...  48.6 us
    pallas_call x4, Pallas kernels, attention_call(): pl.pallas_call(kernel, out_shape=tuple(out_shapes), in_specs=[pl.BlockSpe...  47.2 us
    pallas_call x7, Pallas kernels, weight_rows(): pl.pallas_call(kernel, out_shape=tuple(out_shapes), in_specs=[pl.BlockSpe...  46.5 us
    ppermute x32, starting transfers between devices, from_chip(): return lax.ppermute(values, 'shard', pairs)  34.9 us
    pallas_call x1, Pallas kernels, gram_schulz(): pl.pallas_call(kernel, out_shape=low(2, rows, size), in_specs=[pl.BlockSp...  33.8 us
    unnamed x276, local copies, waits for them, and re-layouts  32.3 us
  transfers between devices with their start and end apart: 91, of which 40 were waited for; matrix products, arithmetic and copies ran while one was open for 13% of the time, Pallas kernels for 22%

profile of v5, /device:TPU:0, one launch (start us, length us, event | category | flops | bytes accessed | tf_op | source)
XLA Modules:
  0.0 763.6 jit_solution(12033090611156669950)
XLA Ops:
  1.3 7.9 %shard_map.318 = (bf16[4,4,128,1024]{3,2,1,0:T(8,128)(2,1)}, bf16[128,1024]{1,0:T(8,128)(2,1)}, bf16[128,1024]{1,0:T(8,128)(2,1)}, bf16[128,1024]{1,0:T(8,128)(2...) custom-call(s32[4]{0:T(128)} %pad_add_fusion.place_ref, f32[4,128,1024]{2,1,0:T(8,128)} %refs_0_.1, ...), custom_call_target="tpu_custom_call" | custom-call | flops 1024 | bytes 1024 | tf_op jit(solution)/shard_map/pallas_call | solution.py:871
  22.3 16.3 %collective-permute-done.1.refs_1_ = bf16[128,1024]{1,0:T(8,128)(2,1)S(1)} collective-permute-done((bf16[128,1024]{1,0:T(8,128)(2,1)S(1)}, bf16[128,1024]{1,0:T(8,128)(2,1)S(1)}, u32[]{:S(2)}, u32[]{:S(2)}) %collective-permute-start.1) | collective-permute-done | bytes 262176 | tf_op jit(solution)/shard_map/ppermute | solution.py:966
  52.5 12.0 %collective-permute-done.6.refs_1_ = bf16[128,1024]{1,0:T(8,128)(2,1)S(1)} collective-permute-done((bf16[128,1024]{1,0:T(8,128)(2,1)}, bf16[128,1024]{1,0:T(8,128)(2,1)S(1)}, u32[]{:S(2)}, u32[]{:S(2)}) %collective-permute-start.6) | collective-permute-done | bytes 262176 | tf_op jit(solution)/shard_map/ppermute | solution.py:966
  64.5 10.2 %collective-permute-done.7.refs_2_ = bf16[128,1024]{1,0:T(8,128)(2,1)S(1)} collective-permute-done((bf16[128,1024]{1,0:T(8,128)(2,1)}, bf16[128,1024]{1,0:T(8,128)(2,1)S(1)}, u32[]{:S(2)}, u32[]{:S(2)}) %collective-permute-start.7) | collective-permute-done | bytes 262176 | tf_op jit(solution)/shard_map/ppermute | solution.py:966
  83.8 8.8 %collective-permute-done.13.refs_0_ = bf16[128,1024]{1,0:T(8,128)(2,1)S(1)} collective-permute-done((bf16[128,1024]{1,0:T(8,128)(2,1)}, bf16[128,1024]{1,0:T(8,128)(2,1)S(1)}, u32[]{:S(2)}, u32[]{:S(2)}) %collective-permute-start.13) | collective-permute-done | bytes 262176 | tf_op jit(solution)/shard_map/ppermute | solution.py:966
  92.6 13.7 %collective-permute-done.14.refs_1_ = bf16[128,1024]{1,0:T(8,128)(2,1)S(1)} collective-permute-done((bf16[128,1024]{1,0:T(8,128)(2,1)}, bf16[128,1024]{1,0:T(8,128)(2,1)S(1)}, u32[]{:S(2)}, u32[]{:S(2)}) %collective-permute-start.14) | collective-permute-done | bytes 262176 | tf_op jit(solution)/shard_map/ppermute | solution.py:966
  124.5 7.8 %shard_map.324 = (bf16[4,2,128,1024]{3,2,1,0:T(8,128)(2,1)}, bf16[4,2,128,1024]{3,2,1,0:T(8,128)(2,1)}, bf16[4,2,128,1024]{3,2,1,0:T(8,128)(2,1)}, bf16[4,2,128,1024]{3,2,1,0:T(8,128)(2,1)}) custom-call(s32[4]{0:T(128)} %pad_add_fusion.place_ref, bf16[4,4,128,1024]{3,2,1,0:T(8,128)(2,1)} %get-tuple-element.118.refs_3_.refs_0_.refs_12_, ...), custom_call_target="tpu_custom_call" | custom-call | flops 1024 | bytes 1024 | tf_op jit(solution)/shard_map/pallas_call | solution.py:740
  156.1 9.6 %shard_map.325.refs_1_ = bf16[256,1024]{1,0:T(8,128)(2,1)} custom-call(s32[1]{0:T(128)S(6)} %copy.87.count_ref, bf16[256,1024]{1,0:T(8,128)(2,1)} %convolution_convert_fusion.6.query_ref.refs_5_, bf16[256,1024]{1,0:T(8,128)(2,1)} %convolution_convert_fusion.5.key_ref.refs_6_, bf16[256,1024]{1,0:T(8,128)(2,1)} %convolution_convert_fusion.4.value_ref.refs_7_), custom_call_target="tpu_custom_call" | custom-call | flops 1024 | bytes 1024 | tf_op jit(solution)/shard_map/pallas_call | solution.py:86
  170.8 7.7 %shard_map.328 = (bf16[4,2,128,1024]{3,2,1,0:T(8,128)(2,1)}, bf16[4,2,128,1024]{3,2,1,0:T(8,128)(2,1)}, bf16[4,2,128,1024]{3,2,1,0:T(8,128)(2,1)}, bf16[4,2,128,1024]{3,2,1,0:T(8,128)(2,1)}) custom-call(s32[4]{0:T(128)} %pad_add_fusion.place_ref, bf16[4,4,128,1024]{3,2,1,0:T(8,128)(2,1)} %get-tuple-element.118.refs_3_.refs_0_.refs_12_, ...), custom_call_target="tpu_custom_call" | custom-call | flops 1024 | bytes 1024 | tf_op jit(solution)/shard_map/pallas_call | solution.py:740
  192.7 10.5 %shard_map.329.refs_2_ = bf16[256,1024]{1,0:T(8,128)(2,1)} custom-call(s32[1]{0:T(128)S(6)} %copy.88.count_ref, bf16[256,1024]{1,0:T(8,128)(2,1)} %convolution_convert_fusion.3.query_ref, bf16[384,1024]{1,0:T(8,128)(2,1)} %fusion.3.key_ref.refs_2_, bf16[384,1024]{1,0:T(8,128)(2,1)} %fusion.4.value_ref.refs_3_), custom_call_target="tpu_custom_call" | custom-call | flops 1024 | bytes 1024 | tf_op jit(solution)/shard_map/pallas_call | solution.py:86
  209.4 17.7 %shard_map.331 = (f32[256,1024]{1,0:T(8,128)}, f32[256,1024]{1,0:T(8,128)}, bf16[256,1024]{1,0:T(8,128)(2,1)}, bf16[256,1024]{1,0:T(8,128)(2,1)}, bf16[256,1024]...) custom-call(s32[4]{0:T(128)} %pad_add_fusion.place_ref, ...), custom_call_target="tpu_custom_call" | custom-call | flops 1024 | bytes 1024 | tf_op jit(solution)/shard_map/pallas_call | solution.py:810
  241.4 14.2 %shard_map.332 = (bf16[256,1024]{1,0:T(8,128)(2,1)}, bf16[384,1024]{1,0:T(8,128)(2,1)}, bf16[384,1024]{1,0:T(8,128)(2,1)}) custom-call(s32[1]{0:T(128)S(6)} %copy.88.count_ref, bf16[256,1024]{1,0:T(8,128)(2,1)} %convolution_convert_fusion.3.query_ref, bf16[384,1024]{1,0:T(8,128)(2,1)} %fusion.3.key_ref.refs_2_, bf16[384,1024]{1,0:T(8,128)(2,1)} %fusion.4.value_ref.refs_3_, ...), custom_call_target="tpu_custom_call" | custom-call | flops 1024 | bytes 1024 | tf_op jit(solution)/shard_map/pallas_call | solution.py:86
  255.6 10.5 %shard_map.335 = (bf16[2,2,256,1024]{3,2,1,0:T(8,128)(2,1)}, bf16[2,2,256,1024]{3,2,1,0:T(8,128)(2,1)}, bf16[2,2,256,1024]{3,2,1,0:T(8,128)(2,1)}, bf16[2,2,256,1024]{3,2,1,0:T(8,128)(2,1)}) custom-call(s32[4]{0:T(128)} %pad_add_fusion.place_ref, bf16[256,1024]{1,0:T(8,128)(2,1)} %add_convert_fusion.1.third_ref.refs_0_, ...), custom_call_target="tpu_custom_call" | custom-call | flops 1024 | bytes 1024 | tf_op jit(solution)/shard_map/pallas_call | solution.py:502
  281.8 13.0 %shard_map.338 = (bf16[256,1024]{1,0:T(8,128)(2,1)}, bf16[256,1024]{1,0:T(8,128)(2,1)}, bf16[256,1024]{1,0:T(8,128)(2,1)}) custom-call(s32[1]{0:T(128)S(6)} %copy.87.count_ref, bf16[256,1024]{1,0:T(8,128)(2,1)} %convolution_convert_fusion.6.query_ref.refs_5_, bf16[256,1024]{1,0:T(8,128)(2,1)} %convolution_convert_fusion.5.key_ref.refs_6_, ...), custom_call_target="tpu_custom_call" | custom-call | flops 1024 | bytes 1024 | tf_op jit(solution)/shard_map/pallas_call | solution.py:86
  294.7 25.9 %collective-permute-done.33.x_ref = bf16[2,2,256,1024]{3,2,1,0:T(8,128)(2,1)S(1)} collective-permute-done((bf16[2,2,256,1024]{3,2,1,0:T(8,128)(2,1)}, bf16[2,2,256,1024]{3,2,1,0:T(8,128)(2,1)S(1)}, u32[]{:S(2)}, u32[]{:S(2)}) %collective-permute-start.33) | collective-permute-done | bytes 2097184 | tf_op jit(solution)/shard_map/ppermute | solution.py:969
  327.2 7.5 shard_map.340
  344.2 21.9 %collective-permute-done.38.last_x_ref = bf16[2,256,1024]{2,1,0:T(8,128)(2,1)S(1)} collective-permute-done((bf16[2,256,1024]{2,1,0:T(8,128)(2,1)S(1)}, bf16[2,256,1024]{2,1,0:T(8,128)(2,1)S(1)}, u32[]{:S(2)}, u32[]{:S(2)}) %collective-permute-start.38) | collective-permute-done | bytes 1048608 | tf_op jit(solution)/shard_map/ppermute | solution.py:969
  374.7 13.4 %collective-permute-done.36.x_ref = bf16[1,2,256,1024]{3,2,1,0:T(8,128)(2,1)S(1)} collective-permute-done((bf16[1,2,256,1024]{3,2,1,0:T(8,128)(2,1)}, bf16[1,2,256,1024]{3,2,1,0:T(8,128)(2,1)S(1)}, u32[]{:S(2)}, u32[]{:S(2)}) %collective-permute-start.36) | collective-permute-done | bytes 1048608 | tf_op jit(solution)/shard_map/ppermute | solution.py:969
  396.0 10.4 %collective-permute-done.40.refs_8_.last_x_ref = bf16[1,256,1024]{2,1,0:T(8,128)(2,1)S(1)} collective-permute-done((bf16[1,256,1024]{2,1,0:T(8,128)(2,1)}, bf16[1,256,1024]{2,1,0:T(8,128)(2,1)S(1)}, u32[]{:S(2)}, u32[]{:S(2)}) %collective-permute-start.40) | collective-permute-done | bytes 524320 | tf_op jit(solution)/shard_map/ppermute | solution.py:969
  408.1 6.6 shard_map.344
  414.7 25.5 %collective-permute-done.45.refs_1_ = bf16[2,128,1024]{2,1,0:T(8,128)(2,1)S(1)} collective-permute-done((bf16[2,128,1024]{2,1,0:T(8,128)(2,1)S(1)}, bf16[2,128,1024]{2,1,0:T(8,128)(2,1)S(1)}, u32[]{:S(2)}, u32[]{:S(2)}) %collective-permute-start.45) | collective-permute-done | bytes 524320 | tf_op jit(solution)/shard_map/ppermute | solution.py:966
  452.1 17.9 %collective-permute-done.50 = bf16[128,1024]{1,0:T(8,128)(2,1)S(1)} collective-permute-done((bf16[128,1024]{1,0:T(8,128)(2,1)}, bf16[128,1024]{1,0:T(8,128)(2,1)S(1)}, u32[]{:S(2)}, u32[]{:S(2)}) %collective-permute-start.50) | collective-permute-done | bytes 262176 | tf_op jit(solution)/shard_map/ppermute | solution.py:966
  479.7 6.3 shard_map.348
  488.5 11.7 %collective-permute-done.59.x_ref = bf16[1,2,128,1024]{3,2,1,0:T(8,128)(2,1)S(1)} collective-permute-done((bf16[1,2,128,1024]{3,2,1,0:T(8,128)(2,1)}, bf16[1,2,128,1024]{3,2,1,0:T(8,128)(2,1)S(1)}, u32[]{:S(2)}, u32[]{:S(2)}) %collective-permute-start.59) | collective-permute-done | bytes 524320 | tf_op jit(solution)/shard_map/ppermute | solution.py:969
  516.7 11.9 %collective-permute-done.54.refs_2_ = bf16[1,128,1024]{2,1,0:T(8,128)(2,1)S(1)} collective-permute-done((bf16[1,128,1024]{2,1,0:T(8,128)(2,1)}, bf16[1,128,1024]{2,1,0:T(8,128)(2,1)S(1)}, u32[]{:S(2)}, u32[]{:S(2)}) %collective-permute-start.54) | collective-permute-done | bytes 262176 | tf_op jit(solution)/shard_map/ppermute | solution.py:966
  549.5 7.2 collective-permute-done.57
  562.0 7.2 collective-permute-start.67
  570.6 33.8 %shard_map.353 = bf16[2,128,1024]{2,1,0:T(8,128)(2,1)} custom-call(s32[4]{0:T(128)} %pad_add_fusion.place_ref, bf16[256,1024]{1,0:T(8,128)(2,1)} %copy-done.74, bf16[256,1024]{1,0:T(8,128)(2,1)} %copy-done.80, bf16[256,1024]{1,0:T(8,128)(2,1)} %copy-done.79, bf16[128,1024]{1,0:T(8,128)(2,1)} %copy-done.64, bf16[128,1024]{1,0:T(8,128)(2,1)} %copy-done.65, ...), custom_call_target="tpu_custom_call" | custom-call | flops 1024 | bytes 1024 | tf_op jit(solution)/shard_map/pallas_call | solution.py:380
  610.7 8.1 %collective-permute-done.71 = bf16[128,1024]{1,0:T(8,128)(2,1)S(1)} collective-permute-done((bf16[128,1024]{1,0:T(8,128)(2,1)S(1)}, bf16[128,1024]{1,0:T(8,128)(2,1)S(1)}, u32[]{:S(2)}, u32[]{:S(2)}) %collective-permute-start.71) | collective-permute-done | bytes 262176 | tf_op jit(solution)/shard_map/ppermute | solution.py:966
  627.0 20.0 %collective-permute-done.84.refs_2_ = bf16[2,128,1024]{2,1,0:T(8,128)(2,1)S(1)} collective-permute-done((bf16[2,128,1024]{2,1,0:T(8,128)(2,1)S(1)}, bf16[2,128,1024]{2,1,0:T(8,128)(2,1)S(1)}, u32[]{:S(2)}, u32[]{:S(2)}) %collective-permute-start.84) | collective-permute-done | bytes 524320 | tf_op jit(solution)/shard_map/ppermute | solution.py:969
  649.1 25.5 %shard_map.354.refs_1_ = bf16[2,128,1024]{2,1,0:T(8,128)(2,1)} custom-call(bf16[512,1024]{1,0:T(8,128)(2,1)} %copy-done.44, bf16[512,1024]{1,0:T(8,128)(2,1)} %collective-permute-done.70.sibling_ref, bf16[2,128,1024]{2,1,0:T(8,128)(2,1)} %copy-done.29), custom_call_target="tpu_custom_call" | custom-call | flops 1024 | bytes 1024 | tf_op jit(solution)/shard_map/pallas_call | solution.py:233
  729.6 7.5 collective-permute-done.85.refs_2_
  (560 shorter events, 331.9 us)
Async XLA Ops:
  9.3 65.4 %collective-permute-start.8 = (bf16[4,4,128,1024]{3,2,1,0:T(8,128)(2,1)}, bf16[4,4,128,1024]{3,2,1,0:T(8,128)(2,1)}, u32[]{:S(2)}, u32[]{:S(2)}) collective-permute-start(bf16[4,4,128,1024]{3,2,1,0:T(8,128)(2,1)} %get-tuple-element.118.refs_3_.refs_0_.refs_12_), channel_id=1, source_target_pairs={{0,1},{1,0},{2,3},{3,2},{4,5},{5,4},{6,7},{7,6},{8,9},{9,8},{10,11... | collective-permute-start | bytes 12582920 | tf_op jit(solution)/shard_map/ppermute | solution.py:958
  42.6 32.1 %collective-permute-start.9 = (bf16[384,1024]{1,0:T(8,128)(2,1)}, bf16[384,1024]{1,0:T(8,128)(2,1)S(1)}, u32[]{:S(2)}, u32[]{:S(2)}) collective-permute-start(bf16[384,1024]{1,0:T(8,128)(2,1)} %get-tuple-element.122.refs_1_), channel_id=1, source_target_pairs={{0,1},{1,0},{2,3},{3,2},{4,5},{5,4},{6,7},{7,6},{8,9},{9,8},{10,11... | collective-permute-start | bytes 2359304 | tf_op jit(solution)/shard_map/ppermute | solution.py:958
  42.6 32.1 %collective-permute-start.3 = (bf16[384,1024]{1,0:T(8,128)(2,1)}, bf16[384,1024]{1,0:T(8,128)(2,1)S(1)}, u32[]{:S(2)}, u32[]{:S(2)}) collective-permute-start(bf16[384,1024]{1,0:T(8,128)(2,1)} %get-tuple-element.119.refs_1_), channel_id=1, source_target_pairs={{8,0},{0,8},{24,16},{16,24},{9,1},{1,9},{25,17},{17,25},{10,2},{2,... | collective-permute-start | bytes 2359304 | tf_op jit(solution)/shard_map/ppermute | solution.py:969
  44.1 30.6 %collective-permute-start.4 = (bf16[384,1024]{1,0:T(8,128)(2,1)}, bf16[384,1024]{1,0:T(8,128)(2,1)S(1)}, u32[]{:S(2)}, u32[]{:S(2)}) collective-permute-start(bf16[384,1024]{1,0:T(8,128)(2,1)} %get-tuple-element.120), channel_id=1, source_target_pairs={{16,0},{24,8},{0,16},{8,24},{17,1},{25,9},{1,17},{9,25},{18,2},{26... | collective-permute-start | bytes 2359304 | tf_op jit(solution)/shard_map/ppermute | solution.py:969
  80.2 29.8 %collective-permute-start.12 = (bf16[1152,1024]{1,0:T(8,128)(2,1)}, bf16[1152,1024]{1,0:T(8,128)(2,1)S(1)}, u32[]{:S(2)}, u32[]{:S(2)}) collective-permute-start(bf16[1152,1024]{1,0:T(8,128)(2,1)} %get-tuple-element.125.refs_1_), channel_id=1, source_target_pairs={{0,1},{1,0},{2,3},{3,2},{4,5},{5,4},{6,7},{7,6},{8,9},{9,8},{10,11... | collective-permute-start | bytes 7077896 | tf_op jit(solution)/shard_map/ppermute | solution.py:958
  80.2 28.6 %collective-permute-start.10 = (bf16[576,1024]{1,0:T(8,128)(2,1)}, bf16[576,1024]{1,0:T(8,128)(2,1)S(1)}, u32[]{:S(2)}, u32[]{:S(2)}) collective-permute-start(bf16[576,1024]{1,0:T(8,128)(2,1)} %get-tuple-element.123.refs_1_), channel_id=1, source_target_pairs={{8,0},{0,8},{24,16},{16,24},{9,1},{1,9},{25,17},{17,25},{10,2},{2,... | collective-permute-start | bytes 3538952 | tf_op jit(solution)/shard_map/ppermute | solution.py:969
  81.7 28.3 %collective-permute-start.11 = (bf16[576,1024]{1,0:T(8,128)(2,1)}, bf16[576,1024]{1,0:T(8,128)(2,1)S(1)}, u32[]{:S(2)}, u32[]{:S(2)}) collective-permute-start(bf16[576,1024]{1,0:T(8,128)(2,1)} %get-tuple-element.124), channel_id=1, source_target_pairs={{16,0},{24,8},{0,16},{8,24},{17,1},{25,9},{1,17},{9,25},{18,2},{26... | collective-permute-start | bytes 3538952 | tf_op jit(solution)/shard_map/ppermute | solution.py:969
  117.3 28.7 %collective-permute-start.17 = (bf16[576,1024]{1,0:T(8,128)(2,1)}, bf16[576,1024]{1,0:T(8,128)(2,1)S(1)}, u32[]{:S(2)}, u32[]{:S(2)}) collective-permute-start(bf16[576,1024]{1,0:T(8,128)(2,1)} %get-tuple-element.132.refs_1_), channel_id=1, source_target_pairs={{8,0},{0,8},{24,16},{16,24},{9,1},{1,9},{25,17},{17,25},{10,2},{2,... | collective-permute-start | bytes 3538952 | tf_op jit(solution)/shard_map/ppermute | solution.py:969
  118.1 28.3 %collective-permute-start.18 = (bf16[576,1024]{1,0:T(8,128)(2,1)}, bf16[576,1024]{1,0:T(8,128)(2,1)S(1)}, u32[]{:S(2)}, u32[]{:S(2)}) collective-permute-start(bf16[576,1024]{1,0:T(8,128)(2,1)} %get-tuple-element.133), channel_id=1, source_target_pairs={{16,0},{24,8},{0,16},{8,24},{17,1},{25,9},{1,17},{9,25},{18,2},{26... | collective-permute-start | bytes 3538952 | tf_op jit(solution)/shard_map/ppermute | solution.py:969
  152.5 31.5 %collective-permute-start.23 = (bf16[576,1024]{1,0:T(8,128)(2,1)}, bf16[576,1024]{1,0:T(8,128)(2,1)S(1)}, u32[]{:S(2)}, u32[]{:S(2)}) collective-permute-start(bf16[576,1024]{1,0:T(8,128)(2,1)} %get-tuple-element.140.refs_13_), channel_id=1, source_target_pairs={{8,0},{0,8},{24,16},{16,24},{9,1},{1,9},{25,17},{17,25},{10,2},{2,... | collective-permute-start | bytes 3538952 | tf_op jit(solution)/shard_map/ppermute | solution.py:969
  153.3 30.8 %collective-permute-start.24 = (bf16[576,1024]{1,0:T(8,128)(2,1)}, bf16[576,1024]{1,0:T(8,128)(2,1)S(1)}, u32[]{:S(2)}, u32[]{:S(2)}) collective-permute-start(bf16[576,1024]{1,0:T(8,128)(2,1)} %get-tuple-element.141), channel_id=1, source_target_pairs={{16,0},{24,8},{0,16},{8,24},{17,1},{25,9},{1,17},{9,25},{18,2},{26... | collective-permute-start | bytes 3538952 | tf_op jit(solution)/shard_map/ppermute | solution.py:969
  272.4 54.8 %collective-permute-start.32 = (bf16[4,512,1024]{2,1,0:T(8,128)(2,1)}, bf16[4,512,1024]{2,1,0:T(8,128)(2,1)}, u32[]{:S(2)}, u32[]{:S(2)}) collective-permute-start(bf16[4,512,1024]{2,1,0:T(8,128)(2,1)} %shard_map.336.refs_0_), channel_id=1, source_target_pairs={{0,1},{1,0},{2,3},{3,2},{4,5},{5,4},{6,7},{7,6},{8,9},{9,8},{10,11... | collective-permute-start | bytes 12582920 | tf_op jit(solution)/shard_map/ppermute | solution.py:958
  272.5 48.1 %collective-permute-start.33 = (bf16[2,2,256,1024]{3,2,1,0:T(8,128)(2,1)}, bf16[2,2,256,1024]{3,2,1,0:T(8,128)(2,1)S(1)}, u32[]{:S(2)}, u32[]{:S(2)}) collective-permute-start(bf16[2,2,256,1024]{3,2,1,0:T(8,128)(2,1)} %get-tuple-element.166), channel_id=1, source_target_pairs={{8,0},{0,8},{24,16},{16,24},{9,1},{1,9},{25,17},{17,25},{10,2},{2,... | collective-permute-start | bytes 6291464 | tf_op jit(solution)/shard_map/ppermute | solution.py:969
  273.6 47.6 %collective-permute-start.34 = (bf16[2,2,256,1024]{3,2,1,0:T(8,128)(2,1)S(1)}, bf16[2,2,256,1024]{3,2,1,0:T(8,128)(2,1)S(1)}, u32[]{:S(2)}, u32[]{:S(2)}) collective-permute-start(bf16[2,2,256,1024]{3,2,1,0:T(8,128)(2,1)S(1)} %copy-done.125), channel_id=1, source_target_pairs={{16,0},{24,8},{0,16},{8,24},{17,1},{25,9},{1,17},{9,25},{18,2},{26... | collective-permute-start | bytes 6291464 | tf_op jit(solution)/shard_map/ppermute | solution.py:969
  340.0 67.3 %collective-permute-start.35 = (bf16[4,512,1024]{2,1,0:T(8,128)(2,1)}, bf16[4,512,1024]{2,1,0:T(8,128)(2,1)}, u32[]{:S(2)}, u32[]{:S(2)}) collective-permute-start(bf16[4,512,1024]{2,1,0:T(8,128)(2,1)} %shard_map.341.refs_0_), channel_id=1, source_target_pairs={{0,1},{1,0},{2,3},{3,2},{4,5},{5,4},{6,7},{7,6},{8,9},{9,8},{10,11... | collective-permute-start | bytes 12582920 | tf_op jit(solution)/shard_map/ppermute | solution.py:958
  342.6 45.4 %collective-permute-start.36 = (bf16[1,2,256,1024]{3,2,1,0:T(8,128)(2,1)}, bf16[1,2,256,1024]{3,2,1,0:T(8,128)(2,1)S(1)}, u32[]{:S(2)}, u32[]{:S(2)}) collective-permute-start(bf16[1,2,256,1024]{3,2,1,0:T(8,128)(2,1)} %get-tuple-element.171), channel_id=1, source_target_pairs={{8,0},{0,8},{24,16},{16,24},{9,1},{1,9},{25,17},{17,25},{10,2},{2,... | collective-permute-start | bytes 3145736 | tf_op jit(solution)/shard_map/ppermute | solution.py:969
  343.5 45.6 %collective-permute-start.37 = (bf16[1,2,256,1024]{3,2,1,0:T(8,128)(2,1)S(1)}, bf16[1,2,256,1024]{3,2,1,0:T(8,128)(2,1)S(1)}, u32[]{:S(2)}, u32[]{:S(2)}) collective-permute-start(bf16[1,2,256,1024]{3,2,1,0:T(8,128)(2,1)S(1)} %copy-done.126), channel_id=1, source_target_pairs={{16,0},{24,8},{0,16},{8,24},{17,1},{25,9},{1,17},{9,25},{18,2},{26... | collective-permute-start | bytes 3145736 | tf_op jit(solution)/shard_map/ppermute | solution.py:969
  395.9 44.3 %collective-permute-start.45 = (bf16[2,128,1024]{2,1,0:T(8,128)(2,1)S(1)}, bf16[2,128,1024]{2,1,0:T(8,128)(2,1)S(1)}, u32[]{:S(2)}, u32[]{:S(2)}) collective-permute-start(bf16[2,128,1024]{2,1,0:T(8,128)(2,1)S(1)} %copy-done.128), channel_id=1, source_target_pairs={{4,0},{5,1},{6,2},{7,3},{0,4},{1,5},{2,6},{3,7},{12,8},{13,9},{14,... | collective-permute-start | bytes 1572872 | tf_op jit(solution)/shard_map/ppermute | solution.py:966
  406.4 33.8 %collective-permute-start.46 = (bf16[2,128,1024]{2,1,0:T(8,128)(2,1)S(1)}, bf16[2,128,1024]{2,1,0:T(8,128)(2,1)S(1)}, u32[]{:S(2)}, u32[]{:S(2)}) collective-permute-start(bf16[2,128,1024]{2,1,0:T(8,128)(2,1)S(1)} %copy-done.127), channel_id=1, source_target_pairs={{6,0},{7,1},{0,2},{1,3},{2,4},{3,5},{4,6},{5,7},{14,8},{15,9},{8,1... | collective-permute-start | bytes 1572872 | tf_op jit(solution)/shard_map/ppermute | solution.py:966
  516.0 27.9 %collective-permute-start.63 = (bf16[256,1024]{1,0:T(8,128)(2,1)S(1)}, bf16[256,1024]{1,0:T(8,128)(2,1)S(1)}, u32[]{:S(2)}, u32[]{:S(2)}) collective-permute-start(bf16[256,1024]{1,0:T(8,128)(2,1)S(1)} %pad_maximum_fusion.6.q_ref), channel_id=1, source_target_pairs={{16,0},{24,8},{0,16},{8,24},{17,1},{25,9},{1,17},{9,25},{18,2},{26... | collective-permute-start | bytes 1572872 | tf_op jit(solution)/shard_map/ppermute | solution.py:969
  562.0 46.8 %collective-permute-start.67 = (bf16[128,1024]{1,0:T(8,128)(2,1)}, bf16[128,1024]{1,0:T(8,128)(2,1)S(1)}, u32[]{:S(2)}, u32[]{:S(2)}) collective-permute-start(bf16[128,1024]{1,0:T(8,128)(2,1)} %get-tuple-element.208), channel_id=1, source_target_pairs={{2,0},{3,1},{4,2},{5,3},{6,4},{7,5},{0,6},{1,7},{10,8},{11,9},{12,... | collective-permute-start | bytes 786440 | tf_op jit(solution)/shard_map/ppermute | solution.py:966
  569.2 39.7 %collective-permute-start.68 = (bf16[128,1024]{1,0:T(8,128)(2,1)}, bf16[128,1024]{1,0:T(8,128)(2,1)S(1)}, u32[]{:S(2)}, u32[]{:S(2)}) collective-permute-start(bf16[128,1024]{1,0:T(8,128)(2,1)} %get-tuple-element.209), channel_id=1, source_target_pairs={{4,0},{5,1},{6,2},{7,3},{0,4},{1,5},{2,6},{3,7},{12,8},{13,9},{14,... | collective-permute-start | bytes 786440 | tf_op jit(solution)/shard_map/ppermute | solution.py:966
  569.2 39.7 %collective-permute-start.69 = (bf16[128,1024]{1,0:T(8,128)(2,1)}, bf16[128,1024]{1,0:T(8,128)(2,1)S(1)}, u32[]{:S(2)}, u32[]{:S(2)}) collective-permute-start(bf16[128,1024]{1,0:T(8,128)(2,1)} %get-tuple-element.210), channel_id=1, source_target_pairs={{6,0},{7,1},{0,2},{1,3},{2,4},{3,5},{4,6},{5,7},{14,8},{15,9},{8,1... | collective-permute-start | bytes 786440 | tf_op jit(solution)/shard_map/ppermute | solution.py:966
  609.9 39.2 %collective-permute-start.70 = (bf16[512,1024]{1,0:T(8,128)(2,1)S(1)}, bf16[512,1024]{1,0:T(8,128)(2,1)}, u32[]{:S(2)}, u32[]{:S(2)}) collective-permute-start(bf16[512,1024]{1,0:T(8,128)(2,1)S(1)} %pad_maximum_fusion.mine_ref), channel_id=1, source_target_pairs={{0,1},{1,0},{2,3},{3,2},{4,5},{5,4},{6,7},{7,6},{8,9},{9,8},{10,11... | collective-permute-start | bytes 3145736 | tf_op jit(solution)/shard_map/ppermute | solution.py:958
  610.0 66.6 %collective-permute-start.74 = (bf16[4,128,1024]{2,1,0:T(8,128)(2,1)}, bf16[4,128,1024]{2,1,0:T(8,128)(2,1)S(1)}, u32[]{:S(2)}, u32[]{:S(2)}) collective-permute-start(bf16[4,128,1024]{2,1,0:T(8,128)(2,1)} %shard_map.357.refs_0_), channel_id=1, source_target_pairs={{16,0},{24,8},{0,16},{8,24},{17,1},{25,9},{1,17},{9,25},{18,2},{26... | collective-permute-start | bytes 3145736 | tf_op jit(solution)/shard_map/ppermute | solution.py:969
  619.0 28.1 %collective-permute-start.84 = (bf16[2,128,1024]{2,1,0:T(8,128)(2,1)S(1)}, bf16[2,128,1024]{2,1,0:T(8,128)(2,1)S(1)}, u32[]{:S(2)}, u32[]{:S(2)}) collective-permute-start(bf16[2,128,1024]{2,1,0:T(8,128)(2,1)S(1)} %pad_maximum_fusion.7.refs_0_), channel_id=1, source_target_pairs={{16,0},{24,8},{0,16},{8,24},{17,1},{25,9},{1,17},{9,25},{18,2},{26... | collective-permute-start | bytes 1572872 | tf_op jit(solution)/shard_map/ppermute | solution.py:969
  623.2 51.4 %collective-permute-start.83 = (bf16[2,128,1024]{2,1,0:T(8,128)(2,1)S(1)}, bf16[2,128,1024]{2,1,0:T(8,128)(2,1)S(1)}, u32[]{:S(2)}, u32[]{:S(2)}) collective-permute-start(bf16[2,128,1024]{2,1,0:T(8,128)(2,1)S(1)} %pad_maximum_fusion.7.refs_0_), channel_id=1, source_target_pairs={{8,0},{0,8},{24,16},{16,24},{9,1},{1,9},{25,17},{17,25},{10,2},{2,... | collective-permute-start | bytes 1572872 | tf_op jit(solution)/shard_map/ppermute | solution.py:969
  626.3 55.7 %collective-permute-start.72 = (bf16[4,128,1024]{2,1,0:T(8,128)(2,1)S(1)}, bf16[4,128,1024]{2,1,0:T(8,128)(2,1)S(1)}, u32[]{:S(2)}, u32[]{:S(2)}) collective-permute-start(bf16[4,128,1024]{2,1,0:T(8,128)(2,1)S(1)} %copy-done.7), channel_id=1, source_target_pairs={{8,0},{0,8},{24,16},{16,24},{9,1},{1,9},{25,17},{17,25},{10,2},{2,... | collective-permute-start | bytes 3145736 | tf_op jit(solution)/shard_map/ppermute | solution.py:969
  647.8 91.0 %collective-permute-start.89 = (bf16[128,1024]{1,0:T(8,128)(2,1)}, bf16[128,1024]{1,0:T(8,128)(2,1)}, u32[]{:S(2)}, u32[]{:S(2)}) collective-permute-start(bf16[128,1024]{1,0:T(8,128)(2,1)} %slice_bitcast_fusion.2), channel_id=1, source_target_pairs={{8,0},{0,8},{24,16},{16,24},{9,1},{1,9},{25,17},{17,25},{10,2},{2,... | collective-permute-start | bytes 786440 | tf_op jit(solution)/shard_map/ppermute | solution.py:969
  683.0 33.2 %collective-permute-start.73 = (bf16[2,128,1024]{2,1,0:T(8,128)(2,1)}, bf16[2,128,1024]{2,1,0:T(8,128)(2,1)S(1)}, u32[]{:S(2)}, u32[]{:S(2)}) collective-permute-start(bf16[2,128,1024]{2,1,0:T(8,128)(2,1)} %slice.234), channel_id=1, source_target_pairs={{16,0},{24,8},{0,16},{8,24},{17,1},{25,9},{1,17},{9,25},{18,2},{26... | collective-permute-start | bytes 1572872 | tf_op jit(solution)/shard_map/ppermute | solution.py:969
  696.6 26.8 %collective-permute-start.79 = (f32[2,3,1024]{2,1,0:T(4,128)S(1)}, f32[2,3,1024]{2,1,0:T(4,128)S(1)}, u32[]{:S(2)}, u32[]{:S(2)}) collective-permute-start(f32[2,3,1024]{2,1,0:T(4,128)S(1)} %add.172), channel_id=1, source_target_pairs={{2,0},{3,1},{4,2},{5,3},{6,4},{7,5},{0,6},{1,7},{10,8},{11,9},{12,... | collective-permute-start | bytes 73736 | tf_op jit(solution)/shard_map/ppermute | solution.py:966
  725.8 26.8 %collective-permute-start.90 = (bf16[128,1024]{1,0:T(8,128)(2,1)S(1)}, bf16[128,1024]{1,0:T(8,128)(2,1)}, u32[]{:S(2)}, u32[]{:S(2)}) collective-permute-start(bf16[128,1024]{1,0:T(8,128)(2,1)S(1)} %copy-done.115), channel_id=1, source_target_pairs={{16,0},{24,8},{0,16},{8,24},{17,1},{25,9},{1,17},{9,25},{18,2},{26... | collective-permute-start | bytes 786440 | tf_op jit(solution)/shard_map/ppermute | solution.py:969
  (190 other events, 1921.3 us)

commit v6 on v4

--- a/solution.py
+++ b/solution.py
@@ -1035,11 +1035,11 @@
         cut = jnp.stack(pieces).reshape(reps, rows, shards, sub)
         return cut.transpose(1, 2, 0, 3).reshape(rows, hidden_width)
 
-    def prepare():
+    def prepare(first):
         matrices = [self_weights, cross_weights, fc_in, fc_out]
         moments = [self_moment, cross_moment, fc_in_moment, fc_out_moment]
         if sub % 128 == 0:
-            return prepared(place_now, matrices, moments, shards, sub, [])
+            return prepared(place_now, matrices, moments, shards, sub, first)
         whole = jnp.stack(
             [
                 self_weights.astype(jnp.bfloat16),
@@ -1055,9 +1055,11 @@
 
     state = {"by_x": [], "by_y": [], "came": [], "sent": []}
     state["arrived"] = first_blocks(of_rep(self_weights).astype(jnp.bfloat16))
-    state["shards"], state["quarters"], wide_moments, square_moments = prepare()
+    state["shards"], state["quarters"], wide_moments, square_moments = prepare(
+        state["arrived"]
+    )
     state["other_shards"] = swap(state["shards"])
-    run_phase(state, 0, [state["shards"]])
+    run_phase(state, 0, [])
     run_phase(state, 1, [state["other_shards"]])
     run_phase(state, 2, [])
     self_full = placed_blocks(place_now, shares_of(state, 0), 0, chips, [])

time: 761 us -> 764 us (level)
  transfers between devices with their start and end apart: 91 -> 91, of which waited for: 39 -> 40; matrix products, arithmetic and copies ran while one was open for 13% -> 13% of each run, Pallas kernels for 23% -> 23%
where the time goes in v6:
time: 764 us; the launch traced here: 759 us
  waiting for transfers between devices  276 us (36%)
  Pallas kernels  260 us (34%)
  starting transfers between devices  84 us (11%)
  local copies, waits for them, and re-layouts  55 us (7%)
  other arithmetic  46.1 us (6%)
  matrix products  34 us (4%)
    ppermute x32, waiting for transfers between devices, from_chip(): return lax.ppermute(values, 'shard', pairs)  151 us
    ppermute x44, waiting for transfers between devices, from_rep(): lax.ppermute(values, 'rep', [(index ^ step, index) for index in range(rep...  122 us
    ppermute x44, starting transfers between devices, from_rep(): lax.ppermute(values, 'rep', [(index ^ step, index) for index in range(rep...  48 us
    pallas_call x7, Pallas kernels, weight_rows(): pl.pallas_call(kernel, out_shape=tuple(out_shapes), in_specs=[pl.BlockSpe...  47 us
    pallas_call x4, Pallas kernels, attention_call(): pl.pallas_call(kernel, out_shape=tuple(out_shapes), in_specs=[pl.BlockSpe...  46.9 us
    unnamed x258, local copies, waits for them, and re-layouts  35.5 us
    ppermute x32, starting transfers between devices, from_chip(): return lax.ppermute(values, 'shard', pairs)  34.2 us
    pallas_call x1, Pallas kernels, gram_schulz(): pl.pallas_call(kernel, out_shape=low(2, rows, size), in_specs=[pl.BlockSp...  33.9 us
  transfers between devices with their start and end apart: 91, of which 40 were waited for; matrix products, arithmetic and copies ran while one was open for 13% of the time, Pallas kernels for 23%

profile of v6, /device:TPU:0, one launch (start us, length us, event | category | flops | bytes accessed | tf_op | source)
XLA Modules:
  0.0 758.7 jit_solution(14823806765962943424)
XLA Ops:
  13.6 15.6 %collective-permute-done.1.refs_9_.refs_1_ = bf16[128,1024]{1,0:T(8,128)(2,1)S(1)} collective-permute-done((bf16[128,1024]{1,0:T(8,128)(2,1)S(1)}, bf16[128,1024]{1,0:T(8,128)(2,1)S(1)}, u32[]{:S(2)}, u32[]{:S(2)}) %collective-permute-start.1) | collective-permute-done | bytes 262176 | tf_op jit(solution)/shard_map/ppermute | solution.py:966
  30.6 7.9 %shard_map.318 = (bf16[4,4,128,1024]{3,2,1,0:T(8,128)(2,1)}, bf16[128,1024]{1,0:T(8,128)(2,1)}, bf16[128,1024]{1,0:T(8,128)(2,1)}, bf16[128,1024]{1,0:T(8,128)(2...) custom-call(s32[4]{0:T(128)} %pad_add_fusion.place_ref, f32[4,128,1024]{2,1,0:T(8,128)} %refs_0_.1, ...), custom_call_target="tpu_custom_call" | custom-call | flops 1024 | bytes 1024 | tf_op jit(solution)/shard_map/pallas_call | solution.py:871
  52.3 12.5 %collective-permute-done.6.refs_1_ = bf16[128,1024]{1,0:T(8,128)(2,1)S(1)} collective-permute-done((bf16[128,1024]{1,0:T(8,128)(2,1)}, bf16[128,1024]{1,0:T(8,128)(2,1)S(1)}, u32[]{:S(2)}, u32[]{:S(2)}) %collective-permute-start.6) | collective-permute-done | bytes 262176 | tf_op jit(solution)/shard_map/ppermute | solution.py:966
  64.8 9.6 %collective-permute-done.7.refs_2_ = bf16[128,1024]{1,0:T(8,128)(2,1)S(1)} collective-permute-done((bf16[128,1024]{1,0:T(8,128)(2,1)}, bf16[128,1024]{1,0:T(8,128)(2,1)S(1)}, u32[]{:S(2)}, u32[]{:S(2)}) %collective-permute-start.7) | collective-permute-done | bytes 262176 | tf_op jit(solution)/shard_map/ppermute | solution.py:966
  85.4 8.9 %collective-permute-done.13.refs_0_ = bf16[128,1024]{1,0:T(8,128)(2,1)S(1)} collective-permute-done((bf16[128,1024]{1,0:T(8,128)(2,1)}, bf16[128,1024]{1,0:T(8,128)(2,1)S(1)}, u32[]{:S(2)}, u32[]{:S(2)}) %collective-permute-start.13) | collective-permute-done | bytes 262176 | tf_op jit(solution)/shard_map/ppermute | solution.py:966
  98.5 9.6 %collective-permute-done.14.refs_1_ = bf16[128,1024]{1,0:T(8,128)(2,1)S(1)} collective-permute-done((bf16[128,1024]{1,0:T(8,128)(2,1)}, bf16[128,1024]{1,0:T(8,128)(2,1)S(1)}, u32[]{:S(2)}, u32[]{:S(2)}) %collective-permute-start.14) | collective-permute-done | bytes 262176 | tf_op jit(solution)/shard_map/ppermute | solution.py:966
  126.4 7.8 %shard_map.324 = (bf16[4,2,128,1024]{3,2,1,0:T(8,128)(2,1)}, bf16[4,2,128,1024]{3,2,1,0:T(8,128)(2,1)}, bf16[4,2,128,1024]{3,2,1,0:T(8,128)(2,1)}, bf16[4,2,128,1024]{3,2,1,0:T(8,128)(2,1)}) custom-call(s32[4]{0:T(128)} %pad_add_fusion.place_ref, bf16[4,4,128,1024]{3,2,1,0:T(8,128)(2,1)} %get-tuple-element.118.refs_0_.refs_12_, ...), custom_call_target="tpu_custom_call" | custom-call | flops 1024 | bytes 1024 | tf_op jit(solution)/shard_map/pallas_call | solution.py:740
  157.9 9.5 %shard_map.325.refs_1_ = bf16[256,1024]{1,0:T(8,128)(2,1)} custom-call(s32[1]{0:T(128)S(6)} %copy.87.count_ref, bf16[256,1024]{1,0:T(8,128)(2,1)} %convolution_convert_fusion.6.query_ref.refs_5_, bf16[256,1024]{1,0:T(8,128)(2,1)} %convolution_convert_fusion.5.key_ref.refs_6_, bf16[256,1024]{1,0:T(8,128)(2,1)} %convolution_convert_fusion.4.value_ref.refs_7_), custom_call_target="tpu_custom_call" | custom-call | flops 1024 | bytes 1024 | tf_op jit(solution)/shard_map/pallas_call | solution.py:86
  172.6 7.7 %shard_map.328 = (bf16[4,2,128,1024]{3,2,1,0:T(8,128)(2,1)}, bf16[4,2,128,1024]{3,2,1,0:T(8,128)(2,1)}, bf16[4,2,128,1024]{3,2,1,0:T(8,128)(2,1)}, bf16[4,2,128,1024]{3,2,1,0:T(8,128)(2,1)}) custom-call(s32[4]{0:T(128)} %pad_add_fusion.place_ref, bf16[4,4,128,1024]{3,2,1,0:T(8,128)(2,1)} %get-tuple-element.118.refs_0_.refs_12_, ...), custom_call_target="tpu_custom_call" | custom-call | flops 1024 | bytes 1024 | tf_op jit(solution)/shard_map/pallas_call | solution.py:740
  194.6 10.4 %shard_map.329.refs_2_ = bf16[256,1024]{1,0:T(8,128)(2,1)} custom-call(s32[1]{0:T(128)S(6)} %copy.88.count_ref, bf16[256,1024]{1,0:T(8,128)(2,1)} %convolution_convert_fusion.3.query_ref, bf16[384,1024]{1,0:T(8,128)(2,1)} %fusion.3.key_ref.refs_2_, bf16[384,1024]{1,0:T(8,128)(2,1)} %fusion.4.value_ref.refs_3_), custom_call_target="tpu_custom_call" | custom-call | flops 1024 | bytes 1024 | tf_op jit(solution)/shard_map/pallas_call | solution.py:86
  211.8 17.7 %shard_map.331 = (f32[256,1024]{1,0:T(8,128)}, f32[256,1024]{1,0:T(8,128)}, bf16[256,1024]{1,0:T(8,128)(2,1)}, bf16[256,1024]{1,0:T(8,128)(2,1)}, bf16[256,1024]...) custom-call(s32[4]{0:T(128)} %pad_add_fusion.place_ref, ...), custom_call_target="tpu_custom_call" | custom-call | flops 1024 | bytes 1024 | tf_op jit(solution)/shard_map/pallas_call | solution.py:810
  244.8 14.2 %shard_map.332 = (bf16[256,1024]{1,0:T(8,128)(2,1)}, bf16[384,1024]{1,0:T(8,128)(2,1)}, bf16[384,1024]{1,0:T(8,128)(2,1)}) custom-call(s32[1]{0:T(128)S(6)} %copy.88.count_ref, bf16[256,1024]{1,0:T(8,128)(2,1)} %convolution_convert_fusion.3.query_ref, bf16[384,1024]{1,0:T(8,128)(2,1)} %fusion.3.key_ref.refs_2_, bf16[384,1024]{1,0:T(8,128)(2,1)} %fusion.4.value_ref.refs_3_, ...), custom_call_target="tpu_custom_call" | custom-call | flops 1024 | bytes 1024 | tf_op jit(solution)/shard_map/pallas_call | solution.py:86
  259.0 10.5 %shard_map.335 = (bf16[2,2,256,1024]{3,2,1,0:T(8,128)(2,1)}, bf16[2,2,256,1024]{3,2,1,0:T(8,128)(2,1)}, bf16[2,2,256,1024]{3,2,1,0:T(8,128)(2,1)}, bf16[2,2,256,1024]{3,2,1,0:T(8,128)(2,1)}) custom-call(s32[4]{0:T(128)} %pad_add_fusion.place_ref, bf16[256,1024]{1,0:T(8,128)(2,1)} %add_convert_fusion.1.third_ref.refs_0_, ...), custom_call_target="tpu_custom_call" | custom-call | flops 1024 | bytes 1024 | tf_op jit(solution)/shard_map/pallas_call | solution.py:502
  269.5 6.3 shard_map.336.refs_0_
  285.4 12.8 %shard_map.338 = (bf16[256,1024]{1,0:T(8,128)(2,1)}, bf16[256,1024]{1,0:T(8,128)(2,1)}, bf16[256,1024]{1,0:T(8,128)(2,1)}) custom-call(s32[1]{0:T(128)S(6)} %copy.87.count_ref, bf16[256,1024]{1,0:T(8,128)(2,1)} %convolution_convert_fusion.6.query_ref.refs_5_, bf16[256,1024]{1,0:T(8,128)(2,1)} %convolution_convert_fusion.5.key_ref.refs_6_, ...), custom_call_target="tpu_custom_call" | custom-call | flops 1024 | bytes 1024 | tf_op jit(solution)/shard_map/pallas_call | solution.py:86
  298.2 25.9 %collective-permute-done.33.x_ref = bf16[2,2,256,1024]{3,2,1,0:T(8,128)(2,1)S(1)} collective-permute-done((bf16[2,2,256,1024]{3,2,1,0:T(8,128)(2,1)}, bf16[2,2,256,1024]{3,2,1,0:T(8,128)(2,1)S(1)}, u32[]{:S(2)}, u32[]{:S(2)}) %collective-permute-start.33) | collective-permute-done | bytes 2097184 | tf_op jit(solution)/shard_map/ppermute | solution.py:969
  330.6 7.6 %shard_map.340 = (bf16[1,2,256,1024]{3,2,1,0:T(8,128)(2,1)}, bf16[1,2,256,1024]{3,2,1,0:T(8,128)(2,1)}, bf16[1,2,256,1024]{3,2,1,0:T(8,128)(2,1)}, bf16[1,2,256,1024]{3,2,1,0:T(8,128)(2,1)}) custom-call(s32[4]{0:T(128)} %pad_add_fusion.place_ref, bf16[256,1024]{1,0:T(8,128)(2,1)} %copy-done.41, bf16[384,1024]{1,0:T(8,128)(2,1)} %bitcast.336, ...), custom_call_target="tpu_custom_call" | custom-call | flops 1024 | bytes 1024 | tf_op jit(solution)/shard_map/pallas_call | solution.py:502
  347.6 21.9 %collective-permute-done.38.last_x_ref = bf16[2,256,1024]{2,1,0:T(8,128)(2,1)S(1)} collective-permute-done((bf16[2,256,1024]{2,1,0:T(8,128)(2,1)S(1)}, bf16[2,256,1024]{2,1,0:T(8,128)(2,1)S(1)}, u32[]{:S(2)}, u32[]{:S(2)}) %collective-permute-start.38) | collective-permute-done | bytes 1048608 | tf_op jit(solution)/shard_map/ppermute | solution.py:969
  371.0 6.3 shard_map.342
  377.3 14.2 %collective-permute-done.36.x_ref = bf16[1,2,256,1024]{3,2,1,0:T(8,128)(2,1)S(1)} collective-permute-done((bf16[1,2,256,1024]{3,2,1,0:T(8,128)(2,1)}, bf16[1,2,256,1024]{3,2,1,0:T(8,128)(2,1)S(1)}, u32[]{:S(2)}, u32[]{:S(2)}) %collective-permute-start.36) | collective-permute-done | bytes 1048608 | tf_op jit(solution)/shard_map/ppermute | solution.py:969
  399.3 10.6 %collective-permute-done.40.refs_8_.last_x_ref = bf16[1,256,1024]{2,1,0:T(8,128)(2,1)S(1)} collective-permute-done((bf16[1,256,1024]{2,1,0:T(8,128)(2,1)}, bf16[1,256,1024]{2,1,0:T(8,128)(2,1)S(1)}, u32[]{:S(2)}, u32[]{:S(2)}) %collective-permute-start.40) | collective-permute-done | bytes 524320 | tf_op jit(solution)/shard_map/ppermute | solution.py:969
  413.4 6.6 shard_map.344
  420.0 23.8 %collective-permute-done.45.refs_1_ = bf16[2,128,1024]{2,1,0:T(8,128)(2,1)S(1)} collective-permute-done((bf16[2,128,1024]{2,1,0:T(8,128)(2,1)}, bf16[2,128,1024]{2,1,0:T(8,128)(2,1)S(1)}, u32[]{:S(2)}, u32[]{:S(2)}) %collective-permute-start.45) | collective-permute-done | bytes 524320 | tf_op jit(solution)/shard_map/ppermute | solution.py:966
  455.7 17.8 %collective-permute-done.50 = bf16[128,1024]{1,0:T(8,128)(2,1)S(1)} collective-permute-done((bf16[128,1024]{1,0:T(8,128)(2,1)}, bf16[128,1024]{1,0:T(8,128)(2,1)S(1)}, u32[]{:S(2)}, u32[]{:S(2)}) %collective-permute-start.50) | collective-permute-done | bytes 262176 | tf_op jit(solution)/shard_map/ppermute | solution.py:966
  486.9 6.3 shard_map.348
  494.1 7.3 collective-permute-done.54.refs_2_
  523.6 8.8 %collective-permute-done.57 = bf16[1,128,1024]{2,1,0:T(8,128)(2,1)S(1)} collective-permute-done((bf16[1,128,1024]{2,1,0:T(8,128)(2,1)}, bf16[1,128,1024]{2,1,0:T(8,128)(2,1)S(1)}, u32[]{:S(2)}, u32[]{:S(2)}) %collective-permute-start.57) | collective-permute-done | bytes 262176 | tf_op jit(solution)/shard_map/ppermute | solution.py:966
  552.8 15.8 %collective-permute-done.62 = bf16[128,1024]{1,0:T(8,128)(2,1)S(1)} collective-permute-done((bf16[128,1024]{1,0:T(8,128)(2,1)}, bf16[128,1024]{1,0:T(8,128)(2,1)S(1)}, u32[]{:S(2)}, u32[]{:S(2)}) %collective-permute-start.62) | collective-permute-done | bytes 262176 | tf_op jit(solution)/shard_map/ppermute | solution.py:966
  574.9 12.6 %collective-permute-done.69.a_ref = bf16[128,1024]{1,0:T(8,128)(2,1)S(1)} collective-permute-done((bf16[128,1024]{1,0:T(8,128)(2,1)S(1)}, bf16[128,1024]{1,0:T(8,128)(2,1)S(1)}, u32[]{:S(2)}, u32[]{:S(2)}) %collective-permute-start.69) | collective-permute-done | bytes 262176 | tf_op jit(solution)/shard_map/ppermute | solution.py:969
  587.5 11.0 %collective-permute-done.70.b_ref = bf16[128,1024]{1,0:T(8,128)(2,1)S(1)} collective-permute-done((bf16[128,1024]{1,0:T(8,128)(2,1)S(1)}, bf16[128,1024]{1,0:T(8,128)(2,1)S(1)}, u32[]{:S(2)}, u32[]{:S(2)}) %collective-permute-start.70) | collective-permute-done | bytes 262176 | tf_op jit(solution)/shard_map/ppermute | solution.py:969
  599.2 33.9 %shard_map.352 = bf16[2,128,1024]{2,1,0:T(8,128)(2,1)} custom-call(s32[4]{0:T(128)} %pad_add_fusion.place_ref, bf16[256,1024]{1,0:T(8,128)(2,1)} %copy-done.68, bf16[256,1024]{1,0:T(8,128)(2,1)} %copy-done.76, bf16[256,1024]{1,0:T(8,128)(2,1)} %copy-done.75, bf16[128,1024]{1,0:T(8,128)(2,1)} %copy-done.106, bf16[128,1024]{1,0:T(8,128)(2,1)} %copy-done.108, ...), custom_call_target="tpu_custom_call" | custom-call | flops 1024 | bytes 1024 | tf_op jit(solution)/shard_map/pallas_call | solution.py:380
  643.1 25.5 %shard_map.353.refs_1_ = bf16[2,128,1024]{2,1,0:T(8,128)(2,1)} custom-call(bf16[512,1024]{1,0:T(8,128)(2,1)} %constant_dynamic-update-slice_fusion.4.mine_ref, bf16[512,1024]{1,0:T(8,128)(2,1)} %collective-permute-done.64.sibling_ref, bf16[2,128,1024]{2,1,0:T(8,128)(2,1)} %pad_maximum_fusion.5.refs_0_, bf16[4,128,1024]{2,1,0:T(8,128)(2,1)} %copy-done.12, ...), custom_call_target="tpu_custom_call" | custom-call | flops 1024 | bytes 1024 | tf_op jit(solution)/shard_map/pallas_call | solution.py:233
  (540 shorter events, 338.3 us)
Async XLA Ops:
  38.5 36.0 %collective-permute-start.8 = (bf16[4,4,128,1024]{3,2,1,0:T(8,128)(2,1)}, bf16[4,4,128,1024]{3,2,1,0:T(8,128)(2,1)S(1)}, u32[]{:S(2)}, u32[]{:S(2)}) collective-permute-start(bf16[4,4,128,1024]{3,2,1,0:T(8,128)(2,1)} %get-tuple-element.118.refs_0_.refs_12_), channel_id=1, source_target_pairs={{0,1},{1,0},{2,3},{3,2},{4,5},{5,4},{6,7},{7,6},{8,9},{9,8},{10,11... | collective-permute-start | bytes 12582920 | tf_op jit(solution)/shard_map/ppermute | solution.py:958
  41.3 33.2 %collective-permute-start.9 = (bf16[384,1024]{1,0:T(8,128)(2,1)}, bf16[384,1024]{1,0:T(8,128)(2,1)S(1)}, u32[]{:S(2)}, u32[]{:S(2)}) collective-permute-start(bf16[384,1024]{1,0:T(8,128)(2,1)} %get-tuple-element.122.refs_1_), channel_id=1, source_target_pairs={{0,1},{1,0},{2,3},{3,2},{4,5},{5,4},{6,7},{7,6},{8,9},{9,8},{10,11... | collective-permute-start | bytes 2359304 | tf_op jit(solution)/shard_map/ppermute | solution.py:958
  41.8 32.7 %collective-permute-start.3 = (bf16[384,1024]{1,0:T(8,128)(2,1)}, bf16[384,1024]{1,0:T(8,128)(2,1)S(1)}, u32[]{:S(2)}, u32[]{:S(2)}) collective-permute-start(bf16[384,1024]{1,0:T(8,128)(2,1)} %get-tuple-element.119.refs_1_), channel_id=1, source_target_pairs={{8,0},{0,8},{24,16},{16,24},{9,1},{1,9},{25,17},{17,25},{10,2},{2,... | collective-permute-start | bytes 2359304 | tf_op jit(solution)/shard_map/ppermute | solution.py:969
  43.2 31.2 %collective-permute-start.4 = (bf16[384,1024]{1,0:T(8,128)(2,1)}, bf16[384,1024]{1,0:T(8,128)(2,1)S(1)}, u32[]{:S(2)}, u32[]{:S(2)}) collective-permute-start(bf16[384,1024]{1,0:T(8,128)(2,1)} %get-tuple-element.120), channel_id=1, source_target_pairs={{16,0},{24,8},{0,16},{8,24},{17,1},{25,9},{1,17},{9,25},{18,2},{26... | collective-permute-start | bytes 2359304 | tf_op jit(solution)/shard_map/ppermute | solution.py:969
  82.0 29.8 %collective-permute-start.12 = (bf16[1152,1024]{1,0:T(8,128)(2,1)}, bf16[1152,1024]{1,0:T(8,128)(2,1)S(1)}, u32[]{:S(2)}, u32[]{:S(2)}) collective-permute-start(bf16[1152,1024]{1,0:T(8,128)(2,1)} %get-tuple-element.125.refs_1_), channel_id=1, source_target_pairs={{0,1},{1,0},{2,3},{3,2},{4,5},{5,4},{6,7},{7,6},{8,9},{9,8},{10,11... | collective-permute-start | bytes 7077896 | tf_op jit(solution)/shard_map/ppermute | solution.py:958
  82.0 28.6 %collective-permute-start.10 = (bf16[576,1024]{1,0:T(8,128)(2,1)}, bf16[576,1024]{1,0:T(8,128)(2,1)S(1)}, u32[]{:S(2)}, u32[]{:S(2)}) collective-permute-start(bf16[576,1024]{1,0:T(8,128)(2,1)} %get-tuple-element.123.refs_1_), channel_id=1, source_target_pairs={{8,0},{0,8},{24,16},{16,24},{9,1},{1,9},{25,17},{17,25},{10,2},{2,... | collective-permute-start | bytes 3538952 | tf_op jit(solution)/shard_map/ppermute | solution.py:969
  83.5 28.3 %collective-permute-start.11 = (bf16[576,1024]{1,0:T(8,128)(2,1)}, bf16[576,1024]{1,0:T(8,128)(2,1)S(1)}, u32[]{:S(2)}, u32[]{:S(2)}) collective-permute-start(bf16[576,1024]{1,0:T(8,128)(2,1)} %get-tuple-element.124), channel_id=1, source_target_pairs={{16,0},{24,8},{0,16},{8,24},{17,1},{25,9},{1,17},{9,25},{18,2},{26... | collective-permute-start | bytes 3538952 | tf_op jit(solution)/shard_map/ppermute | solution.py:969
  119.2 28.7 %collective-permute-start.17 = (bf16[576,1024]{1,0:T(8,128)(2,1)}, bf16[576,1024]{1,0:T(8,128)(2,1)S(1)}, u32[]{:S(2)}, u32[]{:S(2)}) collective-permute-start(bf16[576,1024]{1,0:T(8,128)(2,1)} %get-tuple-element.132.refs_1_), channel_id=1, source_target_pairs={{8,0},{0,8},{24,16},{16,24},{9,1},{1,9},{25,17},{17,25},{10,2},{2,... | collective-permute-start | bytes 3538952 | tf_op jit(solution)/shard_map/ppermute | solution.py:969
  120.0 28.3 %collective-permute-start.18 = (bf16[576,1024]{1,0:T(8,128)(2,1)}, bf16[576,1024]{1,0:T(8,128)(2,1)S(1)}, u32[]{:S(2)}, u32[]{:S(2)}) collective-permute-start(bf16[576,1024]{1,0:T(8,128)(2,1)} %get-tuple-element.133), channel_id=1, source_target_pairs={{16,0},{24,8},{0,16},{8,24},{17,1},{25,9},{1,17},{9,25},{18,2},{26... | collective-permute-start | bytes 3538952 | tf_op jit(solution)/shard_map/ppermute | solution.py:969
  154.4 31.5 %collective-permute-start.23 = (bf16[576,1024]{1,0:T(8,128)(2,1)}, bf16[576,1024]{1,0:T(8,128)(2,1)S(1)}, u32[]{:S(2)}, u32[]{:S(2)}) collective-permute-start(bf16[576,1024]{1,0:T(8,128)(2,1)} %get-tuple-element.140.refs_13_), channel_id=1, source_target_pairs={{8,0},{0,8},{24,16},{16,24},{9,1},{1,9},{25,17},{17,25},{10,2},{2,... | collective-permute-start | bytes 3538952 | tf_op jit(solution)/shard_map/ppermute | solution.py:969
  155.1 30.8 %collective-permute-start.24 = (bf16[576,1024]{1,0:T(8,128)(2,1)}, bf16[576,1024]{1,0:T(8,128)(2,1)S(1)}, u32[]{:S(2)}, u32[]{:S(2)}) collective-permute-start(bf16[576,1024]{1,0:T(8,128)(2,1)} %get-tuple-element.141), channel_id=1, source_target_pairs={{16,0},{24,8},{0,16},{8,24},{17,1},{25,9},{1,17},{9,25},{18,2},{26... | collective-permute-start | bytes 3538952 | tf_op jit(solution)/shard_map/ppermute | solution.py:969
  275.8 54.8 %collective-permute-start.32 = (bf16[4,512,1024]{2,1,0:T(8,128)(2,1)}, bf16[4,512,1024]{2,1,0:T(8,128)(2,1)}, u32[]{:S(2)}, u32[]{:S(2)}) collective-permute-start(bf16[4,512,1024]{2,1,0:T(8,128)(2,1)} %shard_map.336.refs_0_), channel_id=1, source_target_pairs={{0,1},{1,0},{2,3},{3,2},{4,5},{5,4},{6,7},{7,6},{8,9},{9,8},{10,11... | collective-permute-start | bytes 12582920 | tf_op jit(solution)/shard_map/ppermute | solution.py:958
  275.9 48.1 %collective-permute-start.33 = (bf16[2,2,256,1024]{3,2,1,0:T(8,128)(2,1)}, bf16[2,2,256,1024]{3,2,1,0:T(8,128)(2,1)S(1)}, u32[]{:S(2)}, u32[]{:S(2)}) collective-permute-start(bf16[2,2,256,1024]{3,2,1,0:T(8,128)(2,1)} %get-tuple-element.166), channel_id=1, source_target_pairs={{8,0},{0,8},{24,16},{16,24},{9,1},{1,9},{25,17},{17,25},{10,2},{2,... | collective-permute-start | bytes 6291464 | tf_op jit(solution)/shard_map/ppermute | solution.py:969
  277.1 47.6 %collective-permute-start.34 = (bf16[2,2,256,1024]{3,2,1,0:T(8,128)(2,1)S(1)}, bf16[2,2,256,1024]{3,2,1,0:T(8,128)(2,1)S(1)}, u32[]{:S(2)}, u32[]{:S(2)}) collective-permute-start(bf16[2,2,256,1024]{3,2,1,0:T(8,128)(2,1)S(1)} %copy-done.115), channel_id=1, source_target_pairs={{16,0},{24,8},{0,16},{8,24},{17,1},{25,9},{1,17},{9,25},{18,2},{26... | collective-permute-start | bytes 6291464 | tf_op jit(solution)/shard_map/ppermute | solution.py:969
  343.5 67.1 %collective-permute-start.35 = (bf16[4,512,1024]{2,1,0:T(8,128)(2,1)}, bf16[4,512,1024]{2,1,0:T(8,128)(2,1)S(1)}, u32[]{:S(2)}, u32[]{:S(2)}) collective-permute-start(bf16[4,512,1024]{2,1,0:T(8,128)(2,1)} %shard_map.341.refs_0_), channel_id=1, source_target_pairs={{0,1},{1,0},{2,3},{3,2},{4,5},{5,4},{6,7},{7,6},{8,9},{9,8},{10,11... | collective-permute-start | bytes 12582920 | tf_op jit(solution)/shard_map/ppermute | solution.py:958
  343.5 26.0 %collective-permute-start.38 = (bf16[2,256,1024]{2,1,0:T(8,128)(2,1)S(1)}, bf16[2,256,1024]{2,1,0:T(8,128)(2,1)S(1)}, u32[]{:S(2)}, u32[]{:S(2)}) collective-permute-start(bf16[2,256,1024]{2,1,0:T(8,128)(2,1)S(1)} %copy-done.81), channel_id=1, source_target_pairs={{8,0},{0,8},{24,16},{16,24},{9,1},{1,9},{25,17},{17,25},{10,2},{2,... | collective-permute-start | bytes 3145736 | tf_op jit(solution)/shard_map/ppermute | solution.py:969
  344.7 26.3 %collective-permute-start.39 = (bf16[2,256,1024]{2,1,0:T(8,128)(2,1)}, bf16[2,256,1024]{2,1,0:T(8,128)(2,1)}, u32[]{:S(2)}, u32[]{:S(2)}) collective-permute-start(bf16[2,256,1024]{2,1,0:T(8,128)(2,1)} %get-tuple-element.173), channel_id=1, source_target_pairs={{16,0},{24,8},{0,16},{8,24},{17,1},{25,9},{1,17},{9,25},{18,2},{26... | collective-permute-start | bytes 3145736 | tf_op jit(solution)/shard_map/ppermute | solution.py:969
  346.2 45.3 %collective-permute-start.36 = (bf16[1,2,256,1024]{3,2,1,0:T(8,128)(2,1)}, bf16[1,2,256,1024]{3,2,1,0:T(8,128)(2,1)S(1)}, u32[]{:S(2)}, u32[]{:S(2)}) collective-permute-start(bf16[1,2,256,1024]{3,2,1,0:T(8,128)(2,1)} %get-tuple-element.171), channel_id=1, source_target_pairs={{8,0},{0,8},{24,16},{16,24},{9,1},{1,9},{25,17},{17,25},{10,2},{2,... | collective-permute-start | bytes 3145736 | tf_op jit(solution)/shard_map/ppermute | solution.py:969
  347.1 45.5 %collective-permute-start.37 = (bf16[1,2,256,1024]{3,2,1,0:T(8,128)(2,1)}, bf16[1,2,256,1024]{3,2,1,0:T(8,128)(2,1)S(1)}, u32[]{:S(2)}, u32[]{:S(2)}) collective-permute-start(bf16[1,2,256,1024]{3,2,1,0:T(8,128)(2,1)} %get-tuple-element.172), channel_id=1, source_target_pairs={{16,0},{24,8},{0,16},{8,24},{17,1},{25,9},{1,17},{9,25},{18,2},{26... | collective-permute-start | bytes 3145736 | tf_op jit(solution)/shard_map/ppermute | solution.py:969
  399.3 44.5 %collective-permute-start.45 = (bf16[2,128,1024]{2,1,0:T(8,128)(2,1)}, bf16[2,128,1024]{2,1,0:T(8,128)(2,1)S(1)}, u32[]{:S(2)}, u32[]{:S(2)}) collective-permute-start(bf16[2,128,1024]{2,1,0:T(8,128)(2,1)} %get-tuple-element.182), channel_id=1, source_target_pairs={{4,0},{5,1},{6,2},{7,3},{0,4},{1,5},{2,6},{3,7},{12,8},{13,9},{14,... | collective-permute-start | bytes 1572872 | tf_op jit(solution)/shard_map/ppermute | solution.py:966
  409.9 33.9 %collective-permute-start.46 = (bf16[2,128,1024]{2,1,0:T(8,128)(2,1)}, bf16[2,128,1024]{2,1,0:T(8,128)(2,1)S(1)}, u32[]{:S(2)}, u32[]{:S(2)}) collective-permute-start(bf16[2,128,1024]{2,1,0:T(8,128)(2,1)} %get-tuple-element.183), channel_id=1, source_target_pairs={{6,0},{7,1},{0,2},{1,3},{2,4},{3,5},{4,6},{5,7},{14,8},{15,9},{8,1... | collective-permute-start | bytes 1572872 | tf_op jit(solution)/shard_map/ppermute | solution.py:966
  546.4 25.4 %collective-permute-start.67 = (bf16[256,1024]{1,0:T(8,128)(2,1)S(1)}, bf16[256,1024]{1,0:T(8,128)(2,1)S(1)}, u32[]{:S(2)}, u32[]{:S(2)}) collective-permute-start(bf16[256,1024]{1,0:T(8,128)(2,1)S(1)} %pad_maximum_fusion.4.q_ref), channel_id=1, source_target_pairs={{8,0},{0,8},{24,16},{16,24},{9,1},{1,9},{25,17},{17,25},{10,2},{2,... | collective-permute-start | bytes 1572872 | tf_op jit(solution)/shard_map/ppermute | solution.py:969
  551.0 87.6 %collective-permute-start.72 = (bf16[4,128,1024]{2,1,0:T(8,128)(2,1)S(1)}, bf16[4,128,1024]{2,1,0:T(8,128)(2,1)S(1)}, u32[]{:S(2)}, u32[]{:S(2)}) collective-permute-start(bf16[4,128,1024]{2,1,0:T(8,128)(2,1)S(1)} %constant_dynamic-update-slice_fusion.8.refs_0_), channel_id=1, source_target_pairs={{8,0},{0,8},{24,16},{16,24},{9,1},{1,9},{25,17},{17,25},{10,2},{2,... | collective-permute-start | bytes 3145736 | tf_op jit(solution)/shard_map/ppermute | solution.py:969
  568.6 67.9 %collective-permute-start.73 = (bf16[4,128,1024]{2,1,0:T(8,128)(2,1)S(1)}, bf16[4,128,1024]{2,1,0:T(8,128)(2,1)S(1)}, u32[]{:S(2)}, u32[]{:S(2)}) collective-permute-start(bf16[4,128,1024]{2,1,0:T(8,128)(2,1)S(1)} %constant_dynamic-update-slice_fusion.8.refs_0_), channel_id=1, source_target_pairs={{16,0},{24,8},{0,16},{8,24},{17,1},{25,9},{1,17},{9,25},{18,2},{26... | collective-permute-start | bytes 3145736 | tf_op jit(solution)/shard_map/ppermute | solution.py:969
  570.6 72.4 %collective-permute-start.64 = (bf16[512,1024]{1,0:T(8,128)(2,1)}, bf16[512,1024]{1,0:T(8,128)(2,1)}, u32[]{:S(2)}, u32[]{:S(2)}) collective-permute-start(bf16[512,1024]{1,0:T(8,128)(2,1)} %constant_dynamic-update-slice_fusion.4.mine_ref), channel_id=1, source_target_pairs={{0,1},{1,0},{2,3},{3,2},{4,5},{5,4},{6,7},{7,6},{8,9},{9,8},{10,11... | collective-permute-start | bytes 3145736 | tf_op jit(solution)/shard_map/ppermute | solution.py:958
  572.6 25.9 %collective-permute-start.70 = (bf16[128,1024]{1,0:T(8,128)(2,1)S(1)}, bf16[128,1024]{1,0:T(8,128)(2,1)S(1)}, u32[]{:S(2)}, u32[]{:S(2)}) collective-permute-start(bf16[128,1024]{1,0:T(8,128)(2,1)S(1)} %slice.231), channel_id=1, source_target_pairs={{16,0},{24,8},{0,16},{8,24},{17,1},{25,9},{1,17},{9,25},{18,2},{26... | collective-permute-start | bytes 786440 | tf_op jit(solution)/shard_map/ppermute | solution.py:969
  637.5 51.9 %collective-permute-start.75 = (bf16[2,128,1024]{2,1,0:T(8,128)(2,1)}, bf16[2,128,1024]{2,1,0:T(8,128)(2,1)S(1)}, u32[]{:S(2)}, u32[]{:S(2)}) collective-permute-start(bf16[2,128,1024]{2,1,0:T(8,128)(2,1)} %slice.241), channel_id=1, source_target_pairs={{8,0},{0,8},{24,16},{16,24},{9,1},{1,9},{25,17},{17,25},{10,2},{2,... | collective-permute-start | bytes 1572872 | tf_op jit(solution)/shard_map/ppermute | solution.py:969
  668.5 38.6 %collective-permute-start.74 = (bf16[2,128,1024]{2,1,0:T(8,128)(2,1)}, bf16[2,128,1024]{2,1,0:T(8,128)(2,1)}, u32[]{:S(2)}, u32[]{:S(2)}) collective-permute-start(bf16[2,128,1024]{2,1,0:T(8,128)(2,1)} %slice.234), channel_id=1, source_target_pairs={{16,0},{24,8},{0,16},{8,24},{17,1},{25,9},{1,17},{9,25},{18,2},{26... | collective-permute-start | bytes 1572872 | tf_op jit(solution)/shard_map/ppermute | solution.py:969
  672.8 46.4 %collective-permute-start.83 = (bf16[2,128,1024]{2,1,0:T(8,128)(2,1)S(1)}, bf16[2,128,1024]{2,1,0:T(8,128)(2,1)}, u32[]{:S(2)}, u32[]{:S(2)}) collective-permute-start(bf16[2,128,1024]{2,1,0:T(8,128)(2,1)S(1)} %copy-done.35), channel_id=1, source_target_pairs={{8,0},{0,8},{24,16},{16,24},{9,1},{1,9},{25,17},{17,25},{10,2},{2,... | collective-permute-start | bytes 1572872 | tf_op jit(solution)/shard_map/ppermute | solution.py:969
  687.4 31.8 %collective-permute-start.84 = (bf16[2,128,1024]{2,1,0:T(8,128)(2,1)S(1)}, bf16[2,128,1024]{2,1,0:T(8,128)(2,1)}, u32[]{:S(2)}, u32[]{:S(2)}) collective-permute-start(bf16[2,128,1024]{2,1,0:T(8,128)(2,1)S(1)} %copy-done.35), channel_id=1, source_target_pairs={{16,0},{24,8},{0,16},{8,24},{17,1},{25,9},{1,17},{9,25},{18,2},{26... | collective-permute-start | bytes 1572872 | tf_op jit(solution)/shard_map/ppermute | solution.py:969
  689.4 25.2 %collective-permute-start.82 = (bf16[128,1024]{1,0:T(8,128)(2,1)}, bf16[128,1024]{1,0:T(8,128)(2,1)}, u32[]{:S(2)}, u32[]{:S(2)}) collective-permute-start(bf16[128,1024]{1,0:T(8,128)(2,1)} %slice_bitcast_fusion.6), channel_id=1, source_target_pairs={{4,0},{5,1},{6,2},{7,3},{0,4},{1,5},{2,6},{3,7},{12,8},{13,9},{14,... | collective-permute-start | bytes 786440 | tf_op jit(solution)/shard_map/ppermute | solution.py:966
  689.4 33.3 %collective-permute-start.79 = (f32[2,3,1024]{2,1,0:T(4,128)S(1)}, f32[2,3,1024]{2,1,0:T(4,128)S(1)}, u32[]{:S(2)}, u32[]{:S(2)}) collective-permute-start(f32[2,3,1024]{2,1,0:T(4,128)S(1)} %add.172), channel_id=1, source_target_pairs={{2,0},{3,1},{4,2},{5,3},{6,4},{7,5},{0,6},{1,7},{10,8},{11,9},{12,... | collective-permute-start | bytes 73736 | tf_op jit(solution)/shard_map/ppermute | solution.py:966
  (179 other events, 1692.6 us)
